TPU v7x, 32 devices: a whole 2x2x4 slice. The times are simulated.
32 devices in a mesh: tok: 32 (over z, y, x, core).
Axes of the slice: x: 2, y: 2, z: 4, core: 2. Of those that a mesh axis runs over, the one named last changes fastest.
Arguments:
- tokens: bfloat16 [32768, 768], P('tok'), may hold values from -6 to 6
- doc_lengths: int32 [33], replicated, may hold values from 1 to 2047, as said below
- first_gain: bfloat16 [768], P('tok'), may hold values from 0.5 to 1.5
- qkv_weight: bfloat16 [768, 2304], P('tok'), may hold values from -0.21875 to 0.21875
- attn_weight: bfloat16 [768, 768], P('tok'), may hold values from -0.625 to 0.625
- second_gain: bfloat16 [768], P('tok'), may hold values from 0.5 to 1.5
- feed_in_weight: bfloat16 [768, 2304], P('tok'), may hold values from -0.21875 to 0.21875
- feed_out_weight: bfloat16 [1152, 768], P(None, 'tok'), may hold values from -0.1875 to 0.1875
- cotangent: bfloat16 [32768, 768], P('tok'), may hold values from -6 to 6
Outputs:
- block_output: bfloat16 [32768, 768], P('tok')
- input_grad: float32 [32768, 768], P('tok')
- first_gain_grad: float32 [768], P('tok')
- qkv_grad: float32 [768, 2304], P('tok')
- attn_grad: float32 [768, 768], P('tok')
- second_gain_grad: float32 [768], P('tok')
- feed_in_grad: float32 [768, 2304], P('tok')
- feed_out_grad: float32 [1152, 768], P(None, 'tok')
Inputs may be any that keep to these rules, and one draw needn't show every extreme that they name: Counting the cumulative sums of doc_lengths from 0, the i-th of the first 32 lies in the interval (i * 1024, (i + 1) * 1024], every length is positive, and the last sum equals 32768.
All inputs are finite; a program needn't handle non-finite values.
Results may differ from a plain program's by a relative error of at most 0.015.
Values may be sent and summed in bfloat16 or wider, within the bound.
No kernel may reach another device: no remote copies, remote signals or barrier semaphores. Data moves between devices by JAX's collectives and lax.ppermute only.
A program may use at most 192 MiB of HBM per device.

v0:
```python
from functools import partial

import jax
import jax.numpy as jnp
from jax import lax
from jax.sharding import PartitionSpec as P

D = 768
FF = 1152
HEADS = 12
HEAD_DIM = 64
HALF = 64


def with_halo(cells, sides, width):
    for axis, dim in sides:
        count = lax.axis_size(axis)
        ends = count - 1
        head = lax.slice_in_dim(cells, 0, width, axis=dim)
        tail = lax.slice_in_dim(cells, cells.shape[dim] - width, cells.shape[dim], axis=dim)
        cells = jnp.concatenate(
            [
                lax.ppermute(tail, axis, [(i, (i + 1) % count) for i in range(ends)]),
                cells,
                lax.ppermute(head, axis, [((i + 1) % count, i) for i in range(ends)]),
            ],
            axis=dim,
        )
    return cells


def passed_along(value, axis, steps):
    count = lax.axis_size(axis)
    first, last = (max(0, -steps), min(count, count - steps))
    return lax.ppermute(value, axis, [(source, source + steps) for source in range(first, last)])


def layer_norm(values, gains):
    row_mean = jnp.mean(values, axis=-1, keepdims=True)
    centered = values - row_mean
    variance = jnp.mean(centered * centered, axis=-1, keepdims=True)
    return centered * lax.rsqrt(variance + 1e-05) * gains


def rotary_tables(offsets, head_size):
    frequency = 10000.0 ** (-jnp.arange(0, head_size, 2, dtype=jnp.float32) / head_size)
    angles = offsets.astype(jnp.float32)[:, None] * frequency[None, :]
    angles = jnp.concatenate([angles, angles], axis=-1)
    return (jnp.cos(angles), jnp.sin(angles))


def rotate(values, cosine_table, sine_table):
    half_size = values.shape[-1] // 2
    turned = jnp.concatenate([-values[..., half_size:], values[..., :half_size]], axis=-1)
    return values * cosine_table[:, None, :] + turned * sine_table[:, None, :]


def rotate_back(incoming, cosine_table, sine_table):
    half_size = incoming.shape[-1] // 2
    scaled = incoming * sine_table[:, None, :]
    return incoming * cosine_table[:, None, :] + jnp.concatenate(
        [scaled[..., half_size:], -scaled[..., :half_size]], axis=-1
    )


def doc_tables(doc_lengths, positions):
    doc_ends = jnp.cumsum(doc_lengths)
    token_total = doc_ends[-1]
    passed = doc_ends[None, :] <= positions[:, None]
    segment = jnp.sum(passed.astype(jnp.int32), axis=1)
    inside = (positions >= 0) & (positions < token_total)
    segment = jnp.where(inside, segment, -1)
    doc_start = jnp.max(jnp.where(passed, doc_ends[None, :], 0), axis=1)
    return (segment, positions - doc_start)


def on_device(
    tokens,
    doc_lengths,
    first_gain,
    qkv_weight,
    attn_weight,
    second_gain,
    feed_in_weight,
    feed_out_weight,
    cotangent,
):
    gain_one, weight_qkv, weight_attn, gain_two, weight_in, weight_down = (
        lax.all_gather(first_gain, "tok", axis=0, tiled=True),
        lax.all_gather(qkv_weight, "tok", axis=0, tiled=True),
        lax.all_gather(attn_weight, "tok", axis=0, tiled=True),
        lax.all_gather(second_gain, "tok", axis=0, tiled=True),
        lax.all_gather(feed_in_weight, "tok", axis=0, tiled=True),
        lax.all_gather(feed_out_weight, "tok", axis=1, tiled=True),
    )
    row_count = tokens.shape[0]
    block_size = min(512, row_count)
    block_count = row_count // block_size
    span_size = block_size + 2 * HALF
    positions = lax.axis_index("tok") * row_count + jnp.arange(
        -HALF, row_count + HALF, dtype=jnp.int32
    )
    segment, offsets = doc_tables(doc_lengths, positions)
    cosine_table, sine_table = rotary_tables(offsets[HALF : HALF + row_count], HEAD_DIM)
    row_ids = jnp.arange(block_size, dtype=jnp.int32)[:, None]
    col_ids = jnp.arange(span_size, dtype=jnp.int32)[None, :]
    in_window = jnp.abs(col_ids - HALF - row_ids) <= HALF
    inputs = tokens.astype(jnp.float32)
    gain_first = gain_one.astype(jnp.float32)
    gain_second = gain_two.astype(jnp.float32)
    normed = layer_norm(inputs, gain_first).astype(jnp.bfloat16)
    merged = jnp.dot(normed, weight_qkv, preferred_element_type=jnp.float32)
    queries = rotate(
        merged[:, :D].reshape(row_count, HEADS, HEAD_DIM), cosine_table, sine_table
    ).astype(jnp.bfloat16)
    key_rows = rotate(
        merged[:, D : 2 * D].reshape(row_count, HEADS, HEAD_DIM), cosine_table, sine_table
    ).astype(jnp.bfloat16)
    value_rows = merged[:, 2 * D :].astype(jnp.bfloat16)
    key_value = jnp.concatenate([key_rows.reshape(row_count, D), value_rows], axis=1)
    extended = with_halo(key_value, (("tok", 0),), HALF)
    ext_keys = extended[:, :D].reshape(row_count + 2 * HALF, HEADS, HEAD_DIM)
    ext_values = extended[:, D:].reshape(row_count + 2 * HALF, HEADS, HEAD_DIM)

    def block_scores(first_row):
        allowed = in_window & (
            segment[HALF + first_row : HALF + first_row + block_size][:, None]
            == segment[first_row : first_row + span_size][None, :]
        )
        query_block = queries[first_row : first_row + block_size]
        key_block = ext_keys[first_row : first_row + span_size]
        scores = (
            jnp.einsum("qhd,khd->hqk", query_block, key_block, preferred_element_type=jnp.float32)
            * 0.125
        )
        return (jnp.where(allowed[None], scores, -1e30), query_block, key_block)

    outputs = []
    log_sums = []
    for block_index in range(block_count):
        first_row = block_index * block_size
        scores, query_block, key_block = block_scores(first_row)
        row_peak = jnp.max(scores, axis=-1, keepdims=True)
        expo = jnp.exp(scores - row_peak)
        row_total = jnp.sum(expo, axis=-1, keepdims=True)
        weights_block = (expo / row_total).astype(jnp.bfloat16)
        value_block = ext_values[first_row : first_row + span_size]
        outputs.append(
            jnp.einsum(
                "hqk,khd->qhd", weights_block, value_block, preferred_element_type=jnp.float32
            ).reshape(block_size, D)
        )
        log_sums.append(row_peak + jnp.log(row_total))
    mixed = jnp.concatenate(outputs, axis=0).astype(jnp.bfloat16)
    residual = inputs + jnp.dot(mixed, weight_attn, preferred_element_type=jnp.float32)
    normed_two = layer_norm(residual, gain_second).astype(jnp.bfloat16)
    both_halves = jnp.dot(normed_two, weight_in, preferred_element_type=jnp.float32)
    gate_part = both_halves[:, :FF]
    up_part = both_halves[:, FF:]
    activated, gelu_back = jax.vjp(partial(jax.nn.gelu, approximate=False), gate_part)
    hidden = (activated * up_part).astype(jnp.bfloat16)
    result = residual + jnp.dot(hidden, weight_down, preferred_element_type=jnp.float32)
    grad_down = jnp.dot(hidden.T, cotangent, preferred_element_type=jnp.float32)
    grad_hidden = jnp.dot(cotangent, weight_down.T, preferred_element_type=jnp.float32)
    grad_gate = gelu_back(grad_hidden * up_part)[0]
    grad_both = jnp.concatenate([grad_gate, grad_hidden * activated], axis=1).astype(jnp.bfloat16)
    grad_in = jnp.dot(normed_two.T, grad_both, preferred_element_type=jnp.float32)
    grad_normed_two = jnp.dot(grad_both, weight_in.T, preferred_element_type=jnp.float32)
    second_back = jax.vjp(layer_norm, residual, gain_second)[1]
    grad_residual_norm, grad_gain_second = second_back(grad_normed_two)
    grad_residual = cotangent.astype(jnp.float32) + grad_residual_norm
    grad_attn_low = grad_residual.astype(jnp.bfloat16)
    grad_attn = jnp.dot(mixed.T, grad_attn_low, preferred_element_type=jnp.float32)
    grad_mixed = (
        jnp.dot(grad_attn_low, weight_attn.T, preferred_element_type=jnp.float32)
        .astype(jnp.bfloat16)
        .reshape(row_count, HEADS, HEAD_DIM)
    )
    query_grads = []
    grad_ext = jnp.zeros((row_count + 2 * HALF, 2 * D), jnp.float32)
    for block_index in range(block_count):
        first_row = block_index * block_size
        scores, query_block, key_block = block_scores(first_row)
        weights_full = jnp.exp(scores - log_sums[block_index])
        value_block = ext_values[first_row : first_row + span_size]
        grad_out_block = grad_mixed[first_row : first_row + block_size]
        grad_weights = jnp.einsum(
            "qhd,khd->hqk", grad_out_block, value_block, preferred_element_type=jnp.float32
        )
        grad_scores = weights_full * (
            grad_weights - jnp.sum(weights_full * grad_weights, axis=-1, keepdims=True)
        )
        grad_scores_low = (0.125 * grad_scores).astype(jnp.bfloat16)
        query_grads.append(
            jnp.einsum(
                "hqk,khd->qhd", grad_scores_low, key_block, preferred_element_type=jnp.float32
            )
        )
        grad_key_block = jnp.einsum(
            "hqk,qhd->khd", grad_scores_low, query_block, preferred_element_type=jnp.float32
        )
        grad_value_block = jnp.einsum(
            "hqk,qhd->khd",
            weights_full.astype(jnp.bfloat16),
            grad_out_block,
            preferred_element_type=jnp.float32,
        )
        grad_ext = grad_ext.at[first_row : first_row + span_size].add(
            jnp.concatenate(
                [grad_key_block.reshape(span_size, D), grad_value_block.reshape(span_size, D)],
                axis=1,
            )
        )
    from_upper = passed_along(grad_ext[:HALF].astype(jnp.bfloat16), "tok", -1).astype(jnp.float32)
    from_lower = passed_along(grad_ext[row_count + HALF :].astype(jnp.bfloat16), "tok", 1).astype(
        jnp.float32
    )
    grad_own = grad_ext[HALF : HALF + row_count]
    grad_own = grad_own.at[:HALF].add(from_lower)
    grad_own = grad_own.at[row_count - HALF :].add(from_upper)
    grad_queries = rotate_back(
        jnp.concatenate(query_grads, axis=0), cosine_table, sine_table
    ).reshape(row_count, D)
    grad_keys = rotate_back(
        grad_own[:, :D].reshape(row_count, HEADS, HEAD_DIM), cosine_table, sine_table
    ).reshape(row_count, D)
    grad_merged = jnp.concatenate([grad_queries, grad_keys, grad_own[:, D:]], axis=1).astype(
        jnp.bfloat16
    )
    grad_qkv = jnp.dot(normed.T, grad_merged, preferred_element_type=jnp.float32)
    grad_normed = jnp.dot(grad_merged, weight_qkv.T, preferred_element_type=jnp.float32)
    first_back = jax.vjp(layer_norm, inputs, gain_first)[1]
    grad_inputs_norm, grad_gain_first = first_back(grad_normed)
    input_grad = grad_residual + grad_inputs_norm
    sent_gain_first, sent_qkv, sent_attn, sent_gain_second, sent_in, sent_down = (
        lax.psum_scatter(grad_gain_first, "tok", scatter_dimension=0, tiled=True),
        lax.psum_scatter(grad_qkv, "tok", scatter_dimension=0, tiled=True),
        lax.psum_scatter(grad_attn, "tok", scatter_dimension=0, tiled=True),
        lax.psum_scatter(grad_gain_second, "tok", scatter_dimension=0, tiled=True),
        lax.psum_scatter(grad_in, "tok", scatter_dimension=0, tiled=True),
        lax.psum_scatter(grad_down, "tok", scatter_dimension=1, tiled=True),
    )
    return (
        result.astype(jnp.bfloat16),
        input_grad,
        sent_gain_first,
        sent_qkv,
        sent_attn,
        sent_gain_second,
        sent_in,
        sent_down,
    )


def solution(mesh):
    in_specs = (
        P("tok", None),
        P(),
        P("tok"),
        P("tok", None),
        P("tok", None),
        P("tok"),
        P("tok", None),
        P(None, "tok"),
        P("tok", None),
    )
    out_specs = (
        P("tok", None),
        P("tok", None),
        P("tok"),
        P("tok", None),
        P("tok", None),
        P("tok"),
        P("tok", None),
        P(None, "tok"),
    )
    return jax.shard_map(
        on_device, mesh=mesh, in_specs=in_specs, out_specs=out_specs, check_vma=False
    )
```

profile of v0, /device:TPU:0, one launch (start us, length us, event | category | flops | bytes accessed | tf_op | source)
XLA Modules:
  0.0 746.0 jit_solution(12081924460684448049)
XLA Ops:
  14.0 42.2 %all-reduce.7 = (bf16[768]{0:T(1024)(128)(2,1)S(1)}, bf16[768]{0:T(1024)(128)(2,1)S(1)}) all-reduce(bf16[768]{0:T(1024)(128)(2,1)S(1)} %dynamic-update-slice.12, bf16[768]{0:T(1024)(128)(2,1)S(1)} %dynamic-update-slice.13), channel_id=1, replica_groups=mesh['tok'=32] {'tok'}, use_global_device_ids=true, to_apply=%add.1 | all-reduce | flops 1536 | bytes 6144
  69.8 4.1 all-gather.5.cloned.1.call-done
  74.0 6.0 fusion.70
  97.2 6.9 fusion.96
  128.2 4.5 fusion.102
  138.2 5.8 fusion.61
  152.8 5.3 fusion.62
  163.3 29.0 %all-gather.9.cloned.1.call-done = bf16[768,2304]{1,0:T(8,128)(2,1)} async-done(((bf16[24,2304]{1,0:T(8,128)(2,1)}), bf16[768,2304]{1,0:T(8,128)(2,1)}) %all-gather.9.cloned.1.call-update) | async-done | bytes 3538960 | tf_op jit(solution)/shard_map/all_gather | solution.py:93
  192.3 10.5 %fusion.93 = f32[1024,2304]{1,0:T(8,128)} fusion(bf16[768,2304]{1,0:T(8,128)(2,1)} %all-gather.9.cloned.1.call-done, f32[1024,768]{0,1:T(8,128)} %copy-done.10, f32[768]{0:T(1024)S(1)} %convert_element_type.82, f32[1024]{0:T(1024)S(1)} %fusion.78, f32[1024]{0:T(1024)S(1)} %broadcast_multiply_fusion.2), kind=kOutput, calls=%fused_computation.172 | convolution fusion | flops 3627024384 | bytes 16133120 | tf_op jit(solution)/shard_map/dot_general | solution.py:157
  202.8 46.6 %all-gather.11.cloned.1.call-done = bf16[1152,768]{0,1:T(8,128)(2,1)} async-done(((bf16[1152,24]{0,1:T(8,128)(2,1)}), bf16[1152,768]{0,1:T(8,128)(2,1)}) %all-gather.11.cloned.1.call-update) | async-done | bytes 1769488 | tf_op jit(solution)/shard_map/all_gather | solution.py:94
  249.4 15.2 %add_convert_fusion = (bf16[1024,1152]{1,0:T(8,128)(2,1)S(1)}, f32[1024,1152]{1,0:T(8,128)S(1)}, f32[1024,1152]{1,0:T(8,128)S(1)}) fusion(f32[1024,2304]{1,0:T(8,128)} %fusion.93, bf16[1024,768]{1,0:T(8,128)(2,1)S(1)} %copy-done.30, bf16[1152,768]{0,1:T(8,128)(2,1)} %all-gather.11.cloned.1.call-done), kind=kOutput, calls=%fused_computation.48 | convolution fusion | flops 1898053632 | bytes 24576000 | tf_op jit(solution)/shard_map/dot_general | solution.py:164
  268.3 6.2 multiply_reduce_fusion.2
  281.0 5.7 fusion.107
  293.0 6.5 fusion.56
  299.6 8.3 %fusion.106 = f32[12,512,640]{2,1,0:T(8,128)} fusion(bf16[512,12,64]{0,2,1:T(8,128)(2,1)S(1)} %bitcast.83, bf16[640,12,64]{0,2,1:T(8,128)(2,1)} %bitcast.97), kind=kOutput, calls=%fused_computation.184 | convolution fusion | flops 503316480 | bytes 17498112 | tf_op jit(solution)/shard_map/qhd,khd->hqk/dot_general | solution.py:187
  307.9 49.1 %fusion.29 = f32[12,64,640]{2,1,0:T(8,128)} fusion(f32[12,512,640]{2,1,0:T(8,128)} %fusion.106, f32[12,512,640]{2,1,0:T(8,128)} %copy-done, f32[12,512]{1,0:T(8,128)S(1)} %log_add_fusion, bf16[1024,12,64]{0,2,1:T(8,128)(2,1)} %fusion.52), kind=kOutput, calls=%fused_computation.33 | convolution fusion | flops 530848384 | bytes 65732608 | tf_op jit(solution)/shard_map/hqk,qhd->khd/dot_general | solution.py:199
  357.0 8.0 %fusion.105 = f32[12,512,640]{2,1,0:T(8,128)} fusion(bf16[512,12,64]{0,2,1:T(8,128)(2,1)S(1)} %bitcast.85, bf16[640,12,64]{0,2,1:T(8,128)(2,1)} %bitcast.95), kind=kOutput, calls=%fused_computation.183 | convolution fusion | flops 503316480 | bytes 17498112 | tf_op jit(solution)/shard_map/qhd,khd->hqk/dot_general | solution.py:187
  364.9 49.3 %fusion.23 = f32[12,64,640]{2,1,0:T(8,128)} fusion(f32[12,512,640]{2,1,0:T(8,128)} %fusion.105, f32[12,512,640]{2,1,0:T(8,128)} %copy-done.1, f32[12,512]{1,0:T(8,128)S(1)} %log_add_fusion.1, bf16[1024,12,64]{0,2,1:T(8,128)(2,1)} %fusion.52), kind=kOutput, calls=%fused_computation.31 | convolution fusion | flops 530848384 | bytes 65732608 | tf_op jit(solution)/shard_map/hqk,qhd->khd/dot_general | solution.py:199
  414.2 7.2 fusion.14
  421.5 7.6 %fusion.12 = f32[12,64,640]{2,1,0:T(8,128)S(1)} fusion(bf16[512,12,64]{0,2,1:T(8,128)(2,1)S(1)} %bitcast.84, f32[12,512,640]{2,1,0:T(8,128)} %copy-done, f32[12,512]{1,0:T(8,128)S(1)} %log_add_fusion), kind=kOutput, calls=%fused_computation.20 | convolution fusion | flops 511180800 | bytes 18505728 | tf_op jit(solution)/shard_map/hqk,qhd->khd/dot_general | solution.py:202
  432.3 4.7 slice.286
  443.0 48.2 %fusion.32 = f32[12,64,512]{2,1,0:T(8,128)S(1)} fusion(bf16[640,12,64]{0,2,1:T(8,128)(2,1)} %bitcast.94, f32[12,512,640]{2,1,0:T(8,128)} %fusion.106, f32[12,512,640]{2,1,0:T(8,128)} %copy-done, f32[12,512]{1,0:T(8,128)} %copy-done.36), kind=kOutput, calls=%fused_computation.34 | convolution fusion | flops 530848384 | bytes 34037760 | tf_op jit(solution)/shard_map/hqk,khd->qhd/dot_general | solution.py:195
  491.3 42.2 %fusion.26 = f32[12,64,512]{2,1,0:T(8,128)} fusion(bf16[640,12,64]{0,2,1:T(8,128)(2,1)} %bitcast.91, f32[12,512,640]{2,1,0:T(8,128)} %fusion.105, f32[12,512,640]{2,1,0:T(8,128)} %copy-done.1, f32[12,512]{1,0:T(8,128)} %copy-done.37), kind=kOutput, calls=%fused_computation.32 | convolution fusion | flops 530848384 | bytes 34037760 | tf_op jit(solution)/shard_map/hqk,khd->qhd/dot_general | solution.py:195
  536.0 4.9 scatter-add.16
  543.3 5.1 scatter-add.19
  558.8 5.3 fusion.54
  564.1 8.8 %fusion.59 = f32[768,2304]{1,0:T(8,128)} fusion(bf16[1024,768]{0,1:T(8,128)(2,1)S(1)} %copy-done.31, bf16[1024,768]{0,1:T(8,128)(2,1)} %get-tuple-element.127, bf16[1024,768]{0,1:T(8,128)(2,1)} %get-tuple-element.126, bf16[1024,768]{0,1:T(8,128)(2,1)S(1)} %copy-done.4, f32[768]{0:T(1024)S(1)} %copy-done.41, f32[1024]{0:T(1024)S(1)} %copy-done.43, ...), kind=kOutput, calls=%fused_computation.98 | convolution fusion | flops 3641966592 | bytes 13380608 | tf_op jit(solution)/shard_map/dot_general | solution.py:230
  573.0 6.6 add_convert_fusion.1
  582.2 6.8 fusion.50
  592.0 39.9 %all-reduce.6 = (f32[768]{0:T(1024)S(1)}, f32[768]{0:T(1024)S(1)}) all-reduce(f32[768]{0:T(1024)S(1)} %get-tuple-element.90, f32[768]{0:T(1024)S(1)} %get-tuple-element.88), channel_id=2, replica_groups=mesh['tok'=32] {'tok'}, use_global_device_ids=true, to_apply=%region_18.19.clone | all-reduce | flops 1536 | bytes 12288
  633.1 6.2 add_add_fusion.2
  642.9 96.0 %reduce-scatter.7.cloned.1.call-done = f32[24,2304]{1,0:T(8,128)} async-done(((f32[768,2304]{1,0:T(8,128)}), f32[24,2304]{1,0:T(8,128)}) %reduce-scatter.7.cloned.1.call-update) | async-done | bytes 221200 | tf_op jit(solution)/shard_map/reduce_scatter | solution.py:237
  (217 shorter events, 131.8 us)
Async XLA Ops:
  7.2 66.8 %all-gather.5.cloned.1.call-start = ((), (), s32[]{:S(2)}) async-start(), calls=%async_computation.4 | async-start | bytes 3649536 | tf_op jit(solution)/shard_map/all_gather | solution.py:90
  7.9 150.2 %all-gather.7.cloned.1.call-start = ((), (), s32[]{:S(2)}) async-start(), calls=%async_computation.5 | async-start | bytes 1216512 | tf_op jit(solution)/shard_map/all_gather | solution.py:91
  8.6 183.6 %all-gather.9.cloned.1.call-start = ((), (), s32[]{:S(2)}) async-start(), calls=%async_computation.6 | async-start | bytes 3649536 | tf_op jit(solution)/shard_map/all_gather | solution.py:93
  9.4 240.0 %all-gather.11.cloned.1.call-start = ((), (), s32[]{:S(2)}) async-start(), calls=%async_computation.7 | async-start | bytes 1824768 | tf_op jit(solution)/shard_map/all_gather | solution.py:94
  10.0 632.9 %reduce-scatter.9.cloned.1.call-start = ((), (), s32[]{:S(2)}) async-start(), calls=%async_computation.9 | async-start | bytes 2433024 | tf_op jit(solution)/shard_map/reduce_scatter | solution.py:238
  56.2 17.8 %copy-start.40 = (f32[768]{0:T(1024)}, f32[768]{0:T(1024)S(1)}, u32[]{:S(2)}) copy-start(f32[768]{0:T(1024)S(1)} %convert_element_type.74) | copy-start | bytes 9220
  57.4 34.3 %copy-start.20 = (f32[1024,64]{0,1:T(8,128)}, f32[1024,64]{0,1:T(8,128)S(1)}, u32[]{:S(2)}) copy-start(f32[1024,64]{0,1:T(8,128)S(1)} %get-tuple-element.131) | copy-start | bytes 786436
  57.4 55.7 %copy-start.18 = (f32[1024,64]{0,1:T(8,128)}, f32[1024,64]{0,1:T(8,128)S(1)}, u32[]{:S(2)}) copy-start(f32[1024,64]{0,1:T(8,128)S(1)} %get-tuple-element.130) | copy-start | bytes 786436
  59.3 98.9 %copy-start.3 = (bf16[1024,768]{0,1:T(8,128)(2,1)}, bf16[1024,768]{0,1:T(8,128)(2,1)S(1)}, u32[]{:S(2)}) copy-start(bf16[1024,768]{0,1:T(8,128)(2,1)S(1)} %copy.75) | copy-start | bytes 4718596
  59.6 14.4 %copy-start.38 = (f32[1024]{0:T(1024)}, f32[1024]{0:T(1024)S(1)}, u32[]{:S(2)}) copy-start(f32[1024]{0:T(1024)S(1)} %broadcast_multiply_fusion.3) | copy-start | bytes 12292
  60.1 13.9 %copy-start.42 = (f32[1024]{0:T(1024)}, f32[1024]{0:T(1024)S(1)}, u32[]{:S(2)}) copy-start(f32[1024]{0:T(1024)S(1)} %fusion.77) | copy-start | bytes 12292
  109.0 6.7 collective-permute-start
  111.3 4.4 collective-permute-start.1
  121.3 6.9 copy-start.15
  121.3 6.9 copy-start.35
  138.2 5.8 copy-start.23
  138.2 5.8 copy-start.34
  147.2 5.6 copy-start.1
  147.2 5.6 copy-start.24
  163.3 86.1 %copy-start.30 = (bf16[1024,768]{1,0:T(8,128)(2,1)S(1)}, bf16[1024,768]{1,0:T(8,128)(2,1)}, u32[]{:S(2)}) copy-start(bf16[1024,768]{1,0:T(8,128)(2,1)} %param.25) | copy-start | bytes 4718596
  249.4 15.2 %copy-start.14 = (f32[1024,2304]{1,0:T(8,128)S(1)}, f32[1024,2304]{1,0:T(8,128)}, u32[]{:S(2)}) copy-start(f32[1024,2304]{1,0:T(8,128)} %fusion.93) | copy-start | bytes 28311556
  267.4 7.1 copy-start.26
  281.0 361.9 %reduce-scatter.13.cloned.1.call-start = ((), (), s32[]{:S(2)}) async-start(), calls=%async_computation.11 | async-start | bytes 3649536
  286.8 356.1 %reduce-scatter.11.cloned.1.call-start = ((), (), s32[]{:S(2)}) async-start(), calls=%async_computation.10 | async-start | bytes 7299072 | tf_op jit(solution)/shard_map/reduce_scatter | solution.py:240
  288.2 133.3 %copy-start.36 = (f32[12,512]{1,0:T(8,128)}, f32[12,512]{1,0:T(8,128)S(1)}, u32[]{:S(2)}) copy-start(f32[12,512]{1,0:T(8,128)S(1)} %log_add_fusion) | copy-start | bytes 73732
  299.5 439.4 %reduce-scatter.7.cloned.1.call-start = ((), (), s32[]{:S(2)}) async-start(), calls=%async_computation.8 | async-start | bytes 7299072 | tf_op jit(solution)/shard_map/reduce_scatter | solution.py:237
  299.6 114.6 %copy-start.37 = (f32[12,512]{1,0:T(8,128)}, f32[12,512]{1,0:T(8,128)S(1)}, u32[]{:S(2)}) copy-start(f32[12,512]{1,0:T(8,128)S(1)} %log_add_fusion.1) | copy-start | bytes 73732
  421.5 7.7 %copy-start.29 = (f32[12,64,640]{2,1,0:T(8,128)S(1)}, f32[12,64,640]{2,1,0:T(8,128)}, u32[]{:S(2)}) copy-start(f32[12,64,640]{2,1,0:T(8,128)} %fusion.23) | copy-start | bytes 5898244
  438.0 102.9 %collective-permute-start.3 = (bf16[64,1536]{0,1:T(8,128)(2,1)S(1)}, bf16[64,1536]{0,1:T(8,128)(2,1)}, u32[]{:S(2)}, u32[]{:S(2)}) collective-permute-start(bf16[64,1536]{0,1:T(8,128)(2,1)S(1)} %slice.338), channel_id=1, source_target_pairs={{1,0},{2,1},{3,2},{4,3},{5,4},{6,5},{7,6},{8,7},{9,8},{10,9},{11,1... | collective-permute-start | bytes 589832 | tf_op jit(solution)/shard_map/ppermute | solution.py:35
  439.2 94.3 %collective-permute-start.2 = (bf16[64,1536]{0,1:T(8,128)(2,1)}, bf16[64,1536]{0,1:T(8,128)(2,1)}, u32[]{:S(2)}, u32[]{:S(2)}) collective-permute-start(bf16[64,1536]{0,1:T(8,128)(2,1)} %slice.339), channel_id=1, source_target_pairs={{0,1},{1,2},{2,3},{3,4},{4,5},{5,6},{6,7},{7,8},{8,9},{9,10},{10,1... | collective-permute-start | bytes 589832 | tf_op jit(solution)/shard_map/ppermute | solution.py:35
  491.3 62.9 %copy-start.16 = (f32[12,64,512]{2,1,0:T(8,128)}, f32[12,64,512]{2,1,0:T(8,128)S(1)}, u32[]{:S(2)}) copy-start(f32[12,64,512]{2,1,0:T(8,128)S(1)} %fusion.32) | copy-start | bytes 4718596
  582.2 6.9 copy-start.45
  (34 other events, 108.8 us)
Sparse Core Ops, SparseCore 0:
  10.9 63.0 all-gather.4
  76.9 52.9 all-gather.6
  132.8 59.4 all-gather.8
  195.0 54.4 all-gather.10
  281.1 98.1 reduce-scatter.8
  386.0 102.6 reduce-scatter.12
  495.9 118.1 reduce-scatter.10
  620.4 118.5 reduce-scatter.6
where the time goes:
time: 756 us; the launch traced here: 746 us
  matrix products  320 us (42%)
  waiting for transfers between devices  178 us (24%)
  local copies, waits for them, and re-layouts  85.1 us (11%)
  blocking collectives  82.1 us (11%)
  other arithmetic  56.2 us (7%)
  between operations  15.2 us (2%)
  starting transfers between devices  9 us (1%)
    dot_general x2, matrix products, on_device(): jnp.einsum('hqk,qhd->khd', grad_scores_low, query_block, preferred_elemen...  98.4 us
    reduce_scatter x1, waiting for transfers between devices, on_device(): lax.psum_scatter(grad_qkv, 'tok', scatter_dimension=0, tiled=True)  96 us
    dot_general x2, matrix products, on_device(): jnp.einsum('hqk,khd->qhd', grad_scores_low, key_block, preferred_element_...  90.5 us
    unnamed x2, blocking collectives  82.1 us
    all_gather x1, waiting for transfers between devices, on_device(): lax.all_gather(feed_out_weight, 'tok', axis=1, tiled=True)  46.6 us
    unnamed x118, local copies, waits for them, and re-layouts  33.4 us
    all_gather x1, waiting for transfers between devices, on_device(): lax.all_gather(feed_in_weight, 'tok', axis=0, tiled=True)  29 us
    dot_general x2, matrix products, on_device(): jnp.einsum('qhd,khd->hqk', grad_out_block, value_block, preferred_element...  16.2 us
  transfers between devices with their start and end apart: 12, of which 4 were waited for; matrix products, arithmetic and copies ran while one was open for 55% of the time, Pallas kernels for 0%

commit v1 on v0

v1 whole, which is shorter than its diff:
```python
import jax
import jax.numpy as jnp
from jax import lax
from jax.experimental import pallas as pl
from jax.experimental.pallas import tpu as pltpu
from jax.sharding import PartitionSpec as P

D = 768
FF = 1152
HEADS = 12
HEAD_DIM = 64
HALF = 64
PAIRS = HEADS // 2
BLOCK = 128
SPAN = BLOCK + 2 * HALF
LANES = 128
QKV_HALF = 3 * D // 2
FF_HALF = 2 * FF
MIB = 1024 * 1024
BF = jnp.bfloat16
F32 = jnp.float32


def dot(left, right, left_dim=1, right_dim=0):
    return lax.dot_general(
        left, right, (((left_dim,), (right_dim,)), ((), ())), preferred_element_type=F32
    )


def params(mib):
    return pltpu.CompilerParams(vmem_limit_bytes=mib * MIB)


def whole(shape):
    return pl.BlockSpec(shape, lambda *_: (0,) * len(shape))


def rows(shape):
    return pl.BlockSpec(shape, lambda i: (i,) + (0,) * (len(shape) - 1))


SMEM = pl.BlockSpec(memory_space=pltpu.SMEM)
ANY = pl.BlockSpec(memory_space=pl.ANY)


def lane_ids(shape):
    return lax.broadcasted_iota(jnp.int32, shape, len(shape) - 1)


def swap_halves(values):
    low = (lane_ids(values.shape) & (HEAD_DIM - 1)) < HEAD_DIM // 2
    return jnp.where(
        low, pltpu.roll(values, LANES - HEAD_DIM // 2, 1), pltpu.roll(values, HEAD_DIM // 2, 1)
    )


def normalized(values):
    centered = values - jnp.mean(values, axis=-1, keepdims=True)
    scale = lax.rsqrt(jnp.mean(centered * centered, axis=-1, keepdims=True) + 1e-05)
    return centered * scale, scale


def norm_back(grad, unit, scale, gains):
    grad_unit = grad * gains
    return scale * (
        grad_unit
        - jnp.mean(grad_unit, axis=-1, keepdims=True)
        - unit * jnp.mean(grad_unit * unit, axis=-1, keepdims=True)
    )


def qkv_kernel(x_ref, gain_ref, w_ref, cos_ref, sin_ref, normed_ref, qkv_ref):
    unit, _ = normalized(x_ref[...].astype(F32))
    normed = (unit * gain_ref[...]).astype(BF)
    normed_ref[...] = normed
    cosine = cos_ref[...]
    sine = sin_ref[...]
    for half in range(2):
        merged = dot(normed, w_ref[half, :, :QKV_HALF])
        for tile in range(QKV_HALF // LANES):
            first = half * QKV_HALF + tile * LANES
            part = merged[:, tile * LANES : (tile + 1) * LANES]
            if first < 2 * D:
                part = part * cosine + swap_halves(part) * sine
            qkv_ref[:, first : first + LANES] = part.astype(BF)


def project_qkv(tokens, gain, weights, cosine, sine):
    count = tokens.shape[0]
    size = min(256, count)
    return pl.pallas_call(
        qkv_kernel,
        grid=(count // size,),
        in_specs=[
            rows((size, D)),
            whole((1, D)),
            whole(weights.shape),
            rows((size, LANES)),
            rows((size, LANES)),
        ],
        out_specs=[rows((size, D)), rows((size, 3 * D))],
        out_shape=[
            jax.ShapeDtypeStruct((count, D), BF),
            jax.ShapeDtypeStruct((count, 3 * D), BF),
        ],
        compiler_params=params(40),
        cost_estimate=pl.CostEstimate(
            flops=2 * count * D * 3 * D, bytes_accessed=count * D * 10 + 6 * D * D, transcendentals=0
        ),
        name="qkv",
    )(tokens, gain, weights, cosine, sine)


def window_bias(marks_ref, block):
    shape = (SPAN, 2 * BLOCK)
    first = marks_ref[3] + block * BLOCK
    key = lax.broadcasted_iota(jnp.int32, shape, 0)
    query = lax.broadcasted_iota(jnp.int32, (1, 2 * BLOCK), 1) & (BLOCK - 1)
    place = first + query
    lowest = query
    highest = query + 2 * HALF
    for index in range(3):
        mark = marks_ref[index]
        edge = mark - first + HALF
        past = place >= mark
        lowest = jnp.where(past, jnp.maximum(lowest, edge), lowest)
        highest = jnp.where(past, highest, jnp.minimum(highest, edge - 1))
    return jnp.where((key >= lowest) & (key <= highest), 0.0, -1e30).astype(F32)


def stacked(pair):
    low = lane_ids(pair.shape) < HEAD_DIM
    zero = jnp.zeros_like(pair)
    return jnp.concatenate([jnp.where(low, pair, zero), jnp.where(low, zero, pair)], axis=0)


def unstacked(both):
    low = lane_ids((BLOCK, LANES)) < HEAD_DIM
    return jnp.where(low, both[:BLOCK], both[BLOCK:])


def fill_span(qkv_ref, lower_ref, upper_ref, span_ref, sems):
    count = qkv_ref.shape[0]
    copies = [
        pltpu.make_async_copy(
            qkv_ref.at[:, pl.ds(D, 2 * D)], span_ref.at[pl.ds(HALF, count)], sems.at[0]
        ),
        pltpu.make_async_copy(lower_ref, span_ref.at[pl.ds(0, HALF)], sems.at[1]),
        pltpu.make_async_copy(upper_ref, span_ref.at[pl.ds(HALF + count, HALF)], sems.at[2]),
    ]
    for copy in copies:
        copy.start()
    for copy in copies:
        copy.wait()


def attend_kernel(marks_ref, query_ref, qkv_ref, lower_ref, upper_ref, out_ref, log_ref, span_ref, sems):
    block = pl.program_id(0)

    @pl.when(block == 0)
    def _():
        fill_span(qkv_ref, lower_ref, upper_ref, span_ref, sems)

    bias = window_bias(marks_ref, block)
    window = pl.ds(pl.multiple_of(block * BLOCK, BLOCK), SPAN)
    for pair in range(PAIRS):
        lanes = slice(pair * LANES, (pair + 1) * LANES)
        query = stacked(query_ref[:, lanes] * BF(0.125))
        keys = span_ref[window, lanes]
        values = span_ref[window, D + pair * LANES : D + (pair + 1) * LANES]
        scores = dot(keys, query, 1, 1) + bias
        peak = jnp.max(scores, axis=0, keepdims=True)
        expo = jnp.exp(scores - peak)
        total = jnp.sum(expo, axis=0, keepdims=True)
        weights = (expo * (1.0 / total)).astype(BF)
        out_ref[:, lanes] = unstacked(dot(weights, values, 0, 0)).astype(BF)
        log_ref[0, pair : pair + 1, :] = peak + jnp.log(total)


def attend(marks, qkv, lower, upper):
    count = qkv.shape[0]
    blocks = count // BLOCK
    return pl.pallas_call(
        attend_kernel,
        grid=(blocks,),
        in_specs=[SMEM, rows((BLOCK, D)), ANY, ANY, ANY],
        out_specs=[rows((BLOCK, D)), rows((1, 8, 2 * BLOCK))],
        out_shape=[
            jax.ShapeDtypeStruct((count, D), BF),
            jax.ShapeDtypeStruct((blocks, 8, 2 * BLOCK), F32),
        ],
        scratch_shapes=[
            pltpu.VMEM((count + 2 * HALF, 2 * D), BF),
            pltpu.SemaphoreType.DMA((3,)),
        ],
        compiler_params=params(32),
        cost_estimate=pl.CostEstimate(
            flops=4 * count * SPAN * D * 2, bytes_accessed=count * D * 10, transcendentals=0
        ),
        name="attend",
    )(marks, qkv, qkv, lower, upper)


FF_PARTS = tuple((first, min(256, FF - first)) for first in range(0, FF, 256))


def middle_kernel(
    x_ref,
    mixed_ref,
    cot_ref,
    gain_ref,
    w_ref,
    result_ref,
    normed_ref,
    both_ref,
    hidden_ref,
    low_ref,
    mixed_grad_ref,
    grad_ref,
):
    gain = gain_ref[...]
    cot = cot_ref[...]
    weight_attn = w_ref[1, :, FF : FF + D]
    residual = x_ref[...].astype(F32) + dot(mixed_ref[...], weight_attn)
    unit, scale = normalized(residual)
    normed = (unit * gain).astype(BF)
    normed_ref[...] = normed
    result = residual
    grad_normed = None
    for first, size in FF_PARTS:
        gate_cols = slice(first, first + size)
        up_cols = slice(FF + first, FF + first + size)
        gate = dot(normed, w_ref[0, :, gate_cols])
        up = dot(normed, w_ref[0, :, up_cols])
        grad_hidden = dot(cot, w_ref[1, :, gate_cols])
        share = 0.5 + 0.5 * lax.erf(gate * 0.7071067811865476)
        active = gate * share
        slope = share + gate * (jnp.exp(-0.5 * gate * gate) * 0.3989422804014327)
        hidden = (active * up).astype(BF)
        hidden_ref[:, gate_cols] = hidden
        grad_gate = (grad_hidden * up * slope).astype(BF)
        grad_up = (grad_hidden * active).astype(BF)
        both_ref[:, gate_cols] = grad_gate
        both_ref[:, up_cols] = grad_up
        result = result + dot(hidden, w_ref[1, :, gate_cols], 1, 1)
        piece = dot(grad_gate, w_ref[0, :, gate_cols], 1, 1) + dot(
            grad_up, w_ref[0, :, up_cols], 1, 1
        )
        grad_normed = piece if grad_normed is None else grad_normed + piece
    result_ref[...] = result.astype(BF)
    grad = cot.astype(F32) + norm_back(grad_normed, unit, scale, gain)
    grad_ref[...] = grad
    low = grad.astype(BF)
    low_ref[...] = low
    mixed_grad_ref[...] = dot(low, weight_attn, 1, 1).astype(BF)


def middle(tokens, mixed, cotangent, gain, weights):
    count = tokens.shape[0]
    size = min(256, count)
    wide = [(D, BF), (D, BF), (2 * FF, BF), (FF, BF), (D, BF), (D, BF), (D, F32)]
    return pl.pallas_call(
        middle_kernel,
        grid=(count // size,),
        in_specs=[
            rows((size, D)),
            rows((size, D)),
            rows((size, D)),
            whole((1, D)),
            whole(weights.shape),
        ],
        out_specs=[rows((size, width)) for width, _ in wide],
        out_shape=[jax.ShapeDtypeStruct((count, width), kind) for width, kind in wide],
        compiler_params=params(56),
        cost_estimate=pl.CostEstimate(
            flops=4 * count * D * (D + 3 * FF), bytes_accessed=count * D * 30, transcendentals=0
        ),
        name="middle",
    )(tokens, mixed, cotangent, gain, weights)


def attend_back_kernel(
    marks_ref,
    query_ref,
    mixed_grad_ref,
    log_ref,
    cos_ref,
    sin_ref,
    qkv_ref,
    lower_ref,
    upper_ref,
    grad_ref,
    edge_ref,
    away_ref,
    span_ref,
    sum_ref,
    sems,
):
    block = pl.program_id(0)
    count = qkv_ref.shape[0]

    @pl.when(block == 0)
    def _():
        fill_span(qkv_ref, lower_ref, upper_ref, span_ref, sems)
        sum_ref[0:BLOCK, :] = jnp.zeros((BLOCK, 2 * D), F32)

    bias = window_bias(marks_ref, block)
    start = pl.multiple_of(block * BLOCK, BLOCK)
    window = pl.ds(start, SPAN)
    older = pl.ds(start, BLOCK)
    newer = pl.ds(start + BLOCK, BLOCK)
    cosine = cos_ref[older, :]
    sine = sin_ref[older, :]
    for pair in range(PAIRS):
        lanes = slice(pair * LANES, (pair + 1) * LANES)
        value_lanes = slice(D + pair * LANES, D + (pair + 1) * LANES)
        query = stacked(query_ref[:, lanes] * BF(0.125))
        keys = span_ref[window, lanes]
        values = span_ref[window, value_lanes]
        out_grad = stacked(mixed_grad_ref[:, lanes])
        scores = dot(keys, query, 1, 1) + bias
        weights = jnp.exp(scores - log_ref[0, pair : pair + 1, :])
        weight_grad = dot(values, out_grad, 1, 1)
        score_grad = weights * (
            weight_grad - jnp.sum(weights * weight_grad, axis=0, keepdims=True)
        )
        score_grad = score_grad.astype(BF)
        key_grad = dot(score_grad, query)
        value_grad = dot(weights.astype(BF), out_grad)
        sum_ref[older, lanes] += key_grad[:BLOCK]
        sum_ref[newer, lanes] = key_grad[BLOCK:]
        sum_ref[older, value_lanes] += value_grad[:BLOCK]
        sum_ref[newer, value_lanes] = value_grad[BLOCK:]
        query_grad = unstacked(dot(score_grad, keys, 0, 0)) * 0.125
        query_grad = query_grad * cosine - swap_halves(query_grad) * sine
        grad_ref[older, lanes] = query_grad.astype(BF)

    @pl.when(block > 0)
    def _():
        own = pl.ds(pl.multiple_of(start - HALF, HALF), BLOCK)
        own_cosine = cos_ref[own, :]
        own_sine = sin_ref[own, :]
        for pair in range(PAIRS):
            lanes = slice(pair * LANES, (pair + 1) * LANES)
            done = sum_ref[older, lanes]
            done = done * own_cosine - swap_halves(done) * own_sine
            grad_ref[own, D + pair * LANES : D + (pair + 1) * LANES] = done.astype(BF)
        grad_ref[own, 2 * D :] = sum_ref[older, D:].astype(BF)

    @pl.when(block == pl.num_programs(0) - 1)
    def _():
        away_ref[0:HALF, :] = sum_ref[0:HALF, :].astype(BF)
        away_ref[HALF:, :] = sum_ref[count + HALF :, :].astype(BF)
        edge_ref[0:HALF, :] = sum_ref[HALF : 2 * HALF, :]
        edge_ref[HALF:, :] = sum_ref[count : count + HALF, :]


def attend_back(marks, qkv, mixed_grad, logs, cosine, sine, lower, upper):
    count = qkv.shape[0]
    return pl.pallas_call(
        attend_back_kernel,
        grid=(count // BLOCK,),
        in_specs=[
            SMEM,
            rows((BLOCK, D)),
            rows((BLOCK, D)),
            rows((1, 8, 2 * BLOCK)),
            whole((count, LANES)),
            whole((count, LANES)),
            ANY,
            ANY,
            ANY,
        ],
        out_specs=[whole((count, 3 * D)), whole((2 * HALF, 2 * D)), whole((2 * HALF, 2 * D))],
        out_shape=[
            jax.ShapeDtypeStruct((count, 3 * D), BF),
            jax.ShapeDtypeStruct((2 * HALF, 2 * D), F32),
            jax.ShapeDtypeStruct((2 * HALF, 2 * D), BF),
        ],
        scratch_shapes=[
            pltpu.VMEM((count + 2 * HALF, 2 * D), BF),
            pltpu.VMEM((count + 2 * HALF, 2 * D), F32),
            pltpu.SemaphoreType.DMA((3,)),
        ],
        compiler_params=params(48),
        cost_estimate=pl.CostEstimate(
            flops=10 * count * SPAN * D * 2, bytes_accessed=count * D * 20, transcendentals=0
        ),
        name="attend_back",
    )(marks, qkv, mixed_grad, logs, cosine, sine, qkv, lower, upper)


def patch_kernel(edge_ref, near_ref, cos_ref, sin_ref, _, out_ref):
    part = pl.program_id(1)
    total = edge_ref[...] + near_ref[...].astype(F32)

    @pl.when(part == 0)
    def _():
        cosine = cos_ref[...]
        sine = sin_ref[...]
        for pair in range(PAIRS):
            lanes = slice(pair * LANES, (pair + 1) * LANES)
            done = total[:, lanes]
            out_ref[:, lanes] = (done * cosine - swap_halves(done) * sine).astype(BF)

    @pl.when(part == 1)
    def _():
        out_ref[...] = total.astype(BF)


def patch(edge, near, cosine, sine, grads):
    last = grads.shape[0] // HALF - 1
    return pl.pallas_call(
        patch_kernel,
        grid=(2, 2),
        in_specs=[
            pl.BlockSpec((HALF, D), lambda side, part: (side, part)),
            pl.BlockSpec((HALF, D), lambda side, part: (side, part)),
            pl.BlockSpec((HALF, LANES), lambda side, part: (side * last, 0)),
            pl.BlockSpec((HALF, LANES), lambda side, part: (side * last, 0)),
            ANY,
        ],
        out_specs=pl.BlockSpec((HALF, D), lambda side, part: (side * last, 1 + part)),
        out_shape=jax.ShapeDtypeStruct(grads.shape, BF),
        input_output_aliases={4: 0},
        compiler_params=params(16),
        cost_estimate=pl.CostEstimate(flops=0, bytes_accessed=HALF * D * 24, transcendentals=0),
        name="patch",
    )(edge, near, cosine, sine, grads)


def input_grad_kernel(x_ref, gain_ref, w_ref, dqkv_ref, grad_ref, out_ref):
    unit, scale = normalized(x_ref[...].astype(F32))
    grad_normed = dot(dqkv_ref[:, :QKV_HALF], w_ref[0, :, :QKV_HALF], 1, 1) + dot(
        dqkv_ref[:, QKV_HALF:], w_ref[1, :, :QKV_HALF], 1, 1
    )
    out_ref[...] = grad_ref[...] + norm_back(grad_normed, unit, scale, gain_ref[...])


def input_grad(tokens, gain, weights, dqkv, grad):
    count = tokens.shape[0]
    size = min(256, count)
    return pl.pallas_call(
        input_grad_kernel,
        grid=(count // size,),
        in_specs=[
            rows((size, D)),
            whole((1, D)),
            whole(weights.shape),
            rows((size, 3 * D)),
            rows((size, D)),
        ],
        out_specs=rows((size, D)),
        out_shape=jax.ShapeDtypeStruct((count, D), F32),
        compiler_params=params(40),
        cost_estimate=pl.CostEstimate(
            flops=2 * count * D * 3 * D, bytes_accessed=count * D * 16, transcendentals=0
        ),
        name="input_grad",
    )(tokens, gain, weights, dqkv, grad)


CHIP_ROWS = 48
TILE = 384


def store_slots(slots_ref, out_ref, product):
    step = CHIP_ROWS
    for index in range(D // step):
        place = pl.multiple_of(slots_ref[1 + index] * step, 16)
        out_ref[pl.ds(place, step), :] = product[index * step : (index + 1) * step].astype(BF)


def qkv_weight_kernel(slots_ref, normed_ref, grad_ref, out_ref, turned_ref):
    @pl.when(pl.program_id(0) == 0)
    def _():
        turned_ref[...] = normed_ref[...].T

    store_slots(slots_ref, out_ref, dot(turned_ref[...], grad_ref[...]))


def qkv_weight_grad(slots, normed, dqkv):
    count = normed.shape[0]
    tiles = QKV_HALF // TILE
    return pl.pallas_call(
        qkv_weight_kernel,
        grid_spec=pltpu.PrefetchScalarGridSpec(
            num_scalar_prefetch=1,
            grid=(tiles,),
            in_specs=[
                pl.BlockSpec((count, D), lambda t, s: (0, 0)),
                pl.BlockSpec((count, TILE), lambda t, s: (0, s[0] * tiles + t)),
            ],
            out_specs=pl.BlockSpec((D, TILE), lambda t, s: (0, t)),
            scratch_shapes=[pltpu.VMEM((D, count), BF)],
        ),
        out_shape=jax.ShapeDtypeStruct((D, QKV_HALF), BF),
        compiler_params=params(32),
        cost_estimate=pl.CostEstimate(
            flops=2 * count * D * QKV_HALF, bytes_accessed=count * D * 8, transcendentals=0
        ),
        name="qkv_weight_grad",
    )(slots, normed, dqkv)


def ff_weight_kernel(slots_ref, normed_ref, cot_ref, mixed_ref, both_ref, hidden_ref, low_ref, out_ref, turned_ref):
    step = pl.program_id(0)
    second = slots_ref[0] == 1

    @pl.when((step == 0) & ~second)
    def _():
        turned_ref[...] = normed_ref[...].T

    @pl.when((step == 0) & second)
    def _():
        turned_ref[...] = cot_ref[...].T

    @pl.when((step == 3) & second)
    def _():
        turned_ref[...] = mixed_ref[...].T

    @pl.when(~second)
    def _():
        store_slots(slots_ref, out_ref, dot(turned_ref[...], both_ref[...]))

    @pl.when(second & (step < 3))
    def _():
        store_slots(slots_ref, out_ref, dot(turned_ref[...], hidden_ref[...]))

    @pl.when(second & (step >= 3) & (step < 5))
    def _():
        store_slots(slots_ref, out_ref, dot(turned_ref[...], low_ref[...]))

    @pl.when(second & (step == 5))
    def _():
        out_ref[...] = jnp.zeros_like(out_ref)


def ff_weight_grad(slots, normed, cot, mixed, both, hidden, low):
    count = normed.shape[0]
    full = pl.BlockSpec((count, D), lambda t, s: (0, 0))
    return pl.pallas_call(
        ff_weight_kernel,
        grid_spec=pltpu.PrefetchScalarGridSpec(
            num_scalar_prefetch=1,
            grid=(FF_HALF // TILE,),
            in_specs=[
                full,
                full,
                full,
                pl.BlockSpec((count, TILE), lambda t, s: (0, jnp.where(s[0] == 0, t, 0))),
                pl.BlockSpec((count, TILE), lambda t, s: (0, jnp.where(s[0] == 0, 0, jnp.minimum(t, 2)))),
                pl.BlockSpec(
                    (count, TILE), lambda t, s: (0, jnp.where(s[0] == 0, 0, jnp.clip(t - 3, 0, 1)))
                ),
            ],
            out_specs=pl.BlockSpec((D, TILE), lambda t, s: (0, t)),
            scratch_shapes=[pltpu.VMEM((D, count), BF)],
        ),
        out_shape=jax.ShapeDtypeStruct((D, FF_HALF), BF),
        compiler_params=params(40),
        cost_estimate=pl.CostEstimate(
            flops=2 * count * D * FF_HALF, bytes_accessed=count * D * 12, transcendentals=0
        ),
        name="ff_weight_grad",
    )(slots, normed, cot, mixed, both, hidden, low)


def doc_marks(doc_lengths, row_count):
    me = lax.axis_index("tok")
    ends = jnp.cumsum(doc_lengths).astype(jnp.int32)
    before = jnp.where(me > 0, ends[jnp.maximum(me - 1, 0)], 0)
    return jnp.stack([before, ends[me], ends[me + 1], me * row_count]).astype(jnp.int32)


def rotary_tables(marks, row_count):
    place = marks[3] + jnp.arange(row_count, dtype=jnp.int32)
    offset = place - jnp.where(place >= marks[1], marks[1], marks[0])
    frequency = 10000.0 ** (-jnp.arange(0, HEAD_DIM, 2, dtype=F32) / HEAD_DIM)
    angles = offset.astype(F32)[:, None] * frequency[None, :]
    cosine = jnp.cos(angles)
    sine = jnp.sin(angles)
    return (
        jnp.concatenate([cosine] * 4, axis=1),
        jnp.concatenate([-sine, sine, -sine, sine], axis=1),
    )


def passed_along(value, steps):
    count = lax.axis_size("tok")
    first, last = (max(0, -steps), min(count, count - steps))
    return lax.ppermute(value, "tok", [(at, at + steps) for at in range(first, last)])


def gathered(shard):
    full = lax.all_gather(shard, "tok", axis=0, tiled=True)
    half = full.shape[1] // 2
    return jnp.stack([full[:, :half], full[:, half:]])


def scattered(first, second):
    full = jnp.concatenate([first, second], axis=1)
    return lax.psum_scatter(full.astype(F32), "tok", scatter_dimension=0, tiled=True)


def on_device(
    tokens,
    doc_lengths,
    first_gain,
    qkv_weight,
    attn_weight,
    second_gain,
    feed_in_weight,
    feed_out_weight,
    cotangent,
):
    row_count = tokens.shape[0]
    share = first_gain.shape[0]

    def spread(gain):
        return jnp.broadcast_to(gain[:, None], (share, LANES))

    shard_one = jnp.concatenate(
        [
            qkv_weight[:, :QKV_HALF],
            spread(first_gain),
            qkv_weight[:, QKV_HALF:],
            spread(second_gain),
        ],
        axis=1,
    )
    shard_two = jnp.concatenate(
        [
            feed_in_weight,
            feed_out_weight.T,
            attn_weight,
            jnp.zeros((share, FF_HALF - FF - D), BF),
        ],
        axis=1,
    )
    marks = doc_marks(doc_lengths, row_count)
    cosine, sine = rotary_tables(marks, row_count)
    weights_one = gathered(shard_one)
    weights_two = gathered(shard_two)
    gain_one = weights_one[0, :, QKV_HALF].astype(F32)[None]
    gain_two = weights_one[1, :, QKV_HALF].astype(F32)[None]
    normed, qkv = project_qkv(tokens, gain_one, weights_one, cosine, sine)
    lower = passed_along(qkv[row_count - HALF :, D:], 1)
    upper = passed_along(qkv[:HALF, D:], -1)
    mixed, logs = attend(marks, qkv, lower, upper)
    result, normed_two, both, hidden, low, mixed_grad, grad = middle(
        tokens, mixed, cotangent, gain_two, weights_two
    )
    slots = jnp.arange(D // CHIP_ROWS, dtype=jnp.int32)

    def order(half):
        return jnp.concatenate([jnp.full((1,), half, jnp.int32), slots])

    grads_ff = [
        ff_weight_grad(order(half), normed_two, cotangent, mixed, both, hidden, low)
        for half in range(2)
    ]
    dqkv, edge, away = attend_back(marks, qkv, mixed_grad, logs, cosine, sine, lower, upper)
    from_upper = passed_along(away[:HALF], -1)
    from_lower = passed_along(away[HALF:], 1)
    dqkv = patch(edge, jnp.concatenate([from_lower, from_upper], axis=0), cosine, sine, dqkv)
    grads_qkv = [qkv_weight_grad(order(half), normed, dqkv) for half in range(2)]
    grad_in = input_grad(tokens, gain_one, weights_one, dqkv, grad)
    sum_ff = scattered(*grads_ff)
    sum_qkv = scattered(*grads_qkv)
    sent_in = sum_ff[:, : 2 * FF]
    sent_down = sum_ff[:, 2 * FF : 3 * FF].T
    sent_attn = sum_ff[:, 3 * FF : 3 * FF + D]

    def gain_grad(summed, weight, gain):
        return jnp.sum(summed * weight.astype(F32), axis=1) / gain.astype(F32)

    return (
        result,
        grad_in,
        gain_grad(sum_qkv, qkv_weight, first_gain),
        sum_qkv,
        sent_attn,
        gain_grad(sent_in, feed_in_weight, second_gain),
        sent_in,
        sent_down,
    )


def solution(mesh):
    in_specs = (
        P("tok", None),
        P(),
        P("tok"),
        P("tok", None),
        P("tok", None),
        P("tok"),
        P("tok", None),
        P(None, "tok"),
        P("tok", None),
    )
    out_specs = (
        P("tok", None),
        P("tok", None),
        P("tok"),
        P("tok", None),
        P("tok", None),
        P("tok"),
        P("tok", None),
        P(None, "tok"),
    )
    return jax.shard_map(
        on_device, mesh=mesh, in_specs=in_specs, out_specs=out_specs, check_vma=False
    )
```

time: 756 us -> 542 us (0.72); the launches traced: 746 us -> 541 us
  matrix products: 320 us -> 0 us
  waiting for transfers between devices: 178 us -> 345 us
  Pallas kernels: 0 us -> 102 us
  blocking collectives: 82.1 us -> 0 us
  local copies, waits for them, and re-layouts: 85.1 us -> 43.3 us
  other arithmetic: 56.2 us -> 27.8 us
    dot_general x24 -> x0, matrix products: 320 us -> none  [the longest x2 98.4 us: on_device(): jnp.einsum('hqk,qhd->khd', grad_scores_low, query_block, preferred_elemen...]
    reduce_scatter x3 -> x2, waiting for transfers between devices: 96 us -> 240 us  [scattered(): lax.psum_scatter(full.astype(F32), 'tok', scatter_dimension=0, tiled=True)]
    pallas_call x0 -> x10, Pallas kernels: none -> 102 us  [the longest x1 26.2 us: attend_back(): pl.pallas_call(attend_back_kernel, grid=(count // BLOCK,), in_specs=[SMEM...]
    unnamed x2 -> x0, blocking collectives: 82.1 us -> none
    slice x16 -> x4, local copies, waits for them, and re-layouts: 31.7 us -> 2.43 us  [the longest x1 1.52 us: on_device(): sent_attn = sum_ff[:, 3 * FF:3 * FF + D]]
    all_gather x4 -> x2, waiting for transfers between devices: 79.8 us -> 102 us  [gathered(): full = lax.all_gather(shard, 'tok', axis=0, tiled=True)]
    add x6 -> x0, other arithmetic: 11.1 us -> none  [the longest x1 6.2 us: on_device(): input_grad = grad_residual + grad_inputs_norm]
    convert_element_type x5, other arithmetic: 2.81 us -> 13.5 us  [the longest x2 12.6 us: scattered(): full.astype(F32)]
  transfers between devices with their start and end apart: 12 -> 8, of which waited for: 4 -> 5; matrix products, arithmetic and copies ran while one was open for 55% -> 4% of each run, Pallas kernels for 0% -> 8%
where the time goes in v1:
time: 542 us; the launch traced here: 541 us
  waiting for transfers between devices  345 us (64%)
  Pallas kernels  102 us (19%)
  local copies, waits for them, and re-layouts  43.3 us (8%)
  other arithmetic  27.8 us (5%)
  between operations  14.7 us (3%)
  starting transfers between devices  8.37 us (2%)
    reduce_scatter x2, waiting for transfers between devices, scattered(): lax.psum_scatter(full.astype(F32), 'tok', scatter_dimension=0, tiled=True)  240 us
    all_gather x2, waiting for transfers between devices, gathered(): full = lax.all_gather(shard, 'tok', axis=0, tiled=True)  102 us
    unnamed x50, local copies, waits for them, and re-layouts  30 us
    pallas_call x1, Pallas kernels, attend_back(): pl.pallas_call(attend_back_kernel, grid=(count // BLOCK,), in_specs=[SMEM...  26.2 us
    pallas_call x1, Pallas kernels, middle(): pl.pallas_call(middle_kernel, grid=(count // size,), in_specs=[rows((size...  25 us
    pallas_call x2, Pallas kernels, ff_weight_grad(): pl.pallas_call(ff_weight_kernel, grid_spec=pltpu.PrefetchScalarGridSpec(n...  17.6 us
    convert_element_type x2, other arithmetic, scattered(): full.astype(F32)  12.6 us
    pallas_call x1, Pallas kernels, attend(): pl.pallas_call(attend_kernel, grid=(blocks,), in_specs=[SMEM, rows((BLOCK...  11.3 us
  transfers between devices with their start and end apart: 8, of which 5 were waited for; matrix products, arithmetic and copies ran while one was open for 4% of the time, Pallas kernels for 8%

profile of v1, /device:TPU:0, one launch (start us, length us, event | category | flops | bytes accessed | tf_op | source)
XLA Modules:
  0.0 540.9 jit_solution(12680514519908232423)
XLA Ops:
  10.3 1.7 maximum_maximum_fusion
  14.7 1.9 fusion
  17.5 57.9 %all-gather.3.cloned.1.call-done = bf16[768,2560]{1,0:T(8,128)(2,1)} async-done(((bf16[24,2560]{1,0:T(8,128)(2,1)}), bf16[768,2560]{1,0:T(8,128)(2,1)}) %all-gather.3.cloned.1.call-update) | async-done | bytes 3932176 | tf_op jit(solution)/shard_map/all_gather | solution.py:596
  75.4 2.4 slice_bitcast_fusion.2
  79.5 5.8 %qkv.1 = (bf16[1024,768]{1,0:T(8,128)(2,1)S(1)}, bf16[1024,2304]{1,0:T(8,128)(2,1)S(1)}) custom-call(bf16[1024,768]{1,0:T(8,128)(2,1)S(1)} %copy-done.16, f32[1,768]{1,0:T(1,128)S(1)} %reshape.67.gain_ref, bf16[2,768,1280]{2,1,0:T(8,128)(2,1)S(1)} %pad_maximum_fusion.1.w_ref, f32[1024,128]{1,0:T(8,128)S(1)} %get-tuple-element.54.cos_ref, ...), custom_call_target="tpu_custom_call" | custom-call | flops 3623878656 | bytes 11403264 | tf_op jit(solution)/shard_map/qkv/pallas_call | solution.py:91
  86.7 3.2 collective-permute-start
  92.0 11.3 %attend.1 = (bf16[1024,768]{1,0:T(8,128)(2,1)S(1)}, f32[8,8,256]{2,1,0:T(8,128)S(1)}) custom-call(s32[4]{0:T(128)S(1)} %pad_add_fusion.marks_ref, bf16[1024,2304]{1,0:T(8,128)(2,1)S(1)} %get-tuple-element.22.query_ref.qkv_ref, bf16[1024,2304]{1,0:T(8,128)(2,1)S(1)} %get-tuple-element.22.query_ref.qkv_ref, ...), custom_call_target="tpu_custom_call" | custom-call | flops 1610612736 | bytes 7864320 | tf_op jit(solution)/shard_map/attend/pallas_call | solution.py:183
  103.3 2.2 copy-done.4
  106.7 43.9 %all-gather.5.cloned.1.call-done = bf16[768,4608]{1,0:T(8,128)(2,1)} async-done(((bf16[24,4608]{1,0:T(8,128)(2,1)}), bf16[768,4608]{1,0:T(8,128)(2,1)}) %all-gather.5.cloned.1.call-update) | async-done | bytes 7077904 | tf_op jit(solution)/shard_map/all_gather | solution.py:596
  150.6 3.5 slice_bitcast_fusion.1
  154.1 3.5 pad_maximum_fusion.w_ref
  157.6 25.0 %middle.1 = (bf16[1024,768]{1,0:T(8,128)(2,1)}, bf16[1024,768]{1,0:T(8,128)(2,1)}, bf16[1024,2304]{1,0:T(8,128)(2,1)}, bf16[1024,1152]{1,0:T(8,128)(2,1)}, bf16[...) custom-call(bf16[1024,768]{1,0:T(8,128)(2,1)} %x_ref.5, bf16[1024,768]{1,0:T(8,128)(2,1)} %copy-done.10, ...), custom_call_target="tpu_custom_call" | custom-call | flops 13287555072 | bytes 23592960 | tf_op jit(solution)/shard_map/middle/pallas_call | solution.py:262
  184.1 26.2 %attend_back.1 = (bf16[1024,2304]{1,0:T(8,128)(2,1)}, f32[128,1536]{1,0:T(8,128)S(1)}, bf16[128,1536]{1,0:T(8,128)(2,1)S(1)}) custom-call(s32[4]{0:T(128)S(1)} %pad_add_fusion.marks_ref, bf16[1024,2304]{1,0:T(8,128)(2,1)} %copy-done.4, bf16[1024,768]{1,0:T(8,128)(2,1)S(1)} %copy-done.20, f32[8,8,256]{2,1,0:T(8,128)S(1)} %get-tuple-element.26.log_ref, ...), custom_call_target="tpu_custom_call" | custom-call | flops 4026531840 | bytes 15728640 | tf_op jit(solution)/shard_map/attend_back/pallas_call | solution.py:360
  210.3 2.2 collective-permute-start.2
  214.0 2.6 collective-permute-done.3
  216.6 2.3 copy-done
  219.7 2.2 copy-done.1
  221.8 2.3 copy-done.2
  224.2 4.5 qkv_weight_grad.3
  228.7 4.5 qkv_weight_grad.2
  233.2 3.4 maximum_convert_fusion.1
  243.8 8.6 %ff_weight_grad.3 = bf16[768,2304]{1,0:T(8,128)(2,1)S(1)} custom-call(s32[17]{0:T(128)S(1)} %copy-done.19, bf16[1024,768]{1,0:T(8,128)(2,1)S(1)} %copy-done.13, bf16[1024,768]{1,0:T(8,128)(2,1)S(1)} %copy-done.9, bf16[1024,768]{1,0:T(8,128)(2,1)S(1)} %copy-done.11, bf16[1024,2304]{1,0:T(8,128)(2,1)} %get-tuple-element.33.both_ref, ...), custom_call_target="tpu_custom_call" | custom-call | flops 3623878656 | bytes 9437184 | tf_op jit(solution)/shard_map/ff_weight_grad/pallas_call | solution.py:542
  252.4 9.0 %ff_weight_grad.2 = bf16[768,2304]{1,0:T(8,128)(2,1)S(1)} custom-call(s32[17]{0:T(128)S(1)} %copy-done.18, bf16[1024,768]{1,0:T(8,128)(2,1)S(1)} %copy-done.13, bf16[1024,768]{1,0:T(8,128)(2,1)S(1)} %copy-done.9, bf16[1024,768]{1,0:T(8,128)(2,1)S(1)} %copy-done.12, bf16[1024,2304]{1,0:T(8,128)(2,1)} %get-tuple-element.33.both_ref, ...), custom_call_target="tpu_custom_call" | custom-call | flops 3623878656 | bytes 9437184 | tf_op jit(solution)/shard_map/ff_weight_grad/pallas_call | solution.py:542
  261.4 1.7 copy-done.7
  263.2 9.3 %maximum_convert_fusion = f32[768,4608]{1,0:T(8,128)} fusion(bf16[768,2304]{1,0:T(8,128)(2,1)S(1)} %ff_weight_grad.3, bf16[768,2304]{1,0:T(8,128)(2,1)} %copy-done.7), kind=kLoop, calls=%fused_computation.1 | loop fusion | flops 14155776 | bytes 21233664 | tf_op jit(solution)/shard_map/convert_element_type | solution.py:603
  272.5 2.0 copy-done.15
  274.4 2.5 copy-done.3
  276.9 2.3 copy-done.6
  280.7 6.7 %input_grad.1 = f32[1024,768]{1,0:T(8,128)} custom-call(bf16[1024,768]{1,0:T(8,128)(2,1)S(1)} %copy-done.17, f32[1,768]{1,0:T(1,128)S(1)} %reshape.67.gain_ref, bf16[2,768,1280]{2,1,0:T(8,128)(2,1)S(1)} %copy-done.6, bf16[1024,2304]{1,0:T(8,128)(2,1)S(1)} %copy-done.3, f32[1024,768]{1,0:T(8,128)S(1)} %copy-done.15), custom_call_target="tpu_custom_call" | custom-call | flops 3623878656 | bytes 12582912 | tf_op jit(solution)/shard_map/input_grad/pallas_call | solution.py:443
  287.3 72.7 %reduce-scatter.3.cloned.1.call-done = f32[24,2304]{1,0:T(8,128)} async-done(((f32[768,2304]{1,0:T(8,128)}), f32[24,2304]{1,0:T(8,128)}) %reduce-scatter.3.cloned.1.call-update) | async-done | bytes 221200 | tf_op jit(solution)/shard_map/reduce_scatter | solution.py:603
  361.6 167.4 %reduce-scatter.5.cloned.1.call-done = f32[24,4608]{1,0:T(8,128)} async-done(((f32[768,4608]{1,0:T(8,128)}), f32[24,4608]{1,0:T(8,128)}) %reduce-scatter.5.cloned.1.call-update) | async-done | bytes 442384 | tf_op jit(solution)/shard_map/reduce_scatter | solution.py:603
  529.0 1.7 multiply_reduce_fusion
  (82 shorter events, 30.0 us)
Async XLA Ops:
  7.2 68.2 %all-gather.3.cloned.1.call-start = ((), (), s32[]{:S(2)}) async-start(), calls=%async_computation.2 | async-start | bytes 4055040 | tf_op jit(solution)/shard_map/all_gather | solution.py:596
  10.2 140.4 %all-gather.5.cloned.1.call-start = ((), (), s32[]{:S(2)}) async-start(), calls=%async_computation.3 | async-start | bytes 7299072 | tf_op jit(solution)/shard_map/all_gather | solution.py:596
  12.0 348.0 %reduce-scatter.3.cloned.1.call-start = ((), (), s32[]{:S(2)}) async-start(), calls=%async_computation.4 | async-start | bytes 7299072 | tf_op jit(solution)/shard_map/reduce_scatter | solution.py:603
  77.9 1.6 copy-start.16
  78.3 7.0 %copy-start.5 = (bf16[2,768,1280]{2,1,0:T(8,128)(2,1)}, bf16[2,768,1280]{2,1,0:T(8,128)(2,1)S(1)}, u32[]{:S(2)}) copy-start(bf16[2,768,1280]{2,1,0:T(8,128)(2,1)S(1)} %pad_maximum_fusion.1.w_ref) | copy-start | bytes 11796484
  85.4 6.6 %collective-permute-start.1 = (bf16[64,1536]{1,0:T(8,128)(2,1)S(1)}, bf16[64,1536]{1,0:T(8,128)(2,1)S(1)}, u32[]{:S(2)}, u32[]{:S(2)}) collective-permute-start(bf16[64,1536]{1,0:T(8,128)(2,1)S(1)} %get-tuple-element.40), channel_id=1, source_target_pairs={{1,0},{2,1},{3,2},{4,3},{5,4},{6,5},{7,6},{8,7},{9,8},{10,9},{11,1... | collective-permute-start | bytes 589832 | tf_op jit(solution)/shard_map/ppermute | solution.py:592
  86.7 5.3 collective-permute-start
  103.3 2.2 copy-start.4
  182.6 1.4 copy-start.20
  210.3 3.7 collective-permute-start.2
  212.5 4.1 collective-permute-start.3
  216.6 2.3 copy-start
  219.0 2.9 copy-start.19
  219.7 2.2 copy-start.1
  221.8 2.3 copy-start.2
  224.2 4.5 copy-start.18
  236.5 1.7 copy-start.8
  236.5 292.5 %reduce-scatter.5.cloned.1.call-start = ((), (), s32[]{:S(2)}) async-start(), calls=%async_computation.5 | async-start | bytes 14598144 | tf_op jit(solution)/shard_map/reduce_scatter | solution.py:603
  238.2 1.4 copy-start.9
  239.6 1.4 copy-start.11
  241.0 1.4 copy-start.13
  242.4 1.4 copy-start.14
  243.8 8.6 %copy-start.12 = (bf16[1024,768]{1,0:T(8,128)(2,1)S(1)}, bf16[1024,768]{1,0:T(8,128)(2,1)}, u32[]{:S(2)}) copy-start(bf16[1024,768]{1,0:T(8,128)(2,1)} %copy-done.10) | copy-start | bytes 4718596
  261.4 1.8 copy-start.7
  272.4 2.0 copy-start.15
  274.4 2.5 copy-start.3
  276.9 2.3 copy-start.6
  279.2 1.5 copy-start.17
  280.7 79.3 %copy-start.21 = (bf16[24,2304]{1,0:T(8,128)(2,1)S(1)}, bf16[24,2304]{1,0:T(8,128)(2,1)}, u32[]{:S(2)}) copy-start(bf16[24,2304]{1,0:T(8,128)(2,1)} %param.12) | copy-start | bytes 331780
  280.7 80.4 %copy-start.23 = (bf16[24]{0:T(256)(128)(2,1)S(1)}, bf16[24]{0:T(256)(128)(2,1)}, u32[]{:S(2)}) copy-start(bf16[24]{0:T(256)(128)(2,1)} %param.11) | copy-start | bytes 148
  280.7 248.4 %copy-start.22 = (bf16[24,2304]{1,0:T(8,128)(2,1)S(1)}, bf16[24,2304]{1,0:T(8,128)(2,1)}, u32[]{:S(2)}) copy-start(bf16[24,2304]{1,0:T(8,128)(2,1)} %param.15) | copy-start | bytes 331780
  280.7 250.1 %copy-start.24 = (bf16[24]{0:T(256)(128)(2,1)S(1)}, bf16[24]{0:T(256)(128)(2,1)}, u32[]{:S(2)}) copy-start(bf16[24]{0:T(256)(128)(2,1)} %param.14) | copy-start | bytes 148
  (1 other events, 1.2 us)
Sparse Core Ops, SparseCore 0:
  11.5 63.8 all-gather.2
  78.8 71.7 all-gather.4
  236.7 123.2 reduce-scatter.2
  366.9 162.0 reduce-scatter.4

commit v2 on v1

--- a/solution.py
+++ b/solution.py
@@ -592,15 +592,124 @@
     return lax.ppermute(value, "tok", [(at, at + steps) for at in range(first, last)])
 
 
+STAGED_DEVICES = 32
+
+
+def staged():
+    return lax.axis_size("tok") == STAGED_DEVICES
+
+
+def exchange(value, by_core):
+    pairs = [(at, at ^ by_core[at & 1]) for at in range(lax.axis_size("tok"))]
+    return lax.ppermute(value, "tok", pairs)
+
+
+CORE = (1, 1)
+DEEP = tuple((step << 3, step << 3) for step in range(4))
+NEAR = (2, 4)
+FAR = (4, 2)
+
+
+def slot_codes(core):
+    slot = jnp.arange(16, dtype=jnp.int32)
+    depth, near, far = (slot & 3, (slot >> 2) & 1, slot >> 3)
+    return (depth << 2) | jnp.where(core == 0, (far << 1) | near, (near << 1) | far)
+
+
+def chip_slots(chip, core):
+    code = jnp.arange(16, dtype=jnp.int32) ^ chip
+    depth, second, first = (code >> 2, (code >> 1) & 1, code & 1)
+    return depth | jnp.where(core == 0, (second << 3) | (first << 2), (first << 3) | (second << 2))
+
+
+def assemble_kernel(places_ref, held_ref, far_ref, other_held_ref, other_far_ref, out_ref, sems):
+    core = places_ref[32]
+    copies = []
+    for index, source in enumerate((held_ref, far_ref, other_held_ref, other_far_ref)):
+        half = core if index < 2 else 1 - core
+        for slot in range(8):
+            at = index * 8 + slot
+            place = pl.multiple_of(places_ref[at] * CHIP_ROWS, 16)
+            copies.append(
+                pltpu.make_async_copy(
+                    source.at[pl.ds(slot * CHIP_ROWS, CHIP_ROWS)],
+                    out_ref.at[half, pl.ds(place, CHIP_ROWS)],
+                    sems.at[at],
+                )
+            )
+    for copy in copies:
+        copy.start()
+    for copy in copies:
+        copy.wait()
+
+
+def assemble(held, far, other_held, other_far):
+    me = lax.axis_index("tok")
+    core = me & 1
+    chip = me >> 1
+    places = jnp.concatenate(
+        [slot_codes(core) ^ chip, slot_codes(1 - core) ^ chip, jnp.full((1,), core, jnp.int32)]
+    )
+    width = held.shape[1]
+    return pl.pallas_call(
+        assemble_kernel,
+        in_specs=[SMEM, ANY, ANY, ANY, ANY],
+        out_specs=ANY,
+        out_shape=jax.ShapeDtypeStruct((2, D, width), BF),
+        scratch_shapes=[pltpu.SemaphoreType.DMA((32,))],
+        compiler_params=params(16),
+        cost_estimate=pl.CostEstimate(flops=0, bytes_accessed=8 * D * width, transcendentals=0),
+        name="assemble",
+    )(places, held, far, other_held, other_far)
+
+
 def gathered(shard):
-    full = lax.all_gather(shard, "tok", axis=0, tiled=True)
-    half = full.shape[1] // 2
-    return jnp.stack([full[:, :half], full[:, half:]])
-
-
-def scattered(first, second):
-    full = jnp.concatenate([first, second], axis=1)
-    return lax.psum_scatter(full.astype(F32), "tok", scatter_dimension=0, tiled=True)
+    if not staged():
+        full = lax.all_gather(shard, "tok", axis=0, tiled=True)
+        half = full.shape[1] // 2
+        return jnp.stack([full[:, :half], full[:, half:]])
+    core = lax.axis_index("tok") & 1
+    half = shard.shape[1] // 2
+    keep = jnp.where(core == 0, shard[:, :half], shard[:, half:])
+    send = jnp.where(core == 0, shard[:, half:], shard[:, :half])
+    came = exchange(send, CORE)
+    piece = jnp.concatenate(
+        [jnp.where(core == 0, keep, came), jnp.where(core == 0, came, keep)], axis=0
+    )
+    held = jnp.concatenate([piece] + [exchange(piece, DEEP[step]) for step in (1, 2, 3)], axis=0)
+    held = jnp.concatenate([held, exchange(held, NEAR)], axis=0)
+    far = exchange(held, FAR)
+    return assemble(held, far, exchange(held, CORE), exchange(far, CORE))
+
+
+def added(left, right):
+    return (left.astype(F32) + right.astype(F32)).astype(BF)
+
+
+def scattered(keep, send):
+    if not staged():
+        full = jnp.concatenate([keep, send], axis=1)
+        return lax.psum_scatter(full.astype(F32), "tok", scatter_dimension=0, tiled=True)
+    core = lax.axis_index("tok") & 1
+    came = exchange(send, CORE)
+    near, far = (added(keep[:384], came[:384]), added(keep[384:], came[384:]))
+    came = exchange(far, FAR)
+    near, far = (added(near[:192], came[:192]), added(near[192:], came[192:]))
+    came = exchange(far, NEAR)
+    parts = [
+        added(near[first : first + CHIP_ROWS], came[first : first + CHIP_ROWS])
+        for first in range(0, 192, CHIP_ROWS)
+    ]
+    total = parts[0].astype(F32)
+    for step in (1, 2, 3):
+        total = total + exchange(parts[step], DEEP[step]).astype(F32)
+    share = CHIP_ROWS // 2
+    lower, upper = (total[:share], total[share:])
+    own = jnp.where(core == 0, lower, upper)
+    came = exchange(jnp.where(core == 0, upper, lower), CORE)
+    return jnp.concatenate(
+        [jnp.where(core == 0, own, came), jnp.where(core == 0, came, own)], axis=1
+    )
 
 
 def on_device(
@@ -651,20 +760,28 @@
     result, normed_two, both, hidden, low, mixed_grad, grad = middle(
         tokens, mixed, cotangent, gain_two, weights_two
     )
-    slots = jnp.arange(D // CHIP_ROWS, dtype=jnp.int32)
+    if staged():
+        me = lax.axis_index("tok")
+        halves = (me & 1, 1 - (me & 1))
+    else:
+        halves = (0, 1)
 
     def order(half):
+        if staged():
+            slots = chip_slots(lax.axis_index("tok") >> 1, half)
+        else:
+            slots = jnp.arange(D // CHIP_ROWS, dtype=jnp.int32)
         return jnp.concatenate([jnp.full((1,), half, jnp.int32), slots])
 
     grads_ff = [
         ff_weight_grad(order(half), normed_two, cotangent, mixed, both, hidden, low)
-        for half in range(2)
+        for half in halves
     ]
     dqkv, edge, away = attend_back(marks, qkv, mixed_grad, logs, cosine, sine, lower, upper)
     from_upper = passed_along(away[:HALF], -1)
     from_lower = passed_along(away[HALF:], 1)
     dqkv = patch(edge, jnp.concatenate([from_lower, from_upper], axis=0), cosine, sine, dqkv)
-    grads_qkv = [qkv_weight_grad(order(half), normed, dqkv) for half in range(2)]
+    grads_qkv = [qkv_weight_grad(order(half), normed, dqkv) for half in halves]
     grad_in = input_grad(tokens, gain_one, weights_one, dqkv, grad)
     sum_ff = scattered(*grads_ff)
     sum_qkv = scattered(*grads_qkv)

time: 542 us -> 321 us (0.59)
  waiting for transfers between devices: 345 us -> 114 us
  starting transfers between devices: 8.37 us -> 50.3 us
  local copies, waits for them, and re-layouts: 43.3 us -> 23.9 us
  Pallas kernels: 102 us -> 115 us
  between operations: 14.7 us -> 1.97 us
  other arithmetic: 27.8 us -> 15.6 us
    reduce_scatter x2 -> x0, waiting for transfers between devices: 240 us -> none  [scattered(): lax.psum_scatter(full.astype(F32), 'tok', scatter_dimension=0, tiled=True)]
    ppermute x0 -> x30, waiting for transfers between devices: none -> 111 us  [exchange(): return lax.ppermute(value, 'tok', pairs)]
    all_gather x2 -> x0, waiting for transfers between devices: 102 us -> none  [gathered(): full = lax.all_gather(shard, 'tok', axis=0, tiled=True)]
    ppermute x0 -> x30, starting transfers between devices: none -> 42.3 us  [exchange(): return lax.ppermute(value, 'tok', pairs)]
    unnamed x50 -> x70, local copies, waits for them, and re-layouts: 30 us -> 17.3 us
    pallas_call x0 -> x2, Pallas kernels: none -> 11.3 us  [assemble(): pl.pallas_call(assemble_kernel, in_specs=[SMEM, ANY, ANY, ANY, ANY], out_...]
    convert_element_type x3 -> x6, other arithmetic: 12.7 us -> 5.66 us  [added(): return (left.astype(F32) + right.astype(F32)).astype(BF)]
    another operation x2 -> x0, local copies, waits for them, and re-layouts: 5.93 us -> none  [gathered(): return jnp.stack([full[:, :half], full[:, half:]])]
  transfers between devices with their start and end apart: 8 -> 34, of which waited for: 5 -> 16; matrix products, arithmetic and copies ran while one was open for 4% -> 6% of each run, Pallas kernels for 8% -> 23%
where the time goes in v2:
time: 321 us
  Pallas kernels  115 us (36%)
  waiting for transfers between devices  114 us (36%)
  starting transfers between devices  50.3 us (16%)
  local copies, waits for them, and re-layouts  23.9 us (7%)
  other arithmetic  15.6 us (5%)
    ppermute x30, waiting for transfers between devices, exchange(): return lax.ppermute(value, 'tok', pairs)  111 us
    ppermute x30, starting transfers between devices, exchange(): return lax.ppermute(value, 'tok', pairs)  42.3 us
    pallas_call x1, Pallas kernels, attend_back(): pl.pallas_call(attend_back_kernel, grid=(count // BLOCK,), in_specs=[SMEM...  26.2 us
    pallas_call x1, Pallas kernels, middle(): pl.pallas_call(middle_kernel, grid=(count // size,), in_specs=[rows((size...  25.1 us
    pallas_call x2, Pallas kernels, ff_weight_grad(): pl.pallas_call(ff_weight_kernel, grid_spec=pltpu.PrefetchScalarGridSpec(n...  18.1 us
    unnamed x70, local copies, waits for them, and re-layouts  17.3 us
    pallas_call x2, Pallas kernels, assemble(): pl.pallas_call(assemble_kernel, in_specs=[SMEM, ANY, ANY, ANY, ANY], out_...  11.3 us
    pallas_call x1, Pallas kernels, attend(): pl.pallas_call(attend_kernel, grid=(blocks,), in_specs=[SMEM, rows((BLOCK...  11.3 us
  transfers between devices with their start and end apart: 34, of which 16 were waited for; matrix products, arithmetic and copies ran while one was open for 6% of the time, Pallas kernels for 23%

profile of v2, /device:TPU:0, one launch (start us, length us, event | category | flops | bytes accessed | tf_op | source)
XLA Modules:
  0.0 320.6 jit_solution(9275400231732197577)
XLA Ops:
  4.8 5.1 %collective-permute-start.3 = (bf16[48,1280]{1,0:T(8,128)(2,1)S(1)}, bf16[48,1280]{1,0:T(8,128)(2,1)S(1)}, u32[]{:S(2)}, u32[]{:S(2)}) collective-permute-start(bf16[48,1280]{1,0:T(8,128)(2,1)S(1)} %pad_maximum_fusion.5), channel_id=1, source_target_pairs={{0,24},{1,25},{2,26},{3,27},{4,28},{5,29},{6,30},{7,31},{8,16},{9,... | collective-permute-start | bytes 368648 | tf_op jit(solution)/shard_map/ppermute | solution.py:604
  10.7 3.8 %collective-permute-start.13 = (bf16[48,2304]{1,0:T(8,128)(2,1)S(1)}, bf16[48,2304]{1,0:T(8,128)(2,1)S(1)}, u32[]{:S(2)}, u32[]{:S(2)}) collective-permute-start(bf16[48,2304]{1,0:T(8,128)(2,1)S(1)} %pad_maximum_fusion.3), channel_id=1, source_target_pairs={{0,24},{1,25},{2,26},{3,27},{4,28},{5,29},{6,30},{7,31},{8,16},{9,... | collective-permute-start | bytes 663560 | tf_op jit(solution)/shard_map/ppermute | solution.py:604
  15.8 12.4 %collective-permute-done.11 = bf16[48,2304]{1,0:T(8,128)(2,1)S(1)} collective-permute-done((bf16[48,2304]{1,0:T(8,128)(2,1)S(1)}, bf16[48,2304]{1,0:T(8,128)(2,1)S(1)}, u32[]{:S(2)}, u32[]{:S(2)}) %collective-permute-start.11) | collective-permute-done | bytes 221216 | tf_op jit(solution)/shard_map/ppermute | solution.py:604
  30.4 9.6 %collective-permute-done.12 = bf16[48,2304]{1,0:T(8,128)(2,1)S(1)} collective-permute-done((bf16[48,2304]{1,0:T(8,128)(2,1)S(1)}, bf16[48,2304]{1,0:T(8,128)(2,1)S(1)}, u32[]{:S(2)}, u32[]{:S(2)}) %collective-permute-start.12) | collective-permute-done | bytes 221216 | tf_op jit(solution)/shard_map/ppermute | solution.py:604
  43.7 10.8 %collective-permute-done.14 = bf16[192,2304]{1,0:T(8,128)(2,1)S(1)} collective-permute-done((bf16[192,2304]{1,0:T(8,128)(2,1)S(1)}, bf16[192,2304]{1,0:T(8,128)(2,1)S(1)}, u32[]{:S(2)}, u32[]{:S(2)}) %collective-permute-start.14) | collective-permute-done | bytes 884768 | tf_op jit(solution)/shard_map/ppermute | solution.py:604
  57.0 7.0 %collective-permute-done.4 = bf16[192,1280]{1,0:T(8,128)(2,1)S(1)} collective-permute-done((bf16[192,1280]{1,0:T(8,128)(2,1)S(1)}, bf16[192,1280]{1,0:T(8,128)(2,1)S(1)}, u32[]{:S(2)}, u32[]{:S(2)}) %collective-permute-start.4) | collective-permute-done | bytes 491552 | tf_op jit(solution)/shard_map/ppermute | solution.py:604
  65.7 23.1 %collective-permute-done.5.far_ref = bf16[384,1280]{1,0:T(8,128)(2,1)S(1)} collective-permute-done((bf16[384,1280]{1,0:T(8,128)(2,1)S(1)}, bf16[384,1280]{1,0:T(8,128)(2,1)S(1)}, u32[]{:S(2)}, u32[]{:S(2)}) %collective-permute-start.5) | collective-permute-done | bytes 983072 | tf_op jit(solution)/shard_map/ppermute | solution.py:604
  95.2 5.3 %assemble.2.w_ref = bf16[2,768,1280]{2,1,0:T(8,128)(2,1)S(1)} custom-call(s32[33]{0:T(128)S(1)} %pad_add_fusion.1.places_ref, bf16[384,1280]{1,0:T(8,128)(2,1)S(1)} %constant_dynamic-update-slice_fusion.5.held_ref, bf16[384,1280]{1,0:T(8,128)(2,1)S(1)} %collective-permute-done.5.far_ref, bf16[384,1280]{1,0:T(8,128)(2,1)} %collective-permute-done.6.other_held_ref, ...), custom_call_target="tpu_custom_call" | custom-call | bytes 7864320 | tf_op jit(solution)/shard_map/assemble/pallas_call | solution.py:654
  100.7 6.0 %qkv.1 = (bf16[1024,768]{1,0:T(8,128)(2,1)S(1)}, bf16[1024,2304]{1,0:T(8,128)(2,1)S(1)}) custom-call(bf16[1024,768]{1,0:T(8,128)(2,1)S(1)} %copy-done.17, f32[1,768]{1,0:T(1,128)S(1)} %reshape.67.gain_ref, bf16[2,768,1280]{2,1,0:T(8,128)(2,1)S(1)} %assemble.2.w_ref, f32[1024,128]{1,0:T(8,128)S(1)} %get-tuple-element.95.cos_ref, ...), custom_call_target="tpu_custom_call" | custom-call | flops 3623878656 | bytes 11403264 | tf_op jit(solution)/shard_map/qkv/pallas_call | solution.py:91
  108.1 3.2 %collective-permute-start.8 = (bf16[64,1536]{1,0:T(8,128)(2,1)S(1)}, bf16[64,1536]{1,0:T(8,128)(2,1)S(1)}, u32[]{:S(2)}, u32[]{:S(2)}) collective-permute-start(bf16[64,1536]{1,0:T(8,128)(2,1)S(1)} %get-tuple-element.53), channel_id=1, source_target_pairs={{0,1},{1,2},{2,3},{3,4},{4,5},{5,6},{6,7},{7,8},{8,9},{9,10},{10,1... | collective-permute-start | bytes 589832 | tf_op jit(solution)/shard_map/ppermute | solution.py:592
  113.3 11.3 %attend.1 = (bf16[1024,768]{1,0:T(8,128)(2,1)S(1)}, f32[8,8,256]{2,1,0:T(8,128)S(1)}) custom-call(s32[4]{0:T(128)S(1)} %pad_add_fusion.marks_ref, bf16[1024,2304]{1,0:T(8,128)(2,1)S(1)} %get-tuple-element.22.query_ref.qkv_ref, bf16[1024,2304]{1,0:T(8,128)(2,1)S(1)} %get-tuple-element.22.query_ref.qkv_ref, ...), custom_call_target="tpu_custom_call" | custom-call | flops 1610612736 | bytes 7864320 | tf_op jit(solution)/shard_map/attend/pallas_call | solution.py:183
  124.7 6.0 %assemble.3.w_ref = bf16[2,768,2304]{2,1,0:T(8,128)(2,1)S(1)} custom-call(s32[33]{0:T(128)S(1)} %pad_add_fusion.1.places_ref, bf16[384,2304]{1,0:T(8,128)(2,1)} %constant_dynamic-update-slice_fusion.16.held_ref, bf16[384,2304]{1,0:T(8,128)(2,1)} %collective-permute-done.15.far_ref, bf16[384,2304]{1,0:T(8,128)(2,1)S(1)} %collective-permute-done.16.other_held_ref, ...), custom_call_target="tpu_custom_call" | custom-call | bytes 14155776 | tf_op jit(solution)/shard_map/assemble/pallas_call | solution.py:654
  133.6 25.1 %middle.1 = (bf16[1024,768]{1,0:T(8,128)(2,1)}, bf16[1024,768]{1,0:T(8,128)(2,1)}, bf16[1024,2304]{1,0:T(8,128)(2,1)}, bf16[1024,1152]{1,0:T(8,128)(2,1)}, bf16[...) custom-call(bf16[1024,768]{1,0:T(8,128)(2,1)} %x_ref.5, bf16[1024,768]{1,0:T(8,128)(2,1)} %copy-done.10, ...), custom_call_target="tpu_custom_call" | custom-call | flops 13287555072 | bytes 23592960 | tf_op jit(solution)/shard_map/middle/pallas_call | solution.py:262
  163.2 9.2 %ff_weight_grad.3 = bf16[768,2304]{1,0:T(8,128)(2,1)} custom-call(s32[17]{0:T(128)S(1)} %pad_add_fusion.3.slots_ref, bf16[1024,768]{1,0:T(8,128)(2,1)S(1)} %copy-done.12, bf16[1024,768]{1,0:T(8,128)(2,1)S(1)} %copy-done.9, bf16[1024,768]{1,0:T(8,128)(2,1)S(1)} %copy-done.11, bf16[1024,2304]{1,0:T(8,128)(2,1)} %get-tuple-element.33.both_ref, ...), custom_call_target="tpu_custom_call" | custom-call | flops 3623878656 | bytes 9437184 | tf_op jit(solution)/shard_map/ff_weight_grad/pallas_call | solution.py:542
  172.5 4.7 %collective-permute-start.27 = (bf16[768,2304]{1,0:T(8,128)(2,1)}, bf16[768,2304]{1,0:T(8,128)(2,1)}, u32[]{:S(2)}, u32[]{:S(2)}) collective-permute-start(bf16[768,2304]{1,0:T(8,128)(2,1)} %ff_weight_grad.3), channel_id=1, source_target_pairs={{0,1},{1,0},{2,3},{3,2},{4,5},{5,4},{6,7},{7,6},{8,9},{9,8},{10,11... | collective-permute-start | bytes 10616840 | tf_op jit(solution)/shard_map/ppermute | solution.py:604
  177.1 26.2 %attend_back.1 = (bf16[1024,2304]{1,0:T(8,128)(2,1)}, f32[128,1536]{1,0:T(8,128)S(1)}, bf16[128,1536]{1,0:T(8,128)(2,1)S(1)}) custom-call(s32[4]{0:T(128)S(1)} %pad_add_fusion.marks_ref, bf16[1024,2304]{1,0:T(8,128)(2,1)} %copy-done.3, bf16[1024,768]{1,0:T(8,128)(2,1)S(1)} %copy-done.19, f32[8,8,256]{2,1,0:T(8,128)S(1)} %get-tuple-element.26.log_ref, ...), custom_call_target="tpu_custom_call" | custom-call | flops 4026531840 | bytes 15728640 | tf_op jit(solution)/shard_map/attend_back/pallas_call | solution.py:360
  206.9 3.0 collective-permute-done.19
  217.4 4.5 %qkv_weight_grad.3 = bf16[768,1152]{1,0:T(8,128)(2,1)S(1)} custom-call(s32[17]{0:T(128)S(1)} %pad_add_fusion.3.slots_ref, bf16[1024,768]{1,0:T(8,128)(2,1)S(1)} %get-tuple-element.31.normed_ref, bf16[1024,2304]{1,0:T(8,128)(2,1)S(1)} %copy-done.2), custom_call_target="tpu_custom_call" | custom-call | flops 1811939328 | bytes 6291456 | tf_op jit(solution)/shard_map/qkv_weight_grad/pallas_call | solution.py:485
  221.9 4.2 %collective-permute-start.20 = (bf16[768,1152]{1,0:T(8,128)(2,1)S(1)}, bf16[768,1152]{1,0:T(8,128)(2,1)}, u32[]{:S(2)}, u32[]{:S(2)}) collective-permute-start(bf16[768,1152]{1,0:T(8,128)(2,1)S(1)} %qkv_weight_grad.3), channel_id=1, source_target_pairs={{0,1},{1,0},{2,3},{3,2},{4,5},{5,4},{6,7},{7,6},{8,9},{9,8},{10,11... | collective-permute-start | bytes 5308424 | tf_op jit(solution)/shard_map/ppermute | solution.py:604
  226.2 8.9 %ff_weight_grad.2 = bf16[768,2304]{1,0:T(8,128)(2,1)S(1)} custom-call(s32[17]{0:T(128)S(1)} %pad_add_fusion.2.slots_ref, bf16[1024,768]{1,0:T(8,128)(2,1)S(1)} %copy-done.13, bf16[1024,768]{1,0:T(8,128)(2,1)S(1)} %copy-done.9, bf16[1024,768]{1,0:T(8,128)(2,1)S(1)} %copy-done.11, bf16[1024,2304]{1,0:T(8,128)(2,1)} %get-tuple-element.33.both_ref, ...), custom_call_target="tpu_custom_call" | custom-call | flops 3623878656 | bytes 9437184 | tf_op jit(solution)/shard_map/ff_weight_grad/pallas_call | solution.py:542
  235.2 4.5 %qkv_weight_grad.2 = bf16[768,1152]{1,0:T(8,128)(2,1)S(1)} custom-call(s32[17]{0:T(128)S(1)} %pad_add_fusion.2.slots_ref, bf16[1024,768]{1,0:T(8,128)(2,1)S(1)} %get-tuple-element.31.normed_ref, bf16[1024,2304]{1,0:T(8,128)(2,1)S(1)} %bitcast.13), custom_call_target="tpu_custom_call" | custom-call | flops 1811939328 | bytes 6291456 | tf_op jit(solution)/shard_map/qkv_weight_grad/pallas_call | solution.py:485
  242.7 2.9 add_convert_fusion.1
  246.6 8.0 %collective-permute-done.21 = bf16[384,1152]{1,0:T(8,128)(2,1)S(1)} collective-permute-done((bf16[384,1152]{1,0:T(8,128)(2,1)S(1)}, bf16[384,1152]{1,0:T(8,128)(2,1)S(1)}, u32[]{:S(2)}, u32[]{:S(2)}) %collective-permute-start.21) | collective-permute-done | bytes 884768 | tf_op jit(solution)/shard_map/ppermute | solution.py:604
  254.9 4.4 %collective-permute-start.22 = (bf16[192,1152]{1,0:T(8,128)(2,1)S(1)}, bf16[192,1152]{1,0:T(8,128)(2,1)S(1)}, u32[]{:S(2)}, u32[]{:S(2)}) collective-permute-start(bf16[192,1152]{1,0:T(8,128)(2,1)S(1)} %get-tuple-element.62), channel_id=1, source_target_pairs={{0,2},{1,5},{2,0},{3,7},{4,6},{5,1},{6,4},{7,3},{8,10},{9,13},{10,... | collective-permute-start | bytes 1327112 | tf_op jit(solution)/shard_map/ppermute | solution.py:604
  259.2 11.1 %collective-permute-done.22 = bf16[192,1152]{1,0:T(8,128)(2,1)S(1)} collective-permute-done((bf16[192,1152]{1,0:T(8,128)(2,1)S(1)}, bf16[192,1152]{1,0:T(8,128)(2,1)S(1)}, u32[]{:S(2)}, u32[]{:S(2)}) %collective-permute-start.22) | collective-permute-done | bytes 442400 | tf_op jit(solution)/shard_map/ppermute | solution.py:604
  274.0 3.6 %collective-permute-done.23 = bf16[48,1152]{1,0:T(8,128)(2,1)S(1)} collective-permute-done((bf16[48,1152]{1,0:T(8,128)(2,1)S(1)}, bf16[48,1152]{1,0:T(8,128)(2,1)S(1)}, u32[]{:S(2)}, u32[]{:S(2)}) %collective-permute-start.23) | collective-permute-done | bytes 110624 | tf_op jit(solution)/shard_map/ppermute | solution.py:604
  278.7 3.6 %collective-permute-done.24 = bf16[48,1152]{1,0:T(8,128)(2,1)S(1)} collective-permute-done((bf16[48,1152]{1,0:T(8,128)(2,1)S(1)}, bf16[48,1152]{1,0:T(8,128)(2,1)S(1)}, u32[]{:S(2)}, u32[]{:S(2)}) %collective-permute-start.24) | collective-permute-done | bytes 110624 | tf_op jit(solution)/shard_map/ppermute | solution.py:604
  285.0 6.8 %input_grad.1 = f32[1024,768]{1,0:T(8,128)} custom-call(bf16[1024,768]{1,0:T(8,128)(2,1)S(1)} %copy-done.18, f32[1,768]{1,0:T(1,128)S(1)} %reshape.67.gain_ref, bf16[2,768,1280]{2,1,0:T(8,128)(2,1)S(1)} %copy-done.5, bf16[1024,2304]{1,0:T(8,128)(2,1)S(1)} %bitcast.13, f32[1024,768]{1,0:T(8,128)S(1)} %copy-done.16), custom_call_target="tpu_custom_call" | custom-call | flops 3623878656 | bytes 12582912 | tf_op jit(solution)/shard_map/input_grad/pallas_call | solution.py:443
  291.8 4.2 %collective-permute-done.29 = bf16[192,2304]{1,0:T(8,128)(2,1)S(1)} collective-permute-done((bf16[192,2304]{1,0:T(8,128)(2,1)S(1)}, bf16[192,2304]{1,0:T(8,128)(2,1)S(1)}, u32[]{:S(2)}, u32[]{:S(2)}) %collective-permute-start.29) | collective-permute-done | bytes 884768 | tf_op jit(solution)/shard_map/ppermute | solution.py:604
  300.5 4.3 %collective-permute-done.30 = bf16[48,2304]{1,0:T(8,128)(2,1)S(1)} collective-permute-done((bf16[48,2304]{1,0:T(8,128)(2,1)S(1)}, bf16[48,2304]{1,0:T(8,128)(2,1)S(1)}, u32[]{:S(2)}, u32[]{:S(2)}) %collective-permute-start.30) | collective-permute-done | bytes 221216 | tf_op jit(solution)/shard_map/ppermute | solution.py:604
  304.8 3.5 %collective-permute-done.32 = bf16[48,2304]{1,0:T(8,128)(2,1)S(1)} collective-permute-done((bf16[48,2304]{1,0:T(8,128)(2,1)S(1)}, bf16[48,2304]{1,0:T(8,128)(2,1)S(1)}, u32[]{:S(2)}, u32[]{:S(2)}) %collective-permute-start.32) | collective-permute-done | bytes 221216 | tf_op jit(solution)/shard_map/ppermute | solution.py:604
  308.2 8.0 %collective-permute-done.31 = bf16[48,2304]{1,0:T(8,128)(2,1)S(1)} collective-permute-done((bf16[48,2304]{1,0:T(8,128)(2,1)S(1)}, bf16[48,2304]{1,0:T(8,128)(2,1)S(1)}, u32[]{:S(2)}, u32[]{:S(2)}) %collective-permute-start.31) | collective-permute-done | bytes 221216 | tf_op jit(solution)/shard_map/ppermute | solution.py:604
  (172 shorter events, 64.3 us)
Async XLA Ops:
  4.5 6.0 %collective-permute-start.10 = (bf16[24,2304]{1,0:T(8,128)(2,1)S(1)}, bf16[24,2304]{1,0:T(8,128)(2,1)S(1)}, u32[]{:S(2)}, u32[]{:S(2)}) collective-permute-start(bf16[24,2304]{1,0:T(8,128)(2,1)S(1)} %broadcast_select_fusion.4), channel_id=1, source_target_pairs={{0,1},{1,0},{2,3},{3,2},{4,5},{5,4},{6,7},{7,6},{8,9},{9,8},{10,11... | collective-permute-start | bytes 331784 | tf_op jit(solution)/shard_map/ppermute | solution.py:604
  4.8 38.3 %collective-permute-start.3 = (bf16[48,1280]{1,0:T(8,128)(2,1)S(1)}, bf16[48,1280]{1,0:T(8,128)(2,1)S(1)}, u32[]{:S(2)}, u32[]{:S(2)}) collective-permute-start(bf16[48,1280]{1,0:T(8,128)(2,1)S(1)} %pad_maximum_fusion.5), channel_id=1, source_target_pairs={{0,24},{1,25},{2,26},{3,27},{4,28},{5,29},{6,30},{7,31},{8,16},{9,... | collective-permute-start | bytes 368648 | tf_op jit(solution)/shard_map/ppermute | solution.py:604
  9.9 33.1 %collective-permute-start.2 = (bf16[48,1280]{1,0:T(8,128)(2,1)S(1)}, bf16[48,1280]{1,0:T(8,128)(2,1)S(1)}, u32[]{:S(2)}, u32[]{:S(2)}) collective-permute-start(bf16[48,1280]{1,0:T(8,128)(2,1)S(1)} %pad_maximum_fusion.5), channel_id=1, source_target_pairs={{0,16},{1,17},{2,18},{3,19},{4,20},{5,21},{6,22},{7,23},{8,24},{9,... | collective-permute-start | bytes 368648 | tf_op jit(solution)/shard_map/ppermute | solution.py:604
  9.9 33.1 %collective-permute-start.1 = (bf16[48,1280]{1,0:T(8,128)(2,1)S(1)}, bf16[48,1280]{1,0:T(8,128)(2,1)S(1)}, u32[]{:S(2)}, u32[]{:S(2)}) collective-permute-start(bf16[48,1280]{1,0:T(8,128)(2,1)S(1)} %pad_maximum_fusion.5), channel_id=1, source_target_pairs={{0,8},{1,9},{2,10},{3,11},{4,12},{5,13},{6,14},{7,15},{8,0},{9,1},... | collective-permute-start | bytes 368648 | tf_op jit(solution)/shard_map/ppermute | solution.py:604
  10.7 30.1 %collective-permute-start.13 = (bf16[48,2304]{1,0:T(8,128)(2,1)S(1)}, bf16[48,2304]{1,0:T(8,128)(2,1)S(1)}, u32[]{:S(2)}, u32[]{:S(2)}) collective-permute-start(bf16[48,2304]{1,0:T(8,128)(2,1)S(1)} %pad_maximum_fusion.3), channel_id=1, source_target_pairs={{0,24},{1,25},{2,26},{3,27},{4,28},{5,29},{6,30},{7,31},{8,16},{9,... | collective-permute-start | bytes 663560 | tf_op jit(solution)/shard_map/ppermute | solution.py:604
  14.5 13.7 %collective-permute-start.11 = (bf16[48,2304]{1,0:T(8,128)(2,1)S(1)}, bf16[48,2304]{1,0:T(8,128)(2,1)S(1)}, u32[]{:S(2)}, u32[]{:S(2)}) collective-permute-start(bf16[48,2304]{1,0:T(8,128)(2,1)S(1)} %pad_maximum_fusion.3), channel_id=1, source_target_pairs={{0,8},{1,9},{2,10},{3,11},{4,12},{5,13},{6,14},{7,15},{8,0},{9,1},... | collective-permute-start | bytes 663560 | tf_op jit(solution)/shard_map/ppermute | solution.py:604
  28.2 11.8 %collective-permute-start.12 = (bf16[48,2304]{1,0:T(8,128)(2,1)S(1)}, bf16[48,2304]{1,0:T(8,128)(2,1)S(1)}, u32[]{:S(2)}, u32[]{:S(2)}) collective-permute-start(bf16[48,2304]{1,0:T(8,128)(2,1)S(1)} %pad_maximum_fusion.3), channel_id=1, source_target_pairs={{0,16},{1,17},{2,18},{3,19},{4,20},{5,21},{6,22},{7,23},{8,24},{9,... | collective-permute-start | bytes 663560 | tf_op jit(solution)/shard_map/ppermute | solution.py:604
  41.5 13.0 %collective-permute-start.14 = (bf16[192,2304]{1,0:T(8,128)(2,1)S(1)}, bf16[192,2304]{1,0:T(8,128)(2,1)S(1)}, u32[]{:S(2)}, u32[]{:S(2)}) collective-permute-start(bf16[192,2304]{1,0:T(8,128)(2,1)S(1)} %get-tuple-element.71), channel_id=1, source_target_pairs={{0,2},{1,5},{2,0},{3,7},{4,6},{5,1},{6,4},{7,3},{8,10},{9,13},{10,... | collective-permute-start | bytes 2654216 | tf_op jit(solution)/shard_map/ppermute | solution.py:604
  43.1 20.9 %collective-permute-start.4 = (bf16[192,1280]{1,0:T(8,128)(2,1)S(1)}, bf16[192,1280]{1,0:T(8,128)(2,1)S(1)}, u32[]{:S(2)}, u32[]{:S(2)}) collective-permute-start(bf16[192,1280]{1,0:T(8,128)(2,1)S(1)} %get-tuple-element.77), channel_id=1, source_target_pairs={{0,2},{1,5},{2,0},{3,7},{4,6},{5,1},{6,4},{7,3},{8,10},{9,13},{10,... | collective-permute-start | bytes 1474568 | tf_op jit(solution)/shard_map/ppermute | solution.py:604
  55.5 36.4 %collective-permute-start.15 = (bf16[384,2304]{1,0:T(8,128)(2,1)}, bf16[384,2304]{1,0:T(8,128)(2,1)}, u32[]{:S(2)}, u32[]{:S(2)}) collective-permute-start(bf16[384,2304]{1,0:T(8,128)(2,1)} %constant_dynamic-update-slice_fusion.16.held_ref), channel_id=1, source_target_pairs={{0,4},{1,3},{2,6},{3,1},{4,0},{5,7},{6,2},{7,5},{8,12},{9,11},{10,... | collective-permute-start | bytes 5308424 | tf_op jit(solution)/shard_map/ppermute | solution.py:604
  64.1 24.7 %collective-permute-start.5 = (bf16[384,1280]{1,0:T(8,128)(2,1)S(1)}, bf16[384,1280]{1,0:T(8,128)(2,1)S(1)}, u32[]{:S(2)}, u32[]{:S(2)}) collective-permute-start(bf16[384,1280]{1,0:T(8,128)(2,1)S(1)} %constant_dynamic-update-slice_fusion.5.held_ref), channel_id=1, source_target_pairs={{0,4},{1,3},{2,6},{3,1},{4,0},{5,7},{6,2},{7,5},{8,12},{9,11},{10,... | collective-permute-start | bytes 2949128 | tf_op jit(solution)/shard_map/ppermute | solution.py:604
  65.7 29.5 %collective-permute-start.6 = (bf16[384,1280]{1,0:T(8,128)(2,1)S(1)}, bf16[384,1280]{1,0:T(8,128)(2,1)}, u32[]{:S(2)}, u32[]{:S(2)}) collective-permute-start(bf16[384,1280]{1,0:T(8,128)(2,1)S(1)} %constant_dynamic-update-slice_fusion.5.held_ref), channel_id=1, source_target_pairs={{0,1},{1,0},{2,3},{3,2},{4,5},{5,4},{6,7},{7,6},{8,9},{9,8},{10,11... | collective-permute-start | bytes 2949128 | tf_op jit(solution)/shard_map/ppermute | solution.py:604
  88.8 6.4 %collective-permute-start.7 = (bf16[384,1280]{1,0:T(8,128)(2,1)S(1)}, bf16[384,1280]{1,0:T(8,128)(2,1)}, u32[]{:S(2)}, u32[]{:S(2)}) collective-permute-start(bf16[384,1280]{1,0:T(8,128)(2,1)S(1)} %collective-permute-done.5.far_ref), channel_id=1, source_target_pairs={{0,1},{1,0},{2,3},{3,2},{4,5},{5,4},{6,7},{7,6},{8,9},{9,8},{10,11... | collective-permute-start | bytes 2949128 | tf_op jit(solution)/shard_map/ppermute | solution.py:604
  91.7 33.0 %collective-permute-start.16 = (bf16[384,2304]{1,0:T(8,128)(2,1)}, bf16[384,2304]{1,0:T(8,128)(2,1)S(1)}, u32[]{:S(2)}, u32[]{:S(2)}) collective-permute-start(bf16[384,2304]{1,0:T(8,128)(2,1)} %constant_dynamic-update-slice_fusion.16.held_ref), channel_id=1, source_target_pairs={{0,1},{1,0},{2,3},{3,2},{4,5},{5,4},{6,7},{7,6},{8,9},{9,8},{10,11... | collective-permute-start | bytes 5308424 | tf_op jit(solution)/shard_map/ppermute | solution.py:604
  91.9 32.8 %collective-permute-start.17 = (bf16[384,2304]{1,0:T(8,128)(2,1)}, bf16[384,2304]{1,0:T(8,128)(2,1)S(1)}, u32[]{:S(2)}, u32[]{:S(2)}) collective-permute-start(bf16[384,2304]{1,0:T(8,128)(2,1)} %collective-permute-done.15.far_ref), channel_id=1, source_target_pairs={{0,1},{1,0},{2,3},{3,2},{4,5},{5,4},{6,7},{7,6},{8,9},{9,8},{10,11... | collective-permute-start | bytes 5308424 | tf_op jit(solution)/shard_map/ppermute | solution.py:604
  106.8 6.6 %collective-permute-start.9 = (bf16[64,1536]{1,0:T(8,128)(2,1)S(1)}, bf16[64,1536]{1,0:T(8,128)(2,1)S(1)}, u32[]{:S(2)}, u32[]{:S(2)}) collective-permute-start(bf16[64,1536]{1,0:T(8,128)(2,1)S(1)} %get-tuple-element.52), channel_id=1, source_target_pairs={{1,0},{2,1},{3,2},{4,3},{5,4},{6,5},{7,6},{8,7},{9,8},{10,9},{11,1... | collective-permute-start | bytes 589832 | tf_op jit(solution)/shard_map/ppermute | solution.py:592
  108.1 5.3 %collective-permute-start.8 = (bf16[64,1536]{1,0:T(8,128)(2,1)S(1)}, bf16[64,1536]{1,0:T(8,128)(2,1)S(1)}, u32[]{:S(2)}, u32[]{:S(2)}) collective-permute-start(bf16[64,1536]{1,0:T(8,128)(2,1)S(1)} %get-tuple-element.53), channel_id=1, source_target_pairs={{0,1},{1,2},{2,3},{3,4},{4,5},{5,6},{6,7},{7,8},{8,9},{9,10},{10,1... | collective-permute-start | bytes 589832 | tf_op jit(solution)/shard_map/ppermute | solution.py:592
  172.5 70.3 %collective-permute-start.27 = (bf16[768,2304]{1,0:T(8,128)(2,1)}, bf16[768,2304]{1,0:T(8,128)(2,1)}, u32[]{:S(2)}, u32[]{:S(2)}) collective-permute-start(bf16[768,2304]{1,0:T(8,128)(2,1)} %ff_weight_grad.3), channel_id=1, source_target_pairs={{0,1},{1,0},{2,3},{3,2},{4,5},{5,4},{6,7},{7,6},{8,9},{9,8},{10,11... | collective-permute-start | bytes 10616840 | tf_op jit(solution)/shard_map/ppermute | solution.py:604
  203.4 3.5 %collective-permute-start.18 = (bf16[64,1536]{1,0:T(8,128)(2,1)S(1)}, bf16[64,1536]{1,0:T(8,128)(2,1)S(1)}, u32[]{:S(2)}, u32[]{:S(2)}) collective-permute-start(bf16[64,1536]{1,0:T(8,128)(2,1)S(1)} %get-tuple-element.67), channel_id=1, source_target_pairs={{0,1},{1,2},{2,3},{3,4},{4,5},{5,6},{6,7},{7,8},{8,9},{9,10},{10,1... | collective-permute-start | bytes 589832 | tf_op jit(solution)/shard_map/ppermute | solution.py:592
  205.3 4.5 %collective-permute-start.19 = (bf16[64,1536]{1,0:T(8,128)(2,1)S(1)}, bf16[64,1536]{1,0:T(8,128)(2,1)S(1)}, u32[]{:S(2)}, u32[]{:S(2)}) collective-permute-start(bf16[64,1536]{1,0:T(8,128)(2,1)S(1)} %get-tuple-element.68), channel_id=1, source_target_pairs={{1,0},{2,1},{3,2},{4,3},{5,4},{6,5},{7,6},{8,7},{9,8},{10,9},{11,1... | collective-permute-start | bytes 589832 | tf_op jit(solution)/shard_map/ppermute | solution.py:592
  221.9 17.7 %collective-permute-start.20 = (bf16[768,1152]{1,0:T(8,128)(2,1)S(1)}, bf16[768,1152]{1,0:T(8,128)(2,1)}, u32[]{:S(2)}, u32[]{:S(2)}) collective-permute-start(bf16[768,1152]{1,0:T(8,128)(2,1)S(1)} %qkv_weight_grad.3), channel_id=1, source_target_pairs={{0,1},{1,0},{2,3},{3,2},{4,5},{5,4},{6,7},{7,6},{8,9},{9,8},{10,11... | collective-permute-start | bytes 5308424 | tf_op jit(solution)/shard_map/ppermute | solution.py:604
  241.5 13.1 %collective-permute-start.21 = (bf16[384,1152]{1,0:T(8,128)(2,1)S(1)}, bf16[384,1152]{1,0:T(8,128)(2,1)S(1)}, u32[]{:S(2)}, u32[]{:S(2)}) collective-permute-start(bf16[384,1152]{1,0:T(8,128)(2,1)S(1)} %get-tuple-element.57), channel_id=1, source_target_pairs={{0,4},{1,3},{2,6},{3,1},{4,0},{5,7},{6,2},{7,5},{8,12},{9,11},{10,... | collective-permute-start | bytes 2654216 | tf_op jit(solution)/shard_map/ppermute | solution.py:604
  245.7 36.7 %collective-permute-start.28 = (bf16[384,2304]{1,0:T(8,128)(2,1)S(1)}, bf16[384,2304]{1,0:T(8,128)(2,1)S(1)}, u32[]{:S(2)}, u32[]{:S(2)}) collective-permute-start(bf16[384,2304]{1,0:T(8,128)(2,1)S(1)} %get-tuple-element.51), channel_id=1, source_target_pairs={{0,4},{1,3},{2,6},{3,1},{4,0},{5,7},{6,2},{7,5},{8,12},{9,11},{10,... | collective-permute-start | bytes 5308424 | tf_op jit(solution)/shard_map/ppermute | solution.py:604
  254.9 15.5 %collective-permute-start.22 = (bf16[192,1152]{1,0:T(8,128)(2,1)S(1)}, bf16[192,1152]{1,0:T(8,128)(2,1)S(1)}, u32[]{:S(2)}, u32[]{:S(2)}) collective-permute-start(bf16[192,1152]{1,0:T(8,128)(2,1)S(1)} %get-tuple-element.62), channel_id=1, source_target_pairs={{0,2},{1,5},{2,0},{3,7},{4,6},{5,1},{6,4},{7,3},{8,10},{9,13},{10,... | collective-permute-start | bytes 1327112 | tf_op jit(solution)/shard_map/ppermute | solution.py:604
  270.4 7.1 %collective-permute-start.23 = (bf16[48,1152]{1,0:T(8,128)(2,1)S(1)}, bf16[48,1152]{1,0:T(8,128)(2,1)S(1)}, u32[]{:S(2)}, u32[]{:S(2)}) collective-permute-start(bf16[48,1152]{1,0:T(8,128)(2,1)S(1)} %get-tuple-element.63), channel_id=1, source_target_pairs={{0,8},{1,9},{2,10},{3,11},{4,12},{5,13},{6,14},{7,15},{8,0},{9,1},... | collective-permute-start | bytes 331784 | tf_op jit(solution)/shard_map/ppermute | solution.py:604
  271.3 7.4 %collective-permute-start.25 = (bf16[48,1152]{1,0:T(8,128)(2,1)S(1)}, bf16[48,1152]{1,0:T(8,128)(2,1)S(1)}, u32[]{:S(2)}, u32[]{:S(2)}) collective-permute-start(bf16[48,1152]{1,0:T(8,128)(2,1)S(1)} %get-tuple-element.64), channel_id=1, source_target_pairs={{0,24},{1,25},{2,26},{3,27},{4,28},{5,29},{6,30},{7,31},{8,16},{9,... | collective-permute-start | bytes 331784 | tf_op jit(solution)/shard_map/ppermute | solution.py:604
  272.9 9.4 %collective-permute-start.24 = (bf16[48,1152]{1,0:T(8,128)(2,1)S(1)}, bf16[48,1152]{1,0:T(8,128)(2,1)S(1)}, u32[]{:S(2)}, u32[]{:S(2)}) collective-permute-start(bf16[48,1152]{1,0:T(8,128)(2,1)S(1)} %get-tuple-element.65), channel_id=1, source_target_pairs={{0,16},{1,17},{2,18},{3,19},{4,20},{5,21},{6,22},{7,23},{8,24},{9,... | collective-permute-start | bytes 331784 | tf_op jit(solution)/shard_map/ppermute | solution.py:604
  282.8 13.1 %collective-permute-start.29 = (bf16[192,2304]{1,0:T(8,128)(2,1)S(1)}, bf16[192,2304]{1,0:T(8,128)(2,1)S(1)}, u32[]{:S(2)}, u32[]{:S(2)}) collective-permute-start(bf16[192,2304]{1,0:T(8,128)(2,1)S(1)} %get-tuple-element.55), channel_id=1, source_target_pairs={{0,2},{1,5},{2,0},{3,7},{4,6},{5,1},{6,4},{7,3},{8,10},{9,13},{10,... | collective-permute-start | bytes 2654216 | tf_op jit(solution)/shard_map/ppermute | solution.py:604
  284.7 7.1 %collective-permute-start.26 = (f32[24,1152]{1,0:T(8,128)S(1)}, f32[24,1152]{1,0:T(8,128)S(1)}, u32[]{:S(2)}, u32[]{:S(2)}) collective-permute-start(f32[24,1152]{1,0:T(8,128)S(1)} %slice_select_fusion.2), channel_id=1, source_target_pairs={{0,1},{1,0},{2,3},{3,2},{4,5},{5,4},{6,7},{7,6},{8,9},{9,8},{10,11... | collective-permute-start | bytes 331784 | tf_op jit(solution)/shard_map/ppermute | solution.py:604
  296.1 8.6 %collective-permute-start.30 = (bf16[48,2304]{1,0:T(8,128)(2,1)S(1)}, bf16[48,2304]{1,0:T(8,128)(2,1)S(1)}, u32[]{:S(2)}, u32[]{:S(2)}) collective-permute-start(bf16[48,2304]{1,0:T(8,128)(2,1)S(1)} %get-tuple-element.58), channel_id=1, source_target_pairs={{0,8},{1,9},{2,10},{3,11},{4,12},{5,13},{6,14},{7,15},{8,0},{9,1},... | collective-permute-start | bytes 663560 | tf_op jit(solution)/shard_map/ppermute | solution.py:604
  296.2 12.0 %collective-permute-start.32 = (bf16[48,2304]{1,0:T(8,128)(2,1)S(1)}, bf16[48,2304]{1,0:T(8,128)(2,1)S(1)}, u32[]{:S(2)}, u32[]{:S(2)}) collective-permute-start(bf16[48,2304]{1,0:T(8,128)(2,1)S(1)} %get-tuple-element.59), channel_id=1, source_target_pairs={{0,24},{1,25},{2,26},{3,27},{4,28},{5,29},{6,30},{7,31},{8,16},{9,... | collective-permute-start | bytes 663560 | tf_op jit(solution)/shard_map/ppermute | solution.py:604
  297.9 18.4 %collective-permute-start.31 = (bf16[48,2304]{1,0:T(8,128)(2,1)S(1)}, bf16[48,2304]{1,0:T(8,128)(2,1)S(1)}, u32[]{:S(2)}, u32[]{:S(2)}) collective-permute-start(bf16[48,2304]{1,0:T(8,128)(2,1)S(1)} %get-tuple-element.60), channel_id=1, source_target_pairs={{0,16},{1,17},{2,18},{3,19},{4,20},{5,21},{6,22},{7,23},{8,24},{9,... | collective-permute-start | bytes 663560 | tf_op jit(solution)/shard_map/ppermute | solution.py:604
  (33 other events, 370.1 us)

commit v3 on v1

v3 whole, which is shorter than its diff:
```python
from functools import partial

import jax
import jax.numpy as jnp
from jax import lax
from jax.experimental import pallas as pl
from jax.experimental.pallas import tpu as pltpu
from jax.sharding import PartitionSpec as P

D = 768
FF = 1152
HEADS = 12
HEAD_DIM = 64
HALF = 64
PAIRS = HEADS // 2
BLOCK = 128
SPAN = BLOCK + 2 * HALF
LANES = 128
QKV_HALF = 3 * D // 2
GROUP = D // 2
GROUP_PAIRS = PAIRS // 2
FF_HALF = 2 * FF
MIB = 1024 * 1024
BF = jnp.bfloat16
F32 = jnp.float32


def dot(left, right, left_dim=1, right_dim=0):
    return lax.dot_general(
        left, right, (((left_dim,), (right_dim,)), ((), ())), preferred_element_type=F32
    )


def params(mib):
    return pltpu.CompilerParams(vmem_limit_bytes=mib * MIB)


def whole(shape):
    return pl.BlockSpec(shape, lambda *_: (0,) * len(shape))


def rows(shape):
    return pl.BlockSpec(shape, lambda i: (i,) + (0,) * (len(shape) - 1))


SMEM = pl.BlockSpec(memory_space=pltpu.SMEM)
ANY = pl.BlockSpec(memory_space=pl.ANY)
VMEM = pl.BlockSpec(memory_space=pltpu.VMEM)


def lane_ids(shape):
    return lax.broadcasted_iota(jnp.int32, shape, len(shape) - 1)


def swap_halves(values):
    low = (lane_ids(values.shape) & (HEAD_DIM - 1)) < HEAD_DIM // 2
    return jnp.where(
        low, pltpu.roll(values, LANES - HEAD_DIM // 2, 1), pltpu.roll(values, HEAD_DIM // 2, 1)
    )


def normalized(values):
    centered = values - jnp.mean(values, axis=-1, keepdims=True)
    scale = lax.rsqrt(jnp.mean(centered * centered, axis=-1, keepdims=True) + 1e-05)
    return centered * scale, scale


def norm_back(grad, unit, scale, gains):
    grad_unit = grad * gains
    return scale * (
        grad_unit
        - jnp.mean(grad_unit, axis=-1, keepdims=True)
        - unit * jnp.mean(grad_unit * unit, axis=-1, keepdims=True)
    )


CHIP_ROWS = 48


class Weights:
    def __init__(self, arrays, places=None):
        self.arrays = arrays
        self.places = places

    def operands(self):
        if self.places is None:
            return list(self.arrays)
        return [self.places, *self.arrays]

    def specs(self):
        if self.places is None:
            return [ANY]
        return [SMEM, VMEM, VMEM, VMEM, VMEM]

    def scratch(self):
        width = self.arrays[0].shape[-1]
        return [pltpu.VMEM((2, D, width), BF), pltpu.SemaphoreType.DMA((1,))]


def load_weights(refs, out_ref, sems):
    if len(refs) == 1:
        copy = pltpu.make_async_copy(refs[0], out_ref, sems.at[0])
        copy.start()
        copy.wait()
        return
    places_ref = refs[0]
    core = places_ref[32]
    for index, source in enumerate(refs[1:]):
        half = core if index < 2 else 1 - core
        for slot in range(8):
            place = pl.multiple_of(places_ref[index * 8 + slot] * CHIP_ROWS, 16)
            out_ref[half, pl.ds(place, CHIP_ROWS), :] = source[
                slot * CHIP_ROWS : (slot + 1) * CHIP_ROWS, :
            ]


def qkv_kernel(count, x_ref, cos_ref, sin_ref, *refs):
    weight_refs = refs[:count]
    normed_ref, qkv_ref, gains_ref, w_ref, sems = refs[count:]

    @pl.when(pl.program_id(0) == 0)
    def _():
        load_weights(weight_refs, w_ref, sems)
        for half in range(2):
            turned = w_ref[half, :, QKV_HALF:].T.astype(F32)
            gains_ref[half * 8 : half * 8 + 8, :] = turned[:8]

    unit, _ = normalized(x_ref[...].astype(F32))
    normed = (unit * gains_ref[0:1, :]).astype(BF)
    normed_ref[...] = normed
    cosine = cos_ref[...]
    sine = sin_ref[...]
    for half in range(2):
        merged = dot(normed, w_ref[half, :, :QKV_HALF])
        for tile in range(QKV_HALF // LANES):
            lanes = slice(tile * LANES, (tile + 1) * LANES)
            part = merged[:, lanes]
            if tile * LANES < 2 * GROUP:
                part = part * cosine + swap_halves(part) * sine
            qkv_ref[half, :, lanes] = part.astype(BF)


def project_qkv(tokens, weights, cosine, sine):
    count = tokens.shape[0]
    size = min(256, count)
    operands = weights.operands()
    return pl.pallas_call(
        partial(qkv_kernel, len(operands)),
        grid=(count // size,),
        in_specs=[rows((size, D)), rows((size, LANES)), rows((size, LANES)), *weights.specs()],
        out_specs=[
            rows((size, D)),
            pl.BlockSpec((2, size, QKV_HALF), lambda i: (0, i, 0)),
            whole((16, D)),
        ],
        out_shape=[
            jax.ShapeDtypeStruct((count, D), BF),
            jax.ShapeDtypeStruct((2, count, QKV_HALF), BF),
            jax.ShapeDtypeStruct((16, D), F32),
        ],
        scratch_shapes=weights.scratch(),
        compiler_params=params(32),
        cost_estimate=pl.CostEstimate(
            flops=2 * count * D * 3 * D, bytes_accessed=count * D * 10 + 6 * D * D, transcendentals=0
        ),
        name="qkv",
    )(tokens, cosine, sine, *operands)


def window_bias(marks_ref, block):
    shape = (SPAN, 2 * BLOCK)
    first = marks_ref[3] + block * BLOCK
    key = lax.broadcasted_iota(jnp.int32, shape, 0)
    query = lax.broadcasted_iota(jnp.int32, (1, 2 * BLOCK), 1) & (BLOCK - 1)
    place = first + query
    lowest = query
    highest = query + 2 * HALF
    for index in range(3):
        mark = marks_ref[index]
        edge = mark - first + HALF
        past = place >= mark
        lowest = jnp.where(past, jnp.maximum(lowest, edge), lowest)
        highest = jnp.where(past, highest, jnp.minimum(highest, edge - 1))
    return jnp.where((key >= lowest) & (key <= highest), 0.0, -1e30).astype(F32)


def stacked(pair):
    low = lane_ids(pair.shape) < HEAD_DIM
    zero = jnp.zeros_like(pair)
    return jnp.concatenate([jnp.where(low, pair, zero), jnp.where(low, zero, pair)], axis=0)


def unstacked(both):
    low = lane_ids((BLOCK, LANES)) < HEAD_DIM
    return jnp.where(low, both[:BLOCK], both[BLOCK:])


def attend_kernel(marks_ref, query_ref, qkv_ref, lower_ref, upper_ref, out_ref, log_ref, span_ref, sems):
    block = pl.program_id(0)
    count = qkv_ref.shape[1]

    @pl.when(block == 0)
    def _():
        copies = []
        for half in range(2):
            copies += [
                pltpu.make_async_copy(
                    qkv_ref.at[half, :, pl.ds(GROUP, 2 * GROUP)],
                    span_ref.at[half, pl.ds(HALF, count)],
                    sems.at[3 * half],
                ),
                pltpu.make_async_copy(
                    lower_ref.at[half], span_ref.at[half, pl.ds(0, HALF)], sems.at[3 * half + 1]
                ),
                pltpu.make_async_copy(
                    upper_ref.at[half],
                    span_ref.at[half, pl.ds(HALF + count, HALF)],
                    sems.at[3 * half + 2],
                ),
            ]
        for copy in copies:
            copy.start()
        for copy in copies:
            copy.wait()

    bias = window_bias(marks_ref, block)
    window = pl.ds(pl.multiple_of(block * BLOCK, BLOCK), SPAN)
    for pair in range(PAIRS):
        half = pair // GROUP_PAIRS
        first = (pair % GROUP_PAIRS) * LANES
        lanes = slice(first, first + LANES)
        query = stacked(query_ref[half, :, lanes] * BF(0.125))
        keys = span_ref[half, window, lanes]
        values = span_ref[half, window, GROUP + first : GROUP + first + LANES]
        scores = dot(keys, query, 1, 1) + bias
        peak = jnp.max(scores, axis=0, keepdims=True)
        expo = jnp.exp(scores - peak)
        total = jnp.sum(expo, axis=0, keepdims=True)
        weights = (expo * (1.0 / total)).astype(BF)
        out_ref[:, pair * LANES : (pair + 1) * LANES] = unstacked(dot(weights, values, 0, 0)).astype(BF)
        log_ref[0, half, pair % GROUP_PAIRS : pair % GROUP_PAIRS + 1, :] = peak + jnp.log(total)


def attend(marks, qkv, lower, upper):
    count = qkv.shape[1]
    blocks = count // BLOCK
    return pl.pallas_call(
        attend_kernel,
        grid=(blocks,),
        in_specs=[SMEM, pl.BlockSpec((2, BLOCK, GROUP), lambda i: (0, i, 0)), ANY, ANY, ANY],
        out_specs=[rows((BLOCK, D)), rows((1, 2, 8, 2 * BLOCK))],
        out_shape=[
            jax.ShapeDtypeStruct((count, D), BF),
            jax.ShapeDtypeStruct((blocks, 2, 8, 2 * BLOCK), F32),
        ],
        scratch_shapes=[
            pltpu.VMEM((2, count + 2 * HALF, 2 * GROUP), BF),
            pltpu.SemaphoreType.DMA((6,)),
        ],
        compiler_params=params(32),
        cost_estimate=pl.CostEstimate(
            flops=4 * count * SPAN * D * 2, bytes_accessed=count * D * 10, transcendentals=0
        ),
        name="attend",
    )(marks, qkv, qkv, lower, upper)


FF_PARTS = tuple((first, min(256, FF - first)) for first in range(0, FF, 256))


def middle_kernel(
    x_ref,
    mixed_ref,
    cot_ref,
    gains_ref,
    w_ref,
    result_ref,
    normed_ref,
    both_ref,
    hidden_ref,
    low_ref,
    mixed_grad_ref,
    grad_ref,
):
    gain = gains_ref[8:9, :]
    cot = cot_ref[...]
    weight_attn = w_ref[:, 3 * FF :]
    residual = x_ref[...].astype(F32) + dot(mixed_ref[...], weight_attn)
    unit, scale = normalized(residual)
    normed = (unit * gain).astype(BF)
    normed_ref[...] = normed
    result = residual
    grad_normed = None
    for first, size in FF_PARTS:
        gate_cols = slice(first, first + size)
        down_cols = slice(2 * FF + first, 2 * FF + first + size)
        up_cols = slice(FF + first, FF + first + size)
        gate = dot(normed, w_ref[:, gate_cols])
        up = dot(normed, w_ref[:, up_cols])
        grad_hidden = dot(cot, w_ref[:, down_cols])
        share = 0.5 + 0.5 * lax.erf(gate * 0.7071067811865476)
        active = gate * share
        slope = share + gate * (jnp.exp(-0.5 * gate * gate) * 0.3989422804014327)
        hidden = (active * up).astype(BF)
        hidden_ref[:, gate_cols] = hidden
        grad_gate = (grad_hidden * up * slope).astype(BF)
        grad_up = (grad_hidden * active).astype(BF)
        both_ref[:, gate_cols] = grad_gate
        both_ref[:, up_cols] = grad_up
        result = result + dot(hidden, w_ref[:, down_cols], 1, 1)
        piece = dot(grad_gate, w_ref[:, gate_cols], 1, 1) + dot(
            grad_up, w_ref[:, up_cols], 1, 1
        )
        grad_normed = piece if grad_normed is None else grad_normed + piece
    result_ref[...] = result.astype(BF)
    grad = cot.astype(F32) + norm_back(grad_normed, unit, scale, gain)
    grad_ref[...] = grad
    low = grad.astype(BF)
    low_ref[...] = low
    mixed_grad_ref[...] = dot(low, weight_attn, 1, 1).astype(BF)


def middle(tokens, mixed, cotangent, gains, weights):
    count = tokens.shape[0]
    size = min(256, count)
    wide = [(D, BF), (D, BF), (2 * FF, BF), (FF, BF), (D, BF), (D, BF), (D, F32)]
    return pl.pallas_call(
        middle_kernel,
        grid=(count // size,),
        in_specs=[
            rows((size, D)),
            rows((size, D)),
            rows((size, D)),
            whole((16, D)),
            whole(weights.shape),
        ],
        out_specs=[rows((size, width)) for width, _ in wide],
        out_shape=[jax.ShapeDtypeStruct((count, width), kind) for width, kind in wide],
        compiler_params=params(48),
        cost_estimate=pl.CostEstimate(
            flops=4 * count * D * (D + 3 * FF), bytes_accessed=count * D * 30, transcendentals=0
        ),
        name="middle",
    )(tokens, mixed, cotangent, gains, weights)


def pair_back(query, keys, values, out_grad, logs, bias):
    scores = dot(keys, query, 1, 1) + bias
    weights = jnp.exp(scores - logs)
    weight_grad = dot(values, out_grad, 1, 1)
    score_grad = weights * (weight_grad - jnp.sum(weights * weight_grad, axis=0, keepdims=True))
    score_grad = score_grad.astype(BF)
    key_grad = dot(score_grad, query)
    value_grad = dot(weights.astype(BF), out_grad)
    query_grad = unstacked(dot(score_grad, keys, 0, 0)) * 0.125
    return query_grad, key_grad, value_grad


def turned_back(values, cosine, sine):
    return values * cosine - swap_halves(values) * sine


def edge_back_kernel(
    marks_ref,
    query_ref,
    mixed_grad_ref,
    log_ref,
    cos_ref,
    sin_ref,
    qkv_ref,
    lower_ref,
    upper_ref,
    grad_ref,
    sum_ref,
    away_ref,
    span_ref,
    sems,
):
    side = pl.program_id(0)
    count = qkv_ref.shape[1]

    def fetch(own_first, own_place, halo_ref, halo_place):
        copies = []
        for half in range(2):
            copies += [
                pltpu.make_async_copy(
                    qkv_ref.at[half, pl.ds(own_first, SPAN - HALF), pl.ds(GROUP, 2 * GROUP)],
                    span_ref.at[half, pl.ds(own_place, SPAN - HALF)],
                    sems.at[2 * half],
                ),
                pltpu.make_async_copy(
                    halo_ref.at[half], span_ref.at[half, pl.ds(halo_place, HALF)], sems.at[2 * half + 1]
                ),
            ]
        for copy in copies:
            copy.start()
        for copy in copies:
            copy.wait()

    @pl.when(side == 0)
    def _():
        fetch(0, HALF, lower_ref, 0)

    @pl.when(side == 1)
    def _():
        fetch(count - SPAN + HALF, 0, upper_ref, SPAN - HALF)

    bias = window_bias(marks_ref, side * (count // BLOCK - 1))
    cosine = cos_ref[...]
    sine = sin_ref[...]
    for pair in range(PAIRS):
        half = pair // GROUP_PAIRS
        sub = pair % GROUP_PAIRS
        lanes = slice(sub * LANES, (sub + 1) * LANES)
        value_lanes = slice(GROUP + sub * LANES, GROUP + (sub + 1) * LANES)
        query_grad, key_grad, value_grad = pair_back(
            stacked(query_ref[half, :, lanes] * BF(0.125)),
            span_ref[half, :, lanes],
            span_ref[half, :, value_lanes],
            stacked(mixed_grad_ref[:, pair * LANES : (pair + 1) * LANES]),
            log_ref[0, half, sub : sub + 1, :],
            bias,
        )
        grad_ref[half, 0, :, lanes] = turned_back(query_grad, cosine, sine).astype(BF)
        sum_ref[half, 0, :, lanes] = key_grad
        sum_ref[half, 0, :, value_lanes] = value_grad

    @pl.when(side == 0)
    def _():
        for half in range(2):
            away_ref[0, half] = sum_ref[half, 0, 0:HALF, :].astype(BF)

    @pl.when(side == 1)
    def _():
        for half in range(2):
            away_ref[0, half] = sum_ref[half, 0, SPAN - HALF :, :].astype(BF)


def edge_back(marks, qkv, mixed_grad, logs, cosine, sine, lower, upper):
    count = qkv.shape[1]
    last = count // BLOCK - 1
    return pl.pallas_call(
        edge_back_kernel,
        grid=(2,),
        in_specs=[
            SMEM,
            pl.BlockSpec((2, BLOCK, GROUP), lambda i: (0, i * last, 0)),
            pl.BlockSpec((BLOCK, D), lambda i: (i * last, 0)),
            pl.BlockSpec((1, 2, 8, 2 * BLOCK), lambda i: (i * last, 0, 0, 0)),
            pl.BlockSpec((BLOCK, LANES), lambda i: (i * last, 0)),
            pl.BlockSpec((BLOCK, LANES), lambda i: (i * last, 0)),
            ANY,
            ANY,
            ANY,
        ],
        out_specs=[
            pl.BlockSpec((2, 1, BLOCK, GROUP), lambda i: (0, i, 0, 0)),
            pl.BlockSpec((2, 1, SPAN, 2 * GROUP), lambda i: (0, i, 0, 0)),
            pl.BlockSpec((1, 2, HALF, 2 * GROUP), lambda i: (i, 0, 0, 0)),
        ],
        out_shape=[
            jax.ShapeDtypeStruct((2, 2, BLOCK, GROUP), BF),
            jax.ShapeDtypeStruct((2, 2, SPAN, 2 * GROUP), F32),
            jax.ShapeDtypeStruct((2, 2, HALF, 2 * GROUP), BF),
        ],
        scratch_shapes=[
            pltpu.VMEM((2, SPAN, 2 * GROUP), BF),
            pltpu.SemaphoreType.DMA((4,)),
        ],
        compiler_params=params(32),
        cost_estimate=pl.CostEstimate(
            flops=10 * 2 * BLOCK * SPAN * D * 2, bytes_accessed=BLOCK * D * 20, transcendentals=0
        ),
        name="edge_back",
    )(marks, qkv, mixed_grad, logs, cosine, sine, qkv, lower, upper)


def inner_back_kernel(
    group_ref,
    marks_ref,
    query_ref,
    mixed_grad_ref,
    log_ref,
    cos_ref,
    sin_ref,
    edge_grad_ref,
    edge_sum_ref,
    from_lower_ref,
    from_upper_ref,
    qkv_ref,
    *rest,
):
    grad_ref, span_ref, sum_ref, sems = rest[-4:]
    step = pl.program_id(0)
    block = step + 1
    count = qkv_ref.shape[1]

    @pl.when(step == 0)
    def _():
        copy = pltpu.make_async_copy(
            qkv_ref.at[group_ref[0], :, pl.ds(GROUP, 2 * GROUP)], span_ref, sems.at[0]
        )
        copy.start()
        sum_ref[0 : SPAN - HALF, :] = edge_sum_ref[0, 0, HALF:, :]
        sum_ref[0:HALF, :] += from_lower_ref[0].astype(F32)
        grad_ref[0:BLOCK, 0:GROUP] = edge_grad_ref[0, 0]
        grad_ref[count - BLOCK :, 0:GROUP] = edge_grad_ref[0, 1]
        copy.wait()

    bias = window_bias(marks_ref, block)
    start = pl.multiple_of(block * BLOCK - HALF, HALF)
    window = pl.ds(start, SPAN)
    older = pl.ds(start, BLOCK)
    newer = pl.ds(pl.multiple_of(start + BLOCK, HALF), BLOCK)
    mine = pl.ds(pl.multiple_of(block * BLOCK, BLOCK), BLOCK)
    cosine = cos_ref[mine, :]
    sine = sin_ref[mine, :]

    def finish(place):
        own_cosine = cos_ref[place, :]
        own_sine = sin_ref[place, :]
        for sub in range(GROUP_PAIRS):
            lanes = slice(sub * LANES, (sub + 1) * LANES)
            key_lanes = slice(GROUP + sub * LANES, GROUP + (sub + 1) * LANES)
            grad_ref[place, key_lanes] = turned_back(
                sum_ref[place, lanes], own_cosine, own_sine
            ).astype(BF)
        grad_ref[place, 2 * GROUP :] = sum_ref[place, GROUP:].astype(BF)

    for sub in range(GROUP_PAIRS):
        lanes = slice(sub * LANES, (sub + 1) * LANES)
        value_lanes = slice(GROUP + sub * LANES, GROUP + (sub + 1) * LANES)
        query_grad, key_grad, value_grad = pair_back(
            stacked(query_ref[0, :, lanes] * BF(0.125)),
            span_ref[window, lanes],
            span_ref[window, value_lanes],
            stacked(mixed_grad_ref[:, lanes]),
            log_ref[0, 0, sub : sub + 1, :],
            bias,
        )
        sum_ref[older, lanes] += key_grad[:BLOCK]
        sum_ref[newer, lanes] = key_grad[BLOCK:]
        sum_ref[older, value_lanes] += value_grad[:BLOCK]
        sum_ref[newer, value_lanes] = value_grad[BLOCK:]
        grad_ref[mine, lanes] = turned_back(query_grad, cosine, sine).astype(BF)

    finish(older)

    @pl.when(step == 0)
    def _():
        finish(pl.ds(0, HALF))

    @pl.when(step == pl.num_programs(0) - 1)
    def _():
        tail = SPAN - HALF
        sum_ref[count - tail : count - HALF, :] += edge_sum_ref[0, 1, 0:BLOCK, :]
        sum_ref[count - HALF :, :] = edge_sum_ref[0, 1, BLOCK:tail, :] + from_upper_ref[0].astype(F32)
        finish(pl.ds(count - tail, tail))


def inner_back(group, marks, qkv, mixed_grad, logs, cosine, sine, edge_grad, edge_sum, from_lower, from_upper, after):
    count = qkv.shape[1]
    steps = count // BLOCK - 2
    return pl.pallas_call(
        inner_back_kernel,
        grid_spec=pltpu.PrefetchScalarGridSpec(
            num_scalar_prefetch=1,
            grid=(steps,),
            in_specs=[
                SMEM,
                pl.BlockSpec((1, BLOCK, GROUP), lambda i, g: (g[0], i + 1, 0)),
                pl.BlockSpec((BLOCK, GROUP), lambda i, g: (i + 1, g[0])),
                pl.BlockSpec((1, 1, 8, 2 * BLOCK), lambda i, g: (i + 1, g[0], 0, 0)),
                pl.BlockSpec((count, LANES), lambda i, g: (0, 0)),
                pl.BlockSpec((count, LANES), lambda i, g: (0, 0)),
                pl.BlockSpec((1, 2, BLOCK, GROUP), lambda i, g: (g[0], 0, 0, 0)),
                pl.BlockSpec((1, 2, SPAN, 2 * GROUP), lambda i, g: (g[0], 0, 0, 0)),
                pl.BlockSpec((1, HALF, 2 * GROUP), lambda i, g: (g[0], 0, 0)),
                pl.BlockSpec((1, HALF, 2 * GROUP), lambda i, g: (g[0], 0, 0)),
                ANY,
                *[ANY for _ in after],
            ],
            out_specs=pl.BlockSpec((count, QKV_HALF), lambda i, g: (0, 0)),
            scratch_shapes=[
                pltpu.VMEM((count, 2 * GROUP), BF),
                pltpu.VMEM((count, 2 * GROUP), F32),
                pltpu.SemaphoreType.DMA((1,)),
            ],
        ),
        out_shape=jax.ShapeDtypeStruct((count, QKV_HALF), BF),
        compiler_params=params(32),
        cost_estimate=pl.CostEstimate(
            flops=10 * count * SPAN * D, bytes_accessed=count * D * 10, transcendentals=0
        ),
        name="inner_back",
    )(
        jnp.reshape(group, (1,)).astype(jnp.int32),
        marks,
        qkv,
        mixed_grad,
        logs,
        cosine,
        sine,
        edge_grad,
        edge_sum,
        from_lower,
        from_upper,
        qkv,
        *after,
    )


def input_grad_kernel(count, order_ref, x_ref, gains_ref, first_ref, second_ref, grad_ref, *refs):
    weight_refs = refs[:count]
    out_ref, w_ref, sems = refs[count:]

    @pl.when(pl.program_id(0) == 0)
    def _():
        load_weights(weight_refs, w_ref, sems)

    unit, scale = normalized(x_ref[...].astype(F32))
    half = order_ref[0]
    grad_normed = dot(first_ref[...], w_ref[half, :, :QKV_HALF], 1, 1) + dot(
        second_ref[...], w_ref[1 - half, :, :QKV_HALF], 1, 1
    )
    out_ref[...] = grad_ref[...] + norm_back(grad_normed, unit, scale, gains_ref[0:1, :])


def input_grad(half, tokens, gains, weights, first, second, grad):
    count = tokens.shape[0]
    size = min(256, count)
    operands = weights.operands()
    return pl.pallas_call(
        partial(input_grad_kernel, len(operands)),
        grid=(count // size,),
        in_specs=[
            SMEM,
            rows((size, D)),
            whole((16, D)),
            rows((size, QKV_HALF)),
            rows((size, QKV_HALF)),
            rows((size, D)),
            *weights.specs(),
        ],
        out_specs=rows((size, D)),
        out_shape=jax.ShapeDtypeStruct((count, D), F32),
        scratch_shapes=weights.scratch(),
        compiler_params=params(32),
        cost_estimate=pl.CostEstimate(
            flops=2 * count * D * 3 * D, bytes_accessed=count * D * 16, transcendentals=0
        ),
        name="input_grad",
    )(jnp.reshape(half, (1,)).astype(jnp.int32), tokens, gains, first, second, grad, *operands)


TILE = 384


def store_slots(slots_ref, out_ref, product):
    step = CHIP_ROWS
    for index in range(D // step):
        place = pl.multiple_of(slots_ref[1 + index] * step, 16)
        out_ref[pl.ds(place, step), :] = product[index * step : (index + 1) * step].astype(BF)


def qkv_weight_kernel(slots_ref, normed_ref, grad_ref, *rest):
    out_ref, turned_ref = rest[-2:]

    @pl.when(pl.program_id(0) == 0)
    def _():
        turned_ref[...] = normed_ref[...].T

    store_slots(slots_ref, out_ref, dot(turned_ref[...], grad_ref[...]))


def qkv_weight_grad(slots, normed, dqkv, after=()):
    count = normed.shape[0]
    tiles = QKV_HALF // TILE
    return pl.pallas_call(
        qkv_weight_kernel,
        grid_spec=pltpu.PrefetchScalarGridSpec(
            num_scalar_prefetch=1,
            grid=(tiles,),
            in_specs=[
                pl.BlockSpec((count, D), lambda t, s: (0, 0)),
                pl.BlockSpec((count, TILE), lambda t, s: (0, t)),
                *[ANY for _ in after],
            ],
            out_specs=pl.BlockSpec((D, TILE), lambda t, s: (0, t)),
            scratch_shapes=[pltpu.VMEM((D, count), BF)],
        ),
        out_shape=jax.ShapeDtypeStruct((D, QKV_HALF), BF),
        compiler_params=params(32),
        cost_estimate=pl.CostEstimate(
            flops=2 * count * D * QKV_HALF, bytes_accessed=count * D * 8, transcendentals=0
        ),
        name="qkv_weight_grad",
    )(slots, normed, dqkv, *after)


def ff_weight_kernel(slots_ref, normed_ref, cot_ref, mixed_ref, both_ref, hidden_ref, low_ref, *rest):
    out_ref, turned_ref = rest[-2:]
    step = pl.program_id(0)
    second = slots_ref[0] == 1

    @pl.when((step == 0) & ~second)
    def _():
        turned_ref[...] = normed_ref[...].T

    @pl.when((step == 0) & second)
    def _():
        turned_ref[...] = cot_ref[...].T

    @pl.when((step == 3) & second)
    def _():
        turned_ref[...] = mixed_ref[...].T

    @pl.when(~second)
    def _():
        store_slots(slots_ref, out_ref, dot(turned_ref[...], both_ref[...]))

    @pl.when(second & (step < 3))
    def _():
        store_slots(slots_ref, out_ref, dot(turned_ref[...], hidden_ref[...]))

    @pl.when(second & (step >= 3) & (step < 5))
    def _():
        store_slots(slots_ref, out_ref, dot(turned_ref[...], low_ref[...]))

    @pl.when(second & (step == 5))
    def _():
        out_ref[...] = jnp.zeros_like(out_ref)


def ff_weight_grad(slots, normed, cot, mixed, both, hidden, low, after):
    count = normed.shape[0]
    full = pl.BlockSpec((count, D), lambda t, s: (0, 0))
    return pl.pallas_call(
        ff_weight_kernel,
        grid_spec=pltpu.PrefetchScalarGridSpec(
            num_scalar_prefetch=1,
            grid=(FF_HALF // TILE,),
            in_specs=[
                full,
                full,
                full,
                pl.BlockSpec((count, TILE), lambda t, s: (0, jnp.where(s[0] == 0, t, 0))),
                pl.BlockSpec((count, TILE), lambda t, s: (0, jnp.where(s[0] == 0, 0, jnp.minimum(t, 2)))),
                pl.BlockSpec(
                    (count, TILE), lambda t, s: (0, jnp.where(s[0] == 0, 0, jnp.clip(t - 3, 0, 1)))
                ),
                *[ANY for _ in after],
            ],
            out_specs=pl.BlockSpec((D, TILE), lambda t, s: (0, t)),
            scratch_shapes=[pltpu.VMEM((D, count), BF)],
        ),
        out_shape=jax.ShapeDtypeStruct((D, FF_HALF), BF),
        compiler_params=params(40),
        cost_estimate=pl.CostEstimate(
            flops=2 * count * D * FF_HALF, bytes_accessed=count * D * 12, transcendentals=0
        ),
        name="ff_weight_grad",
    )(slots, normed, cot, mixed, both, hidden, low, *after)


def doc_marks(doc_lengths, row_count):
    me = lax.axis_index("tok")
    ends = jnp.cumsum(doc_lengths).astype(jnp.int32)
    before = jnp.where(me > 0, ends[jnp.maximum(me - 1, 0)], 0)
    return jnp.stack([before, ends[me], ends[me + 1], me * row_count]).astype(jnp.int32)


def rotary_tables(marks, row_count):
    place = marks[3] + jnp.arange(row_count, dtype=jnp.int32)
    offset = place - jnp.where(place >= marks[1], marks[1], marks[0])
    frequency = 10000.0 ** (-jnp.arange(0, HEAD_DIM, 2, dtype=F32) / HEAD_DIM)
    angles = offset.astype(F32)[:, None] * frequency[None, :]
    cosine = jnp.cos(angles)
    sine = jnp.sin(angles)
    return (
        jnp.concatenate([cosine] * 4, axis=1),
        jnp.concatenate([-sine, sine, -sine, sine], axis=1),
    )


def passed_along(value, steps):
    count = lax.axis_size("tok")
    first, last = (max(0, -steps), min(count, count - steps))
    return lax.ppermute(value, "tok", [(at, at + steps) for at in range(first, last)])


STAGED_DEVICES = 32


def staged():
    return lax.axis_size("tok") == STAGED_DEVICES


def exchange(value, by_core):
    pairs = [(at, at ^ by_core[at & 1]) for at in range(lax.axis_size("tok"))]
    return lax.ppermute(value, "tok", pairs)


CORE = (1, 1)
DEEP = tuple((step << 3, step << 3) for step in range(4))
NEAR = (2, 4)
FAR = (4, 2)


def slot_codes(core):
    slot = jnp.arange(16, dtype=jnp.int32)
    depth, near, far = (slot & 3, (slot >> 2) & 1, slot >> 3)
    return (depth << 2) | jnp.where(core == 0, (far << 1) | near, (near << 1) | far)


def chip_slots(chip, core):
    code = jnp.arange(16, dtype=jnp.int32) ^ chip
    depth, second, first = (code >> 2, (code >> 1) & 1, code & 1)
    return depth | jnp.where(core == 0, (second << 3) | (first << 2), (first << 3) | (second << 2))


def stage_after(value, *others):
    return lax.optimization_barrier((value, *others))[0]


def core_pieces(shard):
    core = lax.axis_index("tok") & 1
    half = shard.shape[1] // 2
    keep = jnp.where(core == 0, shard[:, :half], shard[:, half:])
    send = jnp.where(core == 0, shard[:, half:], shard[:, :half])
    came = exchange(send, CORE)
    return jnp.concatenate(
        [jnp.where(core == 0, keep, came), jnp.where(core == 0, came, keep)], axis=0
    )


def deep_gather(piece):
    return jnp.concatenate([piece] + [exchange(piece, DEEP[step]) for step in (1, 2, 3)], axis=0)


def final_gather(held, far):
    me = lax.axis_index("tok")
    core = me & 1
    chip = me >> 1
    places = jnp.concatenate(
        [slot_codes(core) ^ chip, slot_codes(1 - core) ^ chip, jnp.full((1,), core, jnp.int32)]
    )
    return Weights([held, far, exchange(held, CORE), exchange(far, CORE)], places)


def whole_weights(shard):
    full = lax.all_gather(shard, "tok", axis=0, tiled=True)
    half = full.shape[1] // 2
    return Weights([jnp.stack([full[:, :half], full[:, half:]])])


def added(left, right):
    return (left.astype(F32) + right.astype(F32)).astype(BF)


def core_sum(keep, came):
    return added(keep[:384], came[:384]), added(keep[384:], came[384:])


def far_sum(near, came):
    return added(near[:192], came[:192]), added(near[192:], came[192:])


def near_sum(near, came):
    return [
        added(near[first : first + CHIP_ROWS], came[first : first + CHIP_ROWS])
        for first in range(0, 192, CHIP_ROWS)
    ]


def deep_sum(parts, after):
    core = lax.axis_index("tok") & 1
    total = parts[0].astype(F32)
    for step in (1, 2, 3):
        total = total + stage_after(exchange(parts[step], DEEP[step]), after).astype(F32)
    share = CHIP_ROWS // 2
    lower, upper = (total[:share], total[share:])
    own = jnp.where(core == 0, lower, upper)
    came = exchange(jnp.where(core == 0, upper, lower), CORE)
    return jnp.concatenate(
        [jnp.where(core == 0, own, came), jnp.where(core == 0, came, own)], axis=1
    )


def summed(keep, send):
    full = jnp.concatenate([keep, send], axis=1)
    return lax.psum_scatter(full.astype(F32), "tok", scatter_dimension=0, tiled=True)


def by_part(groups):
    return jnp.concatenate(
        [
            groups[:, half * QKV_HALF + part * GROUP : half * QKV_HALF + (part + 1) * GROUP]
            for part in range(3)
            for half in range(2)
        ],
        axis=1,
    )


def on_device(
    tokens,
    doc_lengths,
    first_gain,
    qkv_weight,
    attn_weight,
    second_gain,
    feed_in_weight,
    feed_out_weight,
    cotangent,
):
    row_count = tokens.shape[0]
    share = first_gain.shape[0]

    def spread(gain):
        return jnp.broadcast_to(gain[:, None], (share, LANES))

    def group_of(half):
        return [
            qkv_weight[:, part * D + half * GROUP : part * D + (half + 1) * GROUP]
            for part in range(3)
        ]

    shard_one = jnp.concatenate(
        [*group_of(0), spread(first_gain), *group_of(1), spread(second_gain)], axis=1
    )
    shard_two = jnp.concatenate([feed_in_weight, feed_out_weight.T, attn_weight], axis=1)
    weights_two = lax.all_gather(shard_two, "tok", axis=0, tiled=True)
    marks = doc_marks(doc_lengths, row_count)
    cosine, sine = rotary_tables(marks, row_count)
    if staged():
        one = deep_gather(core_pieces(shard_one))
        one = jnp.concatenate([one, exchange(one, NEAR)], axis=0)
        weights_one = final_gather(one, exchange(one, FAR))
    else:
        weights_one = whole_weights(shard_one)
    normed, qkv, gains = project_qkv(tokens, weights_one, cosine, sine)
    lower = passed_along(qkv[:, row_count - HALF :, GROUP:], 1)
    upper = passed_along(qkv[:, :HALF, GROUP:], -1)
    mixed, logs = attend(marks, qkv, lower, upper)
    result, normed_two, both, hidden, low, mixed_grad, grad = middle(
        tokens, mixed, cotangent, gains, weights_two
    )
    edge_grad, edge_sum, away = edge_back(marks, qkv, mixed_grad, logs, cosine, sine, lower, upper)
    from_upper = passed_along(away[0], -1)
    from_lower = passed_along(away[1], 1)
    me = lax.axis_index("tok")
    if staged():
        halves = (1 - (me & 1), me & 1)
    else:
        halves = (jnp.int32(1), jnp.int32(0))

    def order(half):
        if staged():
            slots = chip_slots(me >> 1, half)
        else:
            slots = jnp.arange(D // CHIP_ROWS, dtype=jnp.int32)
        return jnp.concatenate([jnp.reshape(half, (1,)).astype(jnp.int32), slots])

    def ff_grad(half, after):
        return ff_weight_grad(order(half), normed_two, cotangent, mixed, both, hidden, low, after)

    def inner(half, after):
        return inner_back(
            half,
            marks,
            qkv,
            mixed_grad,
            logs,
            cosine,
            sine,
            edge_grad,
            edge_sum,
            from_lower,
            from_upper,
            after,
        )

    def finish(first, second):
        return input_grad(halves[0], tokens, gains, weights_one, first, second, grad)

    send, keep = halves
    ff_send = ff_grad(send, [away])
    ff_keep = ff_grad(keep, [ff_send, from_lower, from_upper])
    if staged():
        near, far = core_sum(ff_keep, exchange(ff_send, CORE))
        first = inner(send, [far])
        near, far = far_sum(near, stage_after(exchange(far, FAR), first))
        qkv_send = qkv_weight_grad(order(send), normed, first, [far])
        second = inner(keep, [qkv_send])
        parts = near_sum(near, stage_after(exchange(far, NEAR), second))
        qkv_keep = qkv_weight_grad(order(keep), normed, second, parts)
        near, far = core_sum(qkv_keep, exchange(qkv_send, CORE))
        grad_in = finish(first, stage_after(second, far))
        sum_ff = deep_sum(parts, far)
        near, far = far_sum(near, stage_after(exchange(far, FAR), grad_in))
        sum_qkv = deep_sum(near_sum(near, exchange(far, NEAR)), far)
    else:
        first, second = inner(send, []), inner(keep, [])
        grad_in = finish(first, second)
        sum_ff = summed(ff_keep, ff_send)
        sum_qkv = summed(
            qkv_weight_grad(order(keep), normed, second), qkv_weight_grad(order(send), normed, first)
        )
    sum_qkv = by_part(sum_qkv)
    sent_in = sum_ff[:, : 2 * FF]
    sent_down = sum_ff[:, 2 * FF : 3 * FF].T
    sent_attn = sum_ff[:, 3 * FF : 3 * FF + D]

    def gain_grad(summed, weight, gain):
        return jnp.sum(summed * weight.astype(F32), axis=1) / gain.astype(F32)

    return (
        result,
        grad_in,
        gain_grad(sum_qkv, qkv_weight, first_gain),
        sum_qkv,
        sent_attn,
        gain_grad(sent_in, feed_in_weight, second_gain),
        sent_in,
        sent_down,
    )


def solution(mesh):
    in_specs = (
        P("tok", None),
        P(),
        P("tok"),
        P("tok", None),
        P("tok", None),
        P("tok"),
        P("tok", None),
        P(None, "tok"),
        P("tok", None),
    )
    out_specs = (
        P("tok", None),
        P("tok", None),
        P("tok"),
        P("tok", None),
        P("tok", None),
        P("tok"),
        P("tok", None),
        P(None, "tok"),
    )
    return jax.shard_map(
        on_device, mesh=mesh, in_specs=in_specs, out_specs=out_specs, check_vma=False
    )
```

time: 542 us -> 273 us (0.50)
  waiting for transfers between devices: 345 us -> 74.8 us
  starting transfers between devices: 8.37 us -> 48 us
  local copies, waits for them, and re-layouts: 43.3 us -> 14.4 us
  other arithmetic: 27.8 us -> 13.7 us
    reduce_scatter x2 -> x0, waiting for transfers between devices: 240 us -> none  [scattered(): lax.psum_scatter(full.astype(F32), 'tok', scatter_dimension=0, tiled=True)]
    all_gather x2 -> x1, waiting for transfers between devices: 102 us -> 0.01 us  [on_device(): weights_two = lax.all_gather(shard_two, 'tok', axis=0, tiled=True)]
    ppermute x0 -> x22, waiting for transfers between devices: none -> 73.3 us  [exchange(): return lax.ppermute(value, 'tok', pairs)]
    ppermute x0 -> x22, starting transfers between devices: none -> 38.9 us  [exchange(): return lax.ppermute(value, 'tok', pairs)]
    unnamed x50 -> x71, local copies, waits for them, and re-layouts: 30 us -> 10.1 us
    convert_element_type x4 -> x6, other arithmetic: 12.9 us -> 4.5 us  [added(): return (left.astype(F32) + right.astype(F32)).astype(BF)]
    another operation x2 -> x0, local copies, waits for them, and re-layouts: 5.93 us -> none  [gathered(): return jnp.stack([full[:, :half], full[:, half:]])]
    pallas_call x5 -> x6, Pallas kernels: 50.6 us -> 55.7 us  [the longest x2 20 us: inner_back(): pl.pallas_call(inner_back_kernel, grid_spec=pltpu.PrefetchScalarGridSpec(...]
  transfers between devices with their start and end apart: 8 -> 27, of which waited for: 5 -> 13; matrix products, arithmetic and copies ran while one was open for 4% -> 4% of each run, Pallas kernels for 8% -> 25%
where the time goes in v3:
time: 273 us
  Pallas kernels  107 us (39%)
  waiting for transfers between devices  74.8 us (27%)
  starting transfers between devices  48 us (18%)
  between operations  15.3 us (6%)
  local copies, waits for them, and re-layouts  14.4 us (5%)
  other arithmetic  13.7 us (5%)
    ppermute x22, waiting for transfers between devices, exchange(): return lax.ppermute(value, 'tok', pairs)  73.3 us
    ppermute x22, starting transfers between devices, exchange(): return lax.ppermute(value, 'tok', pairs)  38.9 us
    pallas_call x1, Pallas kernels, middle(): pl.pallas_call(middle_kernel, grid=(count // size,), in_specs=[rows((size...  24.4 us
    pallas_call x2, Pallas kernels, inner_back(): pl.pallas_call(inner_back_kernel, grid_spec=pltpu.PrefetchScalarGridSpec(...  20 us
    pallas_call x2, Pallas kernels, ff_weight_grad(): pl.pallas_call(ff_weight_kernel, grid_spec=pltpu.PrefetchScalarGridSpec(n...  17.8 us
    pallas_call x1, Pallas kernels, attend(): pl.pallas_call(attend_kernel, grid=(blocks,), in_specs=[SMEM, pl.BlockSpe...  11.4 us
    unnamed x71, local copies, waits for them, and re-layouts  10.1 us
    pallas_call x1, Pallas kernels, input_grad(): pl.pallas_call(partial(input_grad_kernel, len(operands)), grid=(count //...  9.11 us
  transfers between devices with their start and end apart: 27, of which 13 were waited for; matrix products, arithmetic and copies ran while one was open for 4% of the time, Pallas kernels for 25%

profile of v3, /device:TPU:0, one launch (start us, length us, event | category | flops | bytes accessed | tf_op | source)
XLA Modules:
  0.0 272.9 jit_solution(13536027355054048928)
XLA Ops:
  12.7 5.0 %collective-permute-start.3 = (bf16[48,1280]{1,0:T(8,128)(2,1)S(1)}, bf16[48,1280]{1,0:T(8,128)(2,1)S(1)}, u32[]{:S(2)}, u32[]{:S(2)}) collective-permute-start(bf16[48,1280]{1,0:T(8,128)(2,1)S(1)} %pad_maximum_fusion.3), channel_id=1, source_target_pairs={{0,24},{1,25},{2,26},{3,27},{4,28},{5,29},{6,30},{7,31},{8,16},{9,... | collective-permute-start | bytes 368648 | tf_op jit(solution)/shard_map/ppermute | solution.py:801
  18.4 9.1 %collective-permute-done.1 = bf16[48,1280]{1,0:T(8,128)(2,1)S(1)} collective-permute-done((bf16[48,1280]{1,0:T(8,128)(2,1)S(1)}, bf16[48,1280]{1,0:T(8,128)(2,1)S(1)}, u32[]{:S(2)}, u32[]{:S(2)}) %collective-permute-start.1) | collective-permute-done | bytes 122912 | tf_op jit(solution)/shard_map/ppermute | solution.py:801
  27.5 2.6 collective-permute-done.2
  31.7 7.3 %collective-permute-done.4 = bf16[192,1280]{1,0:T(8,128)(2,1)S(1)} collective-permute-done((bf16[192,1280]{1,0:T(8,128)(2,1)S(1)}, bf16[192,1280]{1,0:T(8,128)(2,1)S(1)}, u32[]{:S(2)}, u32[]{:S(2)}) %collective-permute-start.4) | collective-permute-done | bytes 491552 | tf_op jit(solution)/shard_map/ppermute | solution.py:801
  40.7 15.2 %collective-permute-done.5.refs_2_ = bf16[384,1280]{1,0:T(8,128)(2,1)S(1)} collective-permute-done((bf16[384,1280]{1,0:T(8,128)(2,1)S(1)}, bf16[384,1280]{1,0:T(8,128)(2,1)S(1)}, u32[]{:S(2)}, u32[]{:S(2)}) %collective-permute-start.5) | collective-permute-done | bytes 983072 | tf_op jit(solution)/shard_map/ppermute | solution.py:801
  58.7 1.9 fusion
  61.5 8.9 %qkv.1 = (bf16[1024,768]{1,0:T(8,128)(2,1)S(1)}, bf16[2,1024,1152]{2,1,0:T(8,128)(2,1)S(1)}, f32[16,768]{1,0:T(8,128)S(1)}) custom-call(bf16[1024,768]{1,0:T(8,128)(2,1)S(1)} %copy-done.15, f32[1024,128]{1,0:T(8,128)S(1)} %get-tuple-element.104.cos_ref, f32[1024,128]{1,0:T(8,128)S(1)} %get-tuple-element.105.sin_ref, s32[33]{0:T(128)S(1)} %pad_add_fusion.1.refs_0_, ...), custom_call_target="tpu_custom_call" | custom-call | flops 3623878656 | bytes 11403264 | tf_op jit(solution)/shard_map/qkv/pallas_call | solution.py:147
  73.0 3.2 %collective-permute-start.8 = (bf16[2,64,768]{2,1,0:T(8,128)(2,1)S(1)}, bf16[2,64,768]{2,1,0:T(8,128)(2,1)S(1)}, u32[]{:S(2)}, u32[]{:S(2)}) collective-permute-start(bf16[2,64,768]{2,1,0:T(8,128)(2,1)S(1)} %get-tuple-element.67), channel_id=1, source_target_pairs={{0,1},{1,2},{2,3},{3,4},{4,5},{5,6},{6,7},{7,8},{8,9},{9,10},{10,1... | collective-permute-start | bytes 589832 | tf_op jit(solution)/shard_map/ppermute | solution.py:789
  77.7 11.4 %attend.1 = (bf16[1024,768]{1,0:T(8,128)(2,1)S(1)}, f32[8,2,8,256]{3,2,1,0:T(8,128)S(1)}) custom-call(s32[4]{0:T(128)S(1)} %pad_add_fusion.marks_ref, bf16[2,1024,1152]{2,1,0:T(8,128)(2,1)S(1)} %get-tuple-element.33.query_ref.qkv_ref, bf16[2,1024,1152]{2,1,0:T(8,128)(2,1)S(1)} %get-tuple-element.33.query_ref.qkv_ref, ...), custom_call_target="tpu_custom_call" | custom-call | flops 1610612736 | bytes 7864320 | tf_op jit(solution)/shard_map/attend/pallas_call | solution.py:247
  89.1 2.1 copy-done
  92.4 24.4 %middle.1 = (bf16[1024,768]{1,0:T(8,128)(2,1)}, bf16[1024,768]{1,0:T(8,128)(2,1)S(1)}, bf16[1024,2304]{1,0:T(8,128)(2,1)}, bf16[1024,1152]{1,0:T(8,128)(2,1)}, b...) custom-call(bf16[1024,768]{1,0:T(8,128)(2,1)} %x_ref.5, ...), custom_call_target="tpu_custom_call" | custom-call | flops 13287555072 | bytes 23592960 | tf_op jit(solution)/shard_map/middle/pallas_call | solution.py:327
  119.2 6.2 %edge_back.1 = (bf16[2,2,128,384]{3,2,1,0:T(8,128)(2,1)S(1)}, f32[2,2,256,768]{3,2,1,0:T(8,128)S(1)}, bf16[2,2,64,768]{3,2,1,0:T(8,128)(2,1)S(1)}) custom-call(s32[4]{0:T(128)S(1)} %pad_add_fusion.marks_ref, bf16[2,1024,1152]{2,1,0:T(8,128)(2,1)S(1)} %bitcast.17, bf16[1024,768]{1,0:T(8,128)(2,1)S(1)} %get-tuple-element.37.mixed_grad_ref, ...), custom_call_target="tpu_custom_call" | custom-call | flops 1006632960 | bytes 1966080 | tf_op jit(solution)/shard_map/edge_back/pallas_call | solution.py:442
  128.5 8.9 %ff_weight_grad.2.rest_0_ = bf16[768,2304]{1,0:T(8,128)(2,1)S(1)} custom-call(s32[17]{0:T(128)S(1)} %pad_add_fusion.3.slots_ref, bf16[1024,768]{1,0:T(8,128)(2,1)S(1)} %copy-done.11, bf16[1024,768]{1,0:T(8,128)(2,1)S(1)} %copy-done.5, bf16[1024,768]{1,0:T(8,128)(2,1)S(1)} %copy-done.8, bf16[1024,2304]{1,0:T(8,128)(2,1)} %get-tuple-element.43.both_ref, ...), custom_call_target="tpu_custom_call" | custom-call | flops 3623878656 | bytes 9437184 | tf_op jit(solution)/shard_map/ff_weight_grad/pallas_call | solution.py:738
  137.4 3.7 %collective-permute-start.12 = (bf16[768,2304]{1,0:T(8,128)(2,1)S(1)}, bf16[768,2304]{1,0:T(8,128)(2,1)}, u32[]{:S(2)}, u32[]{:S(2)}) collective-permute-start(bf16[768,2304]{1,0:T(8,128)(2,1)S(1)} %ff_weight_grad.2.rest_0_), channel_id=1, source_target_pairs={{0,1},{1,0},{2,3},{3,2},{4,5},{5,4},{6,7},{7,6},{8,9},{9,8},{10,11... | collective-permute-start | bytes 10616840 | tf_op jit(solution)/shard_map/ppermute | solution.py:801
  142.4 3.3 %collective-permute-start.10 = (bf16[2,64,768]{2,1,0:T(8,128)(2,1)S(1)}, bf16[2,64,768]{2,1,0:T(8,128)(2,1)S(1)}, u32[]{:S(2)}, u32[]{:S(2)}) collective-permute-start(bf16[2,64,768]{2,1,0:T(8,128)(2,1)S(1)} %get-tuple-element.83), channel_id=1, source_target_pairs={{0,1},{1,2},{2,3},{3,4},{4,5},{5,6},{6,7},{7,8},{8,9},{9,10},{10,1... | collective-permute-start | bytes 589832 | tf_op jit(solution)/shard_map/ppermute | solution.py:789
  147.2 8.9 %ff_weight_grad.3 = bf16[768,2304]{1,0:T(8,128)(2,1)S(1)} custom-call(s32[17]{0:T(128)S(1)} %pad_add_fusion.2.slots_ref, bf16[1024,768]{1,0:T(8,128)(2,1)S(1)} %copy-done.11, bf16[1024,768]{1,0:T(8,128)(2,1)S(1)} %copy-done.6, bf16[1024,768]{1,0:T(8,128)(2,1)S(1)} %copy-done.9, bf16[1024,2304]{1,0:T(8,128)(2,1)} %get-tuple-element.43.both_ref, ...), custom_call_target="tpu_custom_call" | custom-call | flops 3623878656 | bytes 9437184 | tf_op jit(solution)/shard_map/ff_weight_grad/pallas_call | solution.py:738
  156.1 3.1 %add_convert_fusion = (bf16[384,2304]{1,0:T(8,128)(2,1)S(1)}, bf16[384,2304]{1,0:T(8,128)(2,1)S(1)}) fusion(bf16[768,2304]{1,0:T(8,128)(2,1)} %collective-permute-done.12, bf16[768,2304]{1,0:T(8,128)(2,1)S(1)} %ff_weight_grad.3), kind=kLoop, calls=%fused_computation | loop fusion | flops 7077888 | bytes 10616832 | tf_op jit(solution)/shard_map/convert_element_type | solution.py:858
  159.2 7.5 %collective-permute-start.13 = (bf16[384,2304]{1,0:T(8,128)(2,1)S(1)}, bf16[384,2304]{1,0:T(8,128)(2,1)S(1)}, u32[]{:S(2)}, u32[]{:S(2)}) collective-permute-start(bf16[384,2304]{1,0:T(8,128)(2,1)S(1)} %get-tuple-element.65.rest_0_), channel_id=1, source_target_pairs={{0,4},{1,3},{2,6},{3,1},{4,0},{5,7},{6,2},{7,5},{8,12},{9,11},{10,... | collective-permute-start | bytes 5308424 | tf_op jit(solution)/shard_map/ppermute | solution.py:801
  166.7 10.0 %inner_back.2.grad_ref.first_ref = bf16[1024,1152]{1,0:T(8,128)(2,1)S(1)} custom-call(s32[1]{0:T(128)} %bitcast.9.group_ref.order_ref, s32[4]{0:T(128)S(1)} %pad_add_fusion.marks_ref, bf16[2,1024,1152]{2,1,0:T(8,128)(2,1)S(1)} %bitcast.17, bf16[1024,768]{1,0:T(8,128)(2,1)S(1)} %get-tuple-element.37.mixed_grad_ref, ...), custom_call_target="tpu_custom_call" | custom-call | flops 2013265920 | bytes 7864320 | tf_op jit(solution)/shard_map/inner_back/pallas_call | solution.py:564
  176.7 10.5 %collective-permute-done.13 = bf16[384,2304]{1,0:T(8,128)(2,1)S(1)} collective-permute-done((bf16[384,2304]{1,0:T(8,128)(2,1)S(1)}, bf16[384,2304]{1,0:T(8,128)(2,1)S(1)}, u32[]{:S(2)}, u32[]{:S(2)}) %collective-permute-start.13) | collective-permute-done | bytes 1769504 | tf_op jit(solution)/shard_map/ppermute | solution.py:801
  187.6 3.4 %collective-permute-start.14 = (bf16[192,2304]{1,0:T(8,128)(2,1)S(1)}, bf16[192,2304]{1,0:T(8,128)(2,1)S(1)}, u32[]{:S(2)}, u32[]{:S(2)}) collective-permute-start(bf16[192,2304]{1,0:T(8,128)(2,1)S(1)} %get-tuple-element.71.rest_0_), channel_id=1, source_target_pairs={{0,2},{1,5},{2,0},{3,7},{4,6},{5,1},{6,4},{7,3},{8,10},{9,13},{10,... | collective-permute-start | bytes 2654216 | tf_op jit(solution)/shard_map/ppermute | solution.py:801
  191.0 4.5 %qkv_weight_grad.2.rest_0_ = bf16[768,1152]{1,0:T(8,128)(2,1)S(1)} custom-call(s32[17]{0:T(128)S(1)} %pad_add_fusion.3.slots_ref, bf16[1024,768]{1,0:T(8,128)(2,1)S(1)} %copy-done.22, bf16[1024,1152]{1,0:T(8,128)(2,1)S(1)} %inner_back.2.grad_ref.first_ref, bf16[192,2304]{1,0:T(8,128)(2,1)S(1)} %get-tuple-element.71.rest_0_), custom_call_target="tpu_custom_call" | custom-call | flops 1811939328 | bytes 6291456 | tf_op jit(solution)/shard_map/qkv_weight_grad/pallas_call | solution.py:679
  195.6 10.0 %inner_back.3.grad_ref.second_ref = bf16[1024,1152]{1,0:T(8,128)(2,1)S(1)} custom-call(s32[1]{0:T(128)} %bitcast.7.group_ref, s32[4]{0:T(128)S(1)} %pad_add_fusion.marks_ref, bf16[2,1024,1152]{2,1,0:T(8,128)(2,1)S(1)} %bitcast.17, bf16[1024,768]{1,0:T(8,128)(2,1)S(1)} %get-tuple-element.37.mixed_grad_ref, f32[8,2,8,256]{3,2,1,0:T(8,128)S(1)} %get-tuple-element.38.log_ref, ...), custom_call_target="tpu_custom_call" | custom-call | flops 2013265920 | bytes 7864320 | tf_op jit(solution)/shard_map/inner_back/pallas_call | solution.py:564
  205.8 5.7 %collective-permute-start.24 = (bf16[48,2304]{1,0:T(8,128)(2,1)S(1)}, bf16[48,2304]{1,0:T(8,128)(2,1)S(1)}, u32[]{:S(2)}, u32[]{:S(2)}) collective-permute-start(bf16[48,2304]{1,0:T(8,128)(2,1)S(1)} %get-tuple-element.74.rest_3_), channel_id=1, source_target_pairs={{0,24},{1,25},{2,26},{3,27},{4,28},{5,29},{6,30},{7,31},{8,16},{9,... | collective-permute-start | bytes 663560 | tf_op jit(solution)/shard_map/ppermute | solution.py:801
  211.5 2.9 %collective-permute-start.23 = (bf16[48,2304]{1,0:T(8,128)(2,1)S(1)}, bf16[48,2304]{1,0:T(8,128)(2,1)S(1)}, u32[]{:S(2)}, u32[]{:S(2)}) collective-permute-start(bf16[48,2304]{1,0:T(8,128)(2,1)S(1)} %get-tuple-element.75.rest_2_), channel_id=1, source_target_pairs={{0,16},{1,17},{2,18},{3,19},{4,20},{5,21},{6,22},{7,23},{8,24},{9,... | collective-permute-start | bytes 663560 | tf_op jit(solution)/shard_map/ppermute | solution.py:801
  214.4 4.5 %qkv_weight_grad.3 = bf16[768,1152]{1,0:T(8,128)(2,1)S(1)} custom-call(s32[17]{0:T(128)S(1)} %pad_add_fusion.2.slots_ref, bf16[1024,768]{1,0:T(8,128)(2,1)S(1)} %copy-done.22, bf16[1024,1152]{1,0:T(8,128)(2,1)S(1)} %inner_back.3.grad_ref.second_ref, bf16[48,2304]{1,0:T(8,128)(2,1)S(1)} %get-tuple-element.77.rest_0_, ...), custom_call_target="tpu_custom_call" | custom-call | flops 1811939328 | bytes 6291456 | tf_op jit(solution)/shard_map/qkv_weight_grad/pallas_call | solution.py:679
  219.5 12.3 %collective-permute-done.23 = bf16[48,2304]{1,0:T(8,128)(2,1)S(1)} collective-permute-done((bf16[48,2304]{1,0:T(8,128)(2,1)S(1)}, bf16[48,2304]{1,0:T(8,128)(2,1)S(1)}, u32[]{:S(2)}, u32[]{:S(2)}) %collective-permute-start.23) | collective-permute-done | bytes 221216 | tf_op jit(solution)/shard_map/ppermute | solution.py:801
  232.1 9.1 %input_grad.1 = f32[1024,768]{1,0:T(8,128)} custom-call(s32[1]{0:T(128)} %bitcast.9.group_ref.order_ref, bf16[1024,768]{1,0:T(8,128)(2,1)S(1)} %copy-done.16, f32[16,768]{1,0:T(8,128)S(1)} %get-tuple-element.35.gains_ref, bf16[1024,1152]{1,0:T(8,128)(2,1)S(1)} %inner_back.2.grad_ref.first_ref, bf16[1024,1152]{1,0:T(8,128)(2,1)S(1)} %inner_back.3.grad_ref.second_ref, ...), custom_call_target="tpu_custom_call" | custom-call | flops 3623878656 | bytes 12582912 | tf_op jit(solution)/shard_map/input_grad/pallas_call | solution.py:633
  243.5 6.3 %collective-permute-done.17 = bf16[192,1152]{1,0:T(8,128)(2,1)S(1)} collective-permute-done((bf16[192,1152]{1,0:T(8,128)(2,1)S(1)}, bf16[192,1152]{1,0:T(8,128)(2,1)S(1)}, u32[]{:S(2)}, u32[]{:S(2)}) %collective-permute-start.17) | collective-permute-done | bytes 442400 | tf_op jit(solution)/shard_map/ppermute | solution.py:801
  250.7 2.9 %collective-permute-start.20 = (bf16[48,1152]{1,0:T(8,128)(2,1)S(1)}, bf16[48,1152]{1,0:T(8,128)(2,1)S(1)}, u32[]{:S(2)}, u32[]{:S(2)}) collective-permute-start(bf16[48,1152]{1,0:T(8,128)(2,1)S(1)} %get-tuple-element.79), channel_id=1, source_target_pairs={{0,24},{1,25},{2,26},{3,27},{4,28},{5,29},{6,30},{7,31},{8,16},{9,... | collective-permute-start | bytes 331784 | tf_op jit(solution)/shard_map/ppermute | solution.py:801
  254.8 5.2 %collective-permute-done.20 = bf16[48,1152]{1,0:T(8,128)(2,1)S(1)} collective-permute-done((bf16[48,1152]{1,0:T(8,128)(2,1)S(1)}, bf16[48,1152]{1,0:T(8,128)(2,1)S(1)}, u32[]{:S(2)}, u32[]{:S(2)}) %collective-permute-start.20) | collective-permute-done | bytes 110624 | tf_op jit(solution)/shard_map/ppermute | solution.py:801
  259.9 3.8 %collective-permute-done.19 = bf16[48,1152]{1,0:T(8,128)(2,1)S(1)} collective-permute-done((bf16[48,1152]{1,0:T(8,128)(2,1)S(1)}, bf16[48,1152]{1,0:T(8,128)(2,1)S(1)}, u32[]{:S(2)}, u32[]{:S(2)}) %collective-permute-start.19) | collective-permute-done | bytes 110624 | tf_op jit(solution)/shard_map/ppermute | solution.py:801
  (149 shorter events, 33.9 us)
Async XLA Ops:
  7.2 85.2 %all-gather.2.cloned.1.call-start = ((), (), s32[]{:S(2)}) async-start(), calls=%async_computation | async-start | bytes 6690816 | tf_op jit(solution)/shard_map/all_gather | solution.py:933
  9.7 46.8 %copy-start.28 = (s32[33]{0:T(128)S(1)}, s32[33]{0:T(128)}, u32[]{:S(2)}) copy-start(s32[33]{0:T(128)} %param.10) | copy-start | bytes 400
  11.2 1.4 collective-permute-start
  12.7 17.4 %collective-permute-start.3 = (bf16[48,1280]{1,0:T(8,128)(2,1)S(1)}, bf16[48,1280]{1,0:T(8,128)(2,1)S(1)}, u32[]{:S(2)}, u32[]{:S(2)}) collective-permute-start(bf16[48,1280]{1,0:T(8,128)(2,1)S(1)} %pad_maximum_fusion.3), channel_id=1, source_target_pairs={{0,24},{1,25},{2,26},{3,27},{4,28},{5,29},{6,30},{7,31},{8,16},{9,... | collective-permute-start | bytes 368648 | tf_op jit(solution)/shard_map/ppermute | solution.py:801
  17.7 12.4 %collective-permute-start.2 = (bf16[48,1280]{1,0:T(8,128)(2,1)S(1)}, bf16[48,1280]{1,0:T(8,128)(2,1)S(1)}, u32[]{:S(2)}, u32[]{:S(2)}) collective-permute-start(bf16[48,1280]{1,0:T(8,128)(2,1)S(1)} %pad_maximum_fusion.3), channel_id=1, source_target_pairs={{0,16},{1,17},{2,18},{3,19},{4,20},{5,21},{6,22},{7,23},{8,24},{9,... | collective-permute-start | bytes 368648 | tf_op jit(solution)/shard_map/ppermute | solution.py:801
  17.7 9.8 %collective-permute-start.1 = (bf16[48,1280]{1,0:T(8,128)(2,1)S(1)}, bf16[48,1280]{1,0:T(8,128)(2,1)S(1)}, u32[]{:S(2)}, u32[]{:S(2)}) collective-permute-start(bf16[48,1280]{1,0:T(8,128)(2,1)S(1)} %pad_maximum_fusion.3), channel_id=1, source_target_pairs={{0,8},{1,9},{2,10},{3,11},{4,12},{5,13},{6,14},{7,15},{8,0},{9,1},... | collective-permute-start | bytes 368648 | tf_op jit(solution)/shard_map/ppermute | solution.py:801
  30.1 8.9 %collective-permute-start.4 = (bf16[192,1280]{1,0:T(8,128)(2,1)S(1)}, bf16[192,1280]{1,0:T(8,128)(2,1)S(1)}, u32[]{:S(2)}, u32[]{:S(2)}) collective-permute-start(bf16[192,1280]{1,0:T(8,128)(2,1)S(1)} %get-tuple-element.86), channel_id=1, source_target_pairs={{0,2},{1,5},{2,0},{3,7},{4,6},{5,1},{6,4},{7,3},{8,10},{9,13},{10,... | collective-permute-start | bytes 1474568 | tf_op jit(solution)/shard_map/ppermute | solution.py:801
  39.1 22.4 %copy-start.17 = (bf16[384,1280]{1,0:T(8,128)(2,1)}, bf16[384,1280]{1,0:T(8,128)(2,1)S(1)}, u32[]{:S(2)}) copy-start(bf16[384,1280]{1,0:T(8,128)(2,1)S(1)} %constant_dynamic-update-slice_fusion.5.refs_1_) | copy-start | bytes 2949124
  39.1 16.8 %collective-permute-start.5 = (bf16[384,1280]{1,0:T(8,128)(2,1)S(1)}, bf16[384,1280]{1,0:T(8,128)(2,1)S(1)}, u32[]{:S(2)}, u32[]{:S(2)}) collective-permute-start(bf16[384,1280]{1,0:T(8,128)(2,1)S(1)} %constant_dynamic-update-slice_fusion.5.refs_1_), channel_id=1, source_target_pairs={{0,4},{1,3},{2,6},{3,1},{4,0},{5,7},{6,2},{7,5},{8,12},{9,11},{10,... | collective-permute-start | bytes 2949128 | tf_op jit(solution)/shard_map/ppermute | solution.py:801
  40.7 20.8 %collective-permute-start.6 = (bf16[384,1280]{1,0:T(8,128)(2,1)S(1)}, bf16[384,1280]{1,0:T(8,128)(2,1)}, u32[]{:S(2)}, u32[]{:S(2)}) collective-permute-start(bf16[384,1280]{1,0:T(8,128)(2,1)S(1)} %constant_dynamic-update-slice_fusion.5.refs_1_), channel_id=1, source_target_pairs={{0,1},{1,0},{2,3},{3,2},{4,5},{5,4},{6,7},{7,6},{8,9},{9,8},{10,11... | collective-permute-start | bytes 2949128 | tf_op jit(solution)/shard_map/ppermute | solution.py:801
  55.9 5.6 %collective-permute-start.7 = (bf16[384,1280]{1,0:T(8,128)(2,1)S(1)}, bf16[384,1280]{1,0:T(8,128)(2,1)}, u32[]{:S(2)}, u32[]{:S(2)}) collective-permute-start(bf16[384,1280]{1,0:T(8,128)(2,1)S(1)} %collective-permute-done.5.refs_2_), channel_id=1, source_target_pairs={{0,1},{1,0},{2,3},{3,2},{4,5},{5,4},{6,7},{7,6},{8,9},{9,8},{10,11... | collective-permute-start | bytes 2949128 | tf_op jit(solution)/shard_map/ppermute | solution.py:801
  71.7 6.0 %collective-permute-start.9 = (bf16[2,64,768]{2,1,0:T(8,128)(2,1)S(1)}, bf16[2,64,768]{2,1,0:T(8,128)(2,1)S(1)}, u32[]{:S(2)}, u32[]{:S(2)}) collective-permute-start(bf16[2,64,768]{2,1,0:T(8,128)(2,1)S(1)} %get-tuple-element.66), channel_id=1, source_target_pairs={{1,0},{2,1},{3,2},{4,3},{5,4},{6,5},{7,6},{8,7},{9,8},{10,9},{11,1... | collective-permute-start | bytes 589832 | tf_op jit(solution)/shard_map/ppermute | solution.py:789
  73.0 4.7 %collective-permute-start.8 = (bf16[2,64,768]{2,1,0:T(8,128)(2,1)S(1)}, bf16[2,64,768]{2,1,0:T(8,128)(2,1)S(1)}, u32[]{:S(2)}, u32[]{:S(2)}) collective-permute-start(bf16[2,64,768]{2,1,0:T(8,128)(2,1)S(1)} %get-tuple-element.67), channel_id=1, source_target_pairs={{0,1},{1,2},{2,3},{3,4},{4,5},{5,6},{6,7},{7,8},{8,9},{9,10},{10,1... | collective-permute-start | bytes 589832 | tf_op jit(solution)/shard_map/ppermute | solution.py:789
  92.4 26.7 %slice-start = ((s8[4718592]{0:T(1024)(128)(4,1)}), s8[4194304]{0:T(1024)(128)(4,1)S(1)}, s32[]{:S(2)}) async-start(s8[4718592]{0:T(1024)(128)(4,1)} %bitcast.16), calls=%async_computation.1 | async-start | bytes 8388608
  92.4 26.7 %slice-start.1 = ((s8[4718592]{0:T(1024)(128)(4,1)}), s8[524288]{0:T(1024)(128)(4,1)S(1)}, s32[]{:S(2)}) async-start(s8[4718592]{0:T(1024)(128)(4,1)} %bitcast.16), calls=%async_computation.2 | async-start | bytes 1048576
  137.4 18.7 %collective-permute-start.12 = (bf16[768,2304]{1,0:T(8,128)(2,1)S(1)}, bf16[768,2304]{1,0:T(8,128)(2,1)}, u32[]{:S(2)}, u32[]{:S(2)}) collective-permute-start(bf16[768,2304]{1,0:T(8,128)(2,1)S(1)} %ff_weight_grad.2.rest_0_), channel_id=1, source_target_pairs={{0,1},{1,0},{2,3},{3,2},{4,5},{5,4},{6,7},{7,6},{8,9},{9,8},{10,11... | collective-permute-start | bytes 10616840 | tf_op jit(solution)/shard_map/ppermute | solution.py:801
  141.1 6.0 %collective-permute-start.11 = (bf16[2,64,768]{2,1,0:T(8,128)(2,1)S(1)}, bf16[2,64,768]{2,1,0:T(8,128)(2,1)S(1)}, u32[]{:S(2)}, u32[]{:S(2)}) collective-permute-start(bf16[2,64,768]{2,1,0:T(8,128)(2,1)S(1)} %get-tuple-element.82), channel_id=1, source_target_pairs={{1,0},{2,1},{3,2},{4,3},{5,4},{6,5},{7,6},{8,7},{9,8},{10,9},{11,1... | collective-permute-start | bytes 589832 | tf_op jit(solution)/shard_map/ppermute | solution.py:789
  142.4 4.8 %collective-permute-start.10 = (bf16[2,64,768]{2,1,0:T(8,128)(2,1)S(1)}, bf16[2,64,768]{2,1,0:T(8,128)(2,1)S(1)}, u32[]{:S(2)}, u32[]{:S(2)}) collective-permute-start(bf16[2,64,768]{2,1,0:T(8,128)(2,1)S(1)} %get-tuple-element.83), channel_id=1, source_target_pairs={{0,1},{1,2},{2,3},{3,4},{4,5},{5,6},{6,7},{7,8},{8,9},{9,10},{10,1... | collective-permute-start | bytes 589832 | tf_op jit(solution)/shard_map/ppermute | solution.py:789
  159.2 28.0 %collective-permute-start.13 = (bf16[384,2304]{1,0:T(8,128)(2,1)S(1)}, bf16[384,2304]{1,0:T(8,128)(2,1)S(1)}, u32[]{:S(2)}, u32[]{:S(2)}) collective-permute-start(bf16[384,2304]{1,0:T(8,128)(2,1)S(1)} %get-tuple-element.65.rest_0_), channel_id=1, source_target_pairs={{0,4},{1,3},{2,6},{3,1},{4,0},{5,7},{6,2},{7,5},{8,12},{9,11},{10,... | collective-permute-start | bytes 5308424 | tf_op jit(solution)/shard_map/ppermute | solution.py:801
  187.6 18.0 %collective-permute-start.14 = (bf16[192,2304]{1,0:T(8,128)(2,1)S(1)}, bf16[192,2304]{1,0:T(8,128)(2,1)S(1)}, u32[]{:S(2)}, u32[]{:S(2)}) collective-permute-start(bf16[192,2304]{1,0:T(8,128)(2,1)S(1)} %get-tuple-element.71.rest_0_), channel_id=1, source_target_pairs={{0,2},{1,5},{2,0},{3,7},{4,6},{5,1},{6,4},{7,3},{8,10},{9,13},{10,... | collective-permute-start | bytes 2654216 | tf_op jit(solution)/shard_map/ppermute | solution.py:801
  195.5 23.4 %collective-permute-start.15 = (bf16[768,1152]{1,0:T(8,128)(2,1)S(1)}, bf16[768,1152]{1,0:T(8,128)(2,1)S(1)}, u32[]{:S(2)}, u32[]{:S(2)}) collective-permute-start(bf16[768,1152]{1,0:T(8,128)(2,1)S(1)} %qkv_weight_grad.2.rest_0_), channel_id=1, source_target_pairs={{0,1},{1,0},{2,3},{3,2},{4,5},{5,4},{6,7},{7,6},{8,9},{9,8},{10,11... | collective-permute-start | bytes 5308424 | tf_op jit(solution)/shard_map/ppermute | solution.py:801
  205.8 13.6 %collective-permute-start.24 = (bf16[48,2304]{1,0:T(8,128)(2,1)S(1)}, bf16[48,2304]{1,0:T(8,128)(2,1)S(1)}, u32[]{:S(2)}, u32[]{:S(2)}) collective-permute-start(bf16[48,2304]{1,0:T(8,128)(2,1)S(1)} %get-tuple-element.74.rest_3_), channel_id=1, source_target_pairs={{0,24},{1,25},{2,26},{3,27},{4,28},{5,29},{6,30},{7,31},{8,16},{9,... | collective-permute-start | bytes 663560 | tf_op jit(solution)/shard_map/ppermute | solution.py:801
  211.5 20.3 %collective-permute-start.23 = (bf16[48,2304]{1,0:T(8,128)(2,1)S(1)}, bf16[48,2304]{1,0:T(8,128)(2,1)S(1)}, u32[]{:S(2)}, u32[]{:S(2)}) collective-permute-start(bf16[48,2304]{1,0:T(8,128)(2,1)S(1)} %get-tuple-element.75.rest_2_), channel_id=1, source_target_pairs={{0,16},{1,17},{2,18},{3,19},{4,20},{5,21},{6,22},{7,23},{8,24},{9,... | collective-permute-start | bytes 663560 | tf_op jit(solution)/shard_map/ppermute | solution.py:801
  214.4 17.4 %collective-permute-start.22 = (bf16[48,2304]{1,0:T(8,128)(2,1)S(1)}, bf16[48,2304]{1,0:T(8,128)(2,1)S(1)}, u32[]{:S(2)}, u32[]{:S(2)}) collective-permute-start(bf16[48,2304]{1,0:T(8,128)(2,1)S(1)} %get-tuple-element.76.rest_1_), channel_id=1, source_target_pairs={{0,8},{1,9},{2,10},{3,11},{4,12},{5,13},{6,14},{7,15},{8,0},{9,1},... | collective-permute-start | bytes 663560 | tf_op jit(solution)/shard_map/ppermute | solution.py:801
  219.4 21.8 %collective-permute-start.16 = (bf16[384,1152]{1,0:T(8,128)(2,1)S(1)}, bf16[384,1152]{1,0:T(8,128)(2,1)S(1)}, u32[]{:S(2)}, u32[]{:S(2)}) collective-permute-start(bf16[384,1152]{1,0:T(8,128)(2,1)S(1)} %get-tuple-element.69), channel_id=1, source_target_pairs={{0,4},{1,3},{2,6},{3,1},{4,0},{5,7},{6,2},{7,5},{8,12},{9,11},{10,... | collective-permute-start | bytes 2654216 | tf_op jit(solution)/shard_map/ppermute | solution.py:801
  231.9 10.7 %collective-permute-start.25 = (f32[24,2304]{1,0:T(8,128)S(1)}, f32[24,2304]{1,0:T(8,128)S(1)}, u32[]{:S(2)}, u32[]{:S(2)}) collective-permute-start(f32[24,2304]{1,0:T(8,128)S(1)} %slice_select_fusion.1), channel_id=1, source_target_pairs={{0,1},{1,0},{2,3},{3,2},{4,5},{5,4},{6,7},{7,6},{8,9},{9,8},{10,11... | collective-permute-start | bytes 663560 | tf_op jit(solution)/shard_map/ppermute | solution.py:801
  241.4 22.5 %copy-start.26 = (bf16[24]{0:T(256)(128)(2,1)S(1)}, bf16[24]{0:T(256)(128)(2,1)}, u32[]{:S(2)}) copy-start(bf16[24]{0:T(256)(128)(2,1)} %param.14) | copy-start | bytes 148
  241.4 8.4 %collective-permute-start.17 = (bf16[192,1152]{1,0:T(8,128)(2,1)S(1)}, bf16[192,1152]{1,0:T(8,128)(2,1)S(1)}, u32[]{:S(2)}, u32[]{:S(2)}) collective-permute-start(bf16[192,1152]{1,0:T(8,128)(2,1)S(1)} %get-tuple-element.73), channel_id=1, source_target_pairs={{0,2},{1,5},{2,0},{3,7},{4,6},{5,1},{6,4},{7,3},{8,10},{9,13},{10,... | collective-permute-start | bytes 1327112 | tf_op jit(solution)/shard_map/ppermute | solution.py:801
  249.9 4.8 %collective-permute-start.18 = (bf16[48,1152]{1,0:T(8,128)(2,1)S(1)}, bf16[48,1152]{1,0:T(8,128)(2,1)S(1)}, u32[]{:S(2)}, u32[]{:S(2)}) collective-permute-start(bf16[48,1152]{1,0:T(8,128)(2,1)S(1)} %get-tuple-element.78), channel_id=1, source_target_pairs={{0,8},{1,9},{2,10},{3,11},{4,12},{5,13},{6,14},{7,15},{8,0},{9,1},... | collective-permute-start | bytes 331784 | tf_op jit(solution)/shard_map/ppermute | solution.py:801
  250.7 9.2 %collective-permute-start.20 = (bf16[48,1152]{1,0:T(8,128)(2,1)S(1)}, bf16[48,1152]{1,0:T(8,128)(2,1)S(1)}, u32[]{:S(2)}, u32[]{:S(2)}) collective-permute-start(bf16[48,1152]{1,0:T(8,128)(2,1)S(1)} %get-tuple-element.79), channel_id=1, source_target_pairs={{0,24},{1,25},{2,26},{3,27},{4,28},{5,29},{6,30},{7,31},{8,16},{9,... | collective-permute-start | bytes 331784 | tf_op jit(solution)/shard_map/ppermute | solution.py:801
  253.6 10.1 %collective-permute-start.19 = (bf16[48,1152]{1,0:T(8,128)(2,1)S(1)}, bf16[48,1152]{1,0:T(8,128)(2,1)S(1)}, u32[]{:S(2)}, u32[]{:S(2)}) collective-permute-start(bf16[48,1152]{1,0:T(8,128)(2,1)S(1)} %get-tuple-element.80), channel_id=1, source_target_pairs={{0,16},{1,17},{2,18},{3,19},{4,20},{5,21},{6,22},{7,23},{8,24},{9,... | collective-permute-start | bytes 331784 | tf_op jit(solution)/shard_map/ppermute | solution.py:801
  263.8 1.4 collective-permute-start.21
  (26 other events, 203.5 us)
Sparse Core Ops, SparseCore 0:
  11.4 77.1 all-gather.1
